TPU v7x, 32 devices: a whole 2x2x4 slice. The times are simulated.
32 devices in a mesh: dp: 2 (over x), fsdp: 16 (over z, y, core).
Axes of the slice: x: 2, y: 2, z: 4, core: 2. Of those that a mesh axis runs over, the one named last changes fastest.
Arguments:
- tokens: bfloat16 [64, 256, 768], P(('dp', 'fsdp')), may hold values from -6 to 6
- lengths: int32 [64, 3], P(('dp', 'fsdp')), may hold values from 18 to 82, as said below
- keep_mask: int32 [64, 3, 2], P(('dp', 'fsdp')), may hold values 0 or 1
- cotangent: bfloat16 [64, 256, 768], P(('dp', 'fsdp')), may hold values from -6 to 6
- ln1_gain: bfloat16 [768], P('fsdp'), may hold values from 0.5 to 1.5
- ln1_bias: bfloat16 [768], P('fsdp'), may hold values from -3 to 3
- qkv_weight: bfloat16 [768, 2304], P('fsdp'), may hold values from -0.21875 to 0.21875
- q_bias: bfloat16 [768], P('fsdp'), may hold values from -4 to 4
- v_bias: bfloat16 [768], P('fsdp'), may hold values from -0.75 to 0.75
- proj_weight: bfloat16 [768, 768], P('fsdp'), may hold values from -1.25 to 1.25
- proj_bias: bfloat16 [768], P('fsdp'), may hold values from -3 to 3
- ln2_gain: bfloat16 [768], P('fsdp'), may hold values from 0.5 to 1.5
- ln2_bias: bfloat16 [768], P('fsdp'), may hold values from -3 to 3
- fc1_weight: bfloat16 [768, 3072], P('fsdp'), may hold values from -0.21875 to 0.21875
- fc1_bias: bfloat16 [3072], P('fsdp'), may hold values from -4 to 4
- fc2_weight: bfloat16 [3072, 768], P('fsdp'), may hold values from -0.109375 to 0.109375
- fc2_bias: bfloat16 [768], P('fsdp'), may hold values from -3 to 3
Outputs:
- output: bfloat16 [64, 256, 768], P(('dp', 'fsdp'))
- tokens_grad: float32 [64, 256, 768], P(('dp', 'fsdp'))
- ln1_gain_grad: float32 [768], P('fsdp')
- ln1_bias_grad: float32 [768], P('fsdp')
- qkv_weight_grad: float32 [768, 2304], P('fsdp')
- q_bias_grad: float32 [768], P('fsdp')
- v_bias_grad: float32 [768], P('fsdp')
- proj_weight_grad: float32 [768, 768], P('fsdp')
- proj_bias_grad: float32 [768], P('fsdp')
- ln2_gain_grad: float32 [768], P('fsdp')
- ln2_bias_grad: float32 [768], P('fsdp')
- fc1_weight_grad: float32 [768, 3072], P('fsdp')
- fc1_bias_grad: float32 [3072], P('fsdp')
- fc2_weight_grad: float32 [3072, 768], P('fsdp')
- fc2_bias_grad: float32 [768], P('fsdp')
Inputs may be any that keep to these rules, and one draw needn't show every extreme that they name: `lengths`: the 3 images of a row fill its first tokens in order; the remaining tokens of the row are padding.
All inputs are finite; a program needn't handle non-finite values. No bound on the sum of `keep_mask` on one device may be relied on, other than what follows from the above.
Results may differ from a plain program's by a relative error of at most 0.014.
Values may be sent and summed in bfloat16 or wider, within the bound.
No kernel may reach another device: no remote copies, remote signals or barrier semaphores. Data moves between devices by JAX's collectives and lax.ppermute only.
A program may use at most 192 MiB of HBM per device.

v0:
```python
import jax
import jax.numpy as jnp
from jax import lax
from jax.sharding import PartitionSpec as P

HEADS = 12


EPSILON = 1e-06
KEEP_RATE = 0.9
NEGATIVE = -1e30


def normalize(values, gain, shift):
    center = values - jnp.mean(values, axis=-1, keepdims=True)
    spread = jnp.mean(center * center, axis=-1, keepdims=True)
    return center * lax.rsqrt(spread + EPSILON) * gain + shift


def standardize(values):
    center = values - jnp.mean(values, axis=-1, keepdims=True)
    spread = jnp.mean(center * center, axis=-1, keepdims=True)
    return center * lax.rsqrt(spread + EPSILON)


def affine_low(unit_values, gain, shift):
    return (unit_values * gain.astype(jnp.float32) + shift.astype(jnp.float32)).astype(jnp.bfloat16)


def exact_gelu(values):
    return jax.nn.gelu(values, approximate=False)


def norm_back(values, gain, shift, incoming):
    _, pullback = jax.vjp(normalize, values, gain, shift)
    return pullback(incoming)


def inner_rows(left, right):
    return lax.dot_general(
        left, right, (((0,), (0,)), ((), ())), preferred_element_type=jnp.float32
    )


def times_transpose(left, right):
    return lax.dot_general(
        left, right, (((1,), (1,)), ((), ())), preferred_element_type=jnp.float32
    )


def layout(lengths, keep_mask, length):
    image_ends = jnp.cumsum(lengths, axis=-1, dtype=jnp.int32)
    position = jnp.arange(length, dtype=jnp.int32)
    segment = jnp.sum(
        (position[None, :, None] >= image_ends[:, None, :]).astype(jnp.int32),
        axis=-1,
        dtype=jnp.int32,
    )
    images = jnp.arange(lengths.shape[1], dtype=jnp.int32)
    member = (segment[:, :, None] == images[None, None, :]).astype(jnp.float32)
    keeping = keep_mask.astype(jnp.float32)
    scales = jnp.sum(member[:, :, :, None] * keeping[:, None, :, :], axis=2) / KEEP_RATE
    inside = jnp.sum(member, axis=-1)
    return (segment, scales, inside)


def attention_forward(packed, segment, rowset, length, head_size):
    split_view = packed.reshape(rowset, length, 3, HEADS, head_size)
    queries = split_view[:, :, 0]
    keys_all = split_view[:, :, 1]
    values_all = split_view[:, :, 2]
    scores = jnp.einsum(
        "rqhd,rkhd->rhqk", queries, keys_all, preferred_element_type=jnp.float32
    ) * head_size ** (-0.5)
    matching = segment[:, :, None] == segment[:, None, :]
    scores = jnp.where(matching[:, None], scores, NEGATIVE)
    raised = jnp.exp(scores - jnp.max(scores, axis=-1, keepdims=True))
    weighting = raised / jnp.sum(raised, axis=-1, keepdims=True)
    weighting_low = weighting.astype(jnp.bfloat16)
    attended = jnp.einsum(
        "rhqk,rkhd->rqhd", weighting_low, values_all, preferred_element_type=jnp.float32
    )
    attended = attended.reshape(rowset * length, HEADS * head_size).astype(jnp.bfloat16)
    return (queries, keys_all, values_all, weighting, weighting_low, attended)


def per_device(
    tokens,
    lengths,
    keep_mask,
    cotangent,
    ln1_gain,
    ln1_bias,
    qkv_weight,
    q_bias,
    v_bias,
    proj_weight,
    proj_bias,
    ln2_gain,
    ln2_bias,
    fc1_weight,
    fc1_bias,
    fc2_weight,
    fc2_bias,
):
    rowset, length, features = tokens.shape
    head_size = features // HEADS
    token_count = rowset * length
    segment, scales, inside = layout(lengths, keep_mask, length)
    scale_one = scales[:, :, 0].reshape(token_count, 1)
    scale_two = scales[:, :, 1].reshape(token_count, 1)
    inside_column = inside.reshape(token_count, 1)
    flattened = tokens.reshape(token_count, features).astype(jnp.float32)
    unit_one = standardize(flattened)
    qkv_full, proj_full, gain_one, shift_one, query_bias, value_bias, out_bias = (
        lax.all_gather(qkv_weight, "fsdp", axis=0, tiled=True),
        lax.all_gather(proj_weight, "fsdp", axis=0, tiled=True),
        lax.all_gather(ln1_gain, "fsdp", axis=0, tiled=True),
        lax.all_gather(ln1_bias, "fsdp", axis=0, tiled=True),
        lax.all_gather(q_bias, "fsdp", axis=0, tiled=True),
        lax.all_gather(v_bias, "fsdp", axis=0, tiled=True),
        lax.all_gather(proj_bias, "fsdp", axis=0, tiled=True),
    )
    normed_one = affine_low(unit_one, gain_one, shift_one)
    bias_all = jnp.concatenate(
        [
            query_bias.astype(jnp.float32),
            jnp.zeros((features,), jnp.float32),
            value_bias.astype(jnp.float32),
        ]
    )
    packed = (jnp.dot(normed_one, qkv_full, preferred_element_type=jnp.float32) + bias_all).astype(
        jnp.bfloat16
    )
    _, _, _, _, _, attended = attention_forward(packed, segment, rowset, length, head_size)
    branch_one = jnp.dot(attended, proj_full, preferred_element_type=jnp.float32) + out_bias.astype(
        jnp.float32
    )
    middle = flattened + scale_one * branch_one
    unit_two = standardize(middle)
    up_full, down_full, gain_two, shift_two, up_bias, down_bias = (
        lax.all_gather(fc1_weight, "fsdp", axis=0, tiled=True),
        lax.all_gather(fc2_weight, "fsdp", axis=0, tiled=True),
        lax.all_gather(ln2_gain, "fsdp", axis=0, tiled=True),
        lax.all_gather(ln2_bias, "fsdp", axis=0, tiled=True),
        lax.all_gather(fc1_bias, "fsdp", axis=0, tiled=True),
        lax.all_gather(fc2_bias, "fsdp", axis=0, tiled=True),
    )
    normed_two = affine_low(unit_two, gain_two, shift_two)
    hidden = jnp.dot(normed_two, up_full, preferred_element_type=jnp.float32) + up_bias.astype(
        jnp.float32
    )
    active = exact_gelu(hidden).astype(jnp.bfloat16)
    branch_two = jnp.dot(active, down_full, preferred_element_type=jnp.float32) + down_bias.astype(
        jnp.float32
    )
    output = (
        ((middle + scale_two * branch_two) * inside_column)
        .astype(jnp.bfloat16)
        .reshape(rowset, length, features)
    )
    up_full, down_full = (
        lax.all_gather(fc1_weight, "fsdp", axis=0, tiled=True),
        lax.all_gather(fc2_weight, "fsdp", axis=0, tiled=True),
    )
    gain_two_f = gain_two.astype(jnp.float32)
    shift_two_f = shift_two.astype(jnp.float32)
    grad_out = cotangent.reshape(token_count, features).astype(jnp.float32) * inside_column
    grad_two_low = (grad_out * scale_two).astype(jnp.bfloat16)
    fc2_grad = inner_rows(active, grad_two_low)
    fc2_bias_part = jnp.sum(grad_two_low.astype(jnp.float32), axis=0)
    grad_active = times_transpose(grad_two_low, down_full)
    _, gelu_pull = jax.vjp(exact_gelu, hidden)
    grad_hidden_low = gelu_pull(grad_active)[0].astype(jnp.bfloat16)
    fc1_grad = inner_rows(normed_two, grad_hidden_low)
    fc1_bias_part = jnp.sum(grad_hidden_low.astype(jnp.float32), axis=0)
    grad_normed_two = times_transpose(grad_hidden_low, up_full)
    grad_middle_norm, gain_two_part, shift_two_part = norm_back(
        middle, gain_two_f, shift_two_f, grad_normed_two
    )
    grad_middle = grad_out + grad_middle_norm
    qkv_full, proj_full = (
        lax.all_gather(qkv_weight, "fsdp", axis=0, tiled=True),
        lax.all_gather(proj_weight, "fsdp", axis=0, tiled=True),
    )
    gain_one_f = gain_one.astype(jnp.float32)
    shift_one_f = shift_one.astype(jnp.float32)
    queries, keys_all, values_all, weighting, weighting_low, attended = attention_forward(
        packed, segment, rowset, length, head_size
    )
    grad_one_low = (grad_middle * scale_one).astype(jnp.bfloat16)
    proj_grad = inner_rows(attended, grad_one_low)
    proj_bias_part = jnp.sum(grad_one_low.astype(jnp.float32), axis=0)
    grad_attended_low = times_transpose(grad_one_low, proj_full).astype(jnp.bfloat16)
    grad_attended_low = grad_attended_low.reshape(rowset, length, HEADS, head_size)
    grad_weighting = jnp.einsum(
        "rqhd,rkhd->rhqk", grad_attended_low, values_all, preferred_element_type=jnp.float32
    )
    value_grad = jnp.einsum(
        "rhqk,rqhd->rkhd", weighting_low, grad_attended_low, preferred_element_type=jnp.float32
    )
    row_inner = jnp.sum(grad_weighting * weighting, axis=-1, keepdims=True)
    grad_scores_low = (weighting * (grad_weighting - row_inner)).astype(jnp.bfloat16)
    key_scale = head_size ** (-0.5)
    query_grad = (
        jnp.einsum("rhqk,rkhd->rqhd", grad_scores_low, keys_all, preferred_element_type=jnp.float32)
        * key_scale
    )
    key_grad = (
        jnp.einsum("rhqk,rqhd->rkhd", grad_scores_low, queries, preferred_element_type=jnp.float32)
        * key_scale
    )
    grad_packed_low = (
        jnp.stack([query_grad, key_grad, value_grad], axis=2)
        .reshape(token_count, 3 * features)
        .astype(jnp.bfloat16)
    )
    qkv_grad = inner_rows(normed_one, grad_packed_low)
    column_sums = jnp.sum(grad_packed_low.astype(jnp.float32), axis=0)
    query_bias_part = column_sums[:features]
    value_bias_part = column_sums[2 * features :]
    grad_normed_one = times_transpose(grad_packed_low, qkv_full)
    grad_input_norm, gain_one_part, shift_one_part = norm_back(
        flattened, gain_one_f, shift_one_f, grad_normed_one
    )
    tokens_grad = (grad_middle + grad_input_norm).reshape(rowset, length, features)
    (
        gain_two_grad,
        shift_two_grad,
        fc1_weight_part,
        fc1_bias_shard,
        fc2_weight_part,
        fc2_bias_shard,
    ) = (
        lax.psum_scatter(gain_two_part, "fsdp", scatter_dimension=0, tiled=True),
        lax.psum_scatter(shift_two_part, "fsdp", scatter_dimension=0, tiled=True),
        lax.psum_scatter(fc1_grad, "fsdp", scatter_dimension=0, tiled=True),
        lax.psum_scatter(fc1_bias_part, "fsdp", scatter_dimension=0, tiled=True),
        lax.psum_scatter(fc2_grad, "fsdp", scatter_dimension=0, tiled=True),
        lax.psum_scatter(fc2_bias_part, "fsdp", scatter_dimension=0, tiled=True),
    )
    (
        gain_one_grad,
        shift_one_grad,
        qkv_weight_part,
        query_bias_shard,
        value_bias_shard,
        proj_weight_part,
        proj_bias_shard,
    ) = (
        lax.psum_scatter(gain_one_part, "fsdp", scatter_dimension=0, tiled=True),
        lax.psum_scatter(shift_one_part, "fsdp", scatter_dimension=0, tiled=True),
        lax.psum_scatter(qkv_grad, "fsdp", scatter_dimension=0, tiled=True),
        lax.psum_scatter(query_bias_part, "fsdp", scatter_dimension=0, tiled=True),
        lax.psum_scatter(value_bias_part, "fsdp", scatter_dimension=0, tiled=True),
        lax.psum_scatter(proj_grad, "fsdp", scatter_dimension=0, tiled=True),
        lax.psum_scatter(proj_bias_part, "fsdp", scatter_dimension=0, tiled=True),
    )
    summed = (
        lax.psum(gain_one_grad.astype(jnp.bfloat16), "dp").astype(jnp.float32),
        lax.psum(shift_one_grad.astype(jnp.bfloat16), "dp").astype(jnp.float32),
        lax.psum(qkv_weight_part.astype(jnp.bfloat16), "dp").astype(jnp.float32),
        lax.psum(query_bias_shard.astype(jnp.bfloat16), "dp").astype(jnp.float32),
        lax.psum(value_bias_shard.astype(jnp.bfloat16), "dp").astype(jnp.float32),
        lax.psum(proj_weight_part.astype(jnp.bfloat16), "dp").astype(jnp.float32),
        lax.psum(proj_bias_shard.astype(jnp.bfloat16), "dp").astype(jnp.float32),
        lax.psum(gain_two_grad.astype(jnp.bfloat16), "dp").astype(jnp.float32),
        lax.psum(shift_two_grad.astype(jnp.bfloat16), "dp").astype(jnp.float32),
        lax.psum(fc1_weight_part.astype(jnp.bfloat16), "dp").astype(jnp.float32),
        lax.psum(fc1_bias_shard.astype(jnp.bfloat16), "dp").astype(jnp.float32),
        lax.psum(fc2_weight_part.astype(jnp.bfloat16), "dp").astype(jnp.float32),
        lax.psum(fc2_bias_shard.astype(jnp.bfloat16), "dp").astype(jnp.float32),
    )
    return (
        output,
        tokens_grad,
        summed[0],
        summed[1],
        summed[2],
        summed[3],
        summed[4],
        summed[5],
        summed[6],
        summed[7],
        summed[8],
        summed[9],
        summed[10],
        summed[11],
        summed[12],
    )


def solution(mesh):
    in_specs = (
        P(("dp", "fsdp"), None, None),
        P(("dp", "fsdp"), None),
        P(("dp", "fsdp"), None, None),
        P(("dp", "fsdp"), None, None),
        P("fsdp"),
        P("fsdp"),
        P("fsdp", None),
        P("fsdp"),
        P("fsdp"),
        P("fsdp", None),
        P("fsdp"),
        P("fsdp"),
        P("fsdp"),
        P("fsdp", None),
        P("fsdp"),
        P("fsdp", None),
        P("fsdp"),
    )
    out_specs = (
        P(("dp", "fsdp"), None, None),
        P(("dp", "fsdp"), None, None),
        P("fsdp"),
        P("fsdp"),
        P("fsdp", None),
        P("fsdp"),
        P("fsdp"),
        P("fsdp", None),
        P("fsdp"),
        P("fsdp"),
        P("fsdp"),
        P("fsdp", None),
        P("fsdp"),
        P("fsdp", None),
        P("fsdp"),
    )
    return jax.shard_map(
        per_device, mesh=mesh, in_specs=in_specs, out_specs=out_specs, check_vma=False
    )
```

profile of v0, /device:TPU:0, one launch (start us, length us, event | category | flops | bytes accessed | tf_op | source)
XLA Modules:
  0.0 724.1 jit_solution(1822695374023200607)
XLA Ops:
  10.0 1.3 fusion.61
  14.5 1.3 convert_reduce_fusion.2
  15.9 1.5 fusion.22
  25.0 64.0 %all-reduce.19 = (bf16[768]{0:T(1024)(128)(2,1)S(1)}, bf16[768]{0:T(1024)(128)(2,1)S(1)}, bf16[768]{0:T(1024)(128)(2,1)S(1)}, bf16[768]{0:T(1024)(128)(2,1)S(1)}...) all-reduce(bf16[768]{0:T(1024)(128)(2,1)S(1)} %dynamic-update-slice, ...), channel_id=1, replica_groups=mesh['dp'=2,'fsdp'=16] {'fsdp'}, use_global_device_ids=true, to_apply=%add.1 | all-reduce | flops 9216 | bytes 36864
  90.6 1.3 fusion.25
  92.2 5.4 fusion.8
  97.7 4.3 copy.73
  102.0 6.1 reshape.198
  108.1 2.9 fusion.58
  112.1 1.9 fusion.62
  114.6 2.0 copy-done.10
  118.5 2.5 fusion.63
  122.4 32.3 %all-gather.9.cloned.1.call-done = bf16[768,3072]{1,0:T(8,128)(2,1)} async-done(((bf16[48,3072]{1,0:T(8,128)(2,1)}), bf16[768,3072]{1,0:T(8,128)(2,1)}) %all-gather.9.cloned.1.call-update) | async-done | bytes 4718608 | tf_op jit(solution)/shard_map/all_gather | solution.py:142
  154.7 8.2 %fusion.54 = f32[512,3072]{1,0:T(8,128)} fusion(bf16[768,3072]{1,0:T(8,128)(2,1)} %all-gather.9.cloned.1.call-done, f32[512,768]{1,0:T(8,128)} %copy-done.6, f32[768]{0:T(1024)S(1)} %convert_element_type.238, f32[768]{0:T(1024)S(1)} %convert_element_type.237, f32[512]{0:T(512)S(1)} %fusion.45, f32[512]{0:T(512)S(1)} %broadcast_multiply_fusion.1), kind=kOutput, calls=%fused_computation.117 | convolution fusion | flops 2417885184 | bytes 12593152 | tf_op jit(solution)/shard_map/dot_general | solution.py:150
  162.9 45.9 %all-gather.11.cloned.1.call-done = bf16[3072,768]{1,0:T(8,128)(2,1)} async-done(((bf16[192,768]{1,0:T(8,128)(2,1)}), bf16[3072,768]{1,0:T(8,128)(2,1)}) %all-gather.11.cloned.1.call-update) | async-done | bytes 4718608 | tf_op jit(solution)/shard_map/all_gather | solution.py:143
  208.8 20.3 %convert_reduce_fusion = (f32[3072]{0:T(1024)S(1)}, bf16[512,3072]{1,0:T(8,128)(2,1)S(1)}, f32[512,3072]{1,0:T(8,128)}) fusion(f32[512,3072]{1,0:T(8,128)} %fusion.54, f32[3072]{0:T(1024)S(1)} %convert_element_type.240, bf16[512,768]{1,0:T(8,128)(2,1)} %multiply_convert_fusion.4, bf16[3072,768]{1,0:T(8,128)(2,1)} %all-gather.11.cloned.1.call-done), kind=kOutput, calls=%fused_computation.3 | convolution fusion | flops 2533880832 | bytes 21258240 | tf_op jit(solution)/shard_map/dot_general | solution.py:46
  229.1 3.0 multiply_reduce_fusion.1
  234.1 2.2 fusion.65
  236.2 3.2 convolution_convert_fusion
  239.4 2.3 copy.79
  241.7 2.9 reshape.200
  245.2 4.5 multiply_reduce_fusion
  249.6 4.5 multiply_convert_fusion
  256.4 4.1 fusion.31
  260.9 2.5 copy.85
  263.9 1.4 copy-done.3
  265.3 4.9 fusion.64
  270.5 9.2 %fusion.53 = f32[768,3072]{1,0:T(8,128)} fusion(bf16[512,3072]{1,0:T(8,128)(2,1)} %copy-done.32, f32[512,768]{1,0:T(8,128)} %copy-done.6, f32[768]{0:T(1024)S(1)} %convert_element_type.238, f32[768]{0:T(1024)S(1)} %convert_element_type.237, f32[512]{0:T(512)S(1)} %fusion.45, f32[512]{0:T(512)S(1)} %broadcast_multiply_fusion.1), kind=kOutput, calls=%fused_computation.116 | convolution fusion | flops 2417885184 | bytes 14166016 | tf_op jit(solution)/shard_map/dot_general | solution.py:40
  279.7 6.3 multiply_convert_fusion.1
  286.1 1.6 copy-done.14
  287.7 5.1 fusion.66
  295.1 5.0 fusion.55
  300.9 1.8 add_add_fusion.2
  302.7 3.6 reduce-scatter.7.cloned.1.call-done
  306.4 1.6 convert_element_type.266
  307.9 91.9 %reduce-scatter.5.cloned.1.call-done = f32[48,2304]{1,0:T(8,128)} async-done(((f32[768,2304]{1,0:T(8,128)}), f32[48,2304]{1,0:T(8,128)}) %reduce-scatter.5.cloned.1.call-update) | async-done | bytes 442384 | tf_op jit(solution)/shard_map/reduce_scatter | solution.py:253
  399.9 1.7 convert_element_type.259
  401.6 113.3 %reduce-scatter.9.cloned.1.call-done = f32[48,3072]{1,0:T(8,128)} async-done(((f32[768,3072]{1,0:T(8,128)}), f32[48,3072]{1,0:T(8,128)}) %reduce-scatter.9.cloned.1.call-update) | async-done | bytes 589840 | tf_op jit(solution)/shard_map/reduce_scatter | solution.py:237
  514.9 1.8 convert_element_type.275
  516.7 114.0 %reduce-scatter.11.cloned.1.call-done = f32[192,768]{1,0:T(8,128)} async-done(((f32[3072,768]{1,0:T(8,128)}), f32[192,768]{1,0:T(8,128)}) %reduce-scatter.11.cloned.1.call-update) | async-done | bytes 589840 | tf_op jit(solution)/shard_map/reduce_scatter | solution.py:239
  630.7 1.8 convert_element_type.280
  632.6 60.4 %all-reduce.18 = (bf16[768]{0:T(1024)(128)(2,1)S(1)}, bf16[768]{0:T(1024)(128)(2,1)S(1)}, bf16[768]{0:T(1024)(128)(2,1)S(1)}, bf16[768]{0:T(1024)(128)(2,1)S(1)}...) all-reduce(f32[768]{0:T(1024)S(1)} %get-tuple-element.17, ...), channel_id=2, replica_groups=mesh['dp'=2,'fsdp'=16] {'fsdp'}, use_global_device_ids=true, to_apply=%region_16.17.clone | all-reduce | flops 9216 | bytes 55296
  693.7 5.2 all-reduce.20
  703.6 6.8 multiply_convert_fusion.5
  710.4 1.6 convert_element_type.267
  712.0 1.7 convert_element_type.260
  713.7 1.8 convert_element_type.276
  715.5 1.8 convert_element_type.281
  (174 shorter events, 32.1 us)
Async XLA Ops:
  7.2 83.4 %copy-start = (bf16[2,256,768]{2,1,0:T(8,128)(2,1)S(1)}, bf16[2,256,768]{2,1,0:T(8,128)(2,1)}, u32[]{:S(2)}) copy-start(bf16[2,256,768]{2,1,0:T(8,128)(2,1)} %param.17) | copy-start | bytes 2359300
  7.2 82.2 %copy-start.2 = (bf16[2,256,768]{2,1,0:T(8,128)(2,1)S(1)}, bf16[2,256,768]{2,1,0:T(8,128)(2,1)}, u32[]{:S(2)}) copy-start(bf16[2,256,768]{2,1,0:T(8,128)(2,1)} %param.20) | copy-start | bytes 2359300
  7.2 85.0 %all-gather.5.cloned.1.call-start = ((), (), s32[]{:S(2)}) async-start(), calls=%async_computation.4 | async-start | bytes 3760128 | tf_op jit(solution)/shard_map/all_gather | solution.py:116
  7.9 110.5 %all-gather.7.cloned.1.call-start = ((), (), s32[]{:S(2)}) async-start(), calls=%async_computation.5 | async-start | bytes 1253376 | tf_op jit(solution)/shard_map/all_gather | solution.py:117
  8.7 146.0 %all-gather.9.cloned.1.call-start = ((), (), s32[]{:S(2)}) async-start(), calls=%async_computation.6 | async-start | bytes 5013504 | tf_op jit(solution)/shard_map/all_gather | solution.py:142
  9.4 199.4 %all-gather.11.cloned.1.call-start = ((), (), s32[]{:S(2)}) async-start(), calls=%async_computation.7 | async-start | bytes 5013504 | tf_op jit(solution)/shard_map/all_gather | solution.py:143
  10.0 296.4 %reduce-scatter.7.cloned.1.call-start = ((), (), s32[]{:S(2)}) async-start(), calls=%async_computation.9 | async-start | bytes 2506752 | tf_op jit(solution)/shard_map/reduce_scatter | solution.py:256
  13.7 3.7 copy-start.24
  15.9 81.8 %copy-start.20 = (f32[1,2,2,128]{3,1,2,0:T(2,128)}, f32[1,2,2,128]{3,1,2,0:T(2,128)S(1)}, u32[]{:S(2)}) copy-start(f32[1,2,2,128]{3,1,2,0:T(2,128)S(1)} %copy.94) | copy-start | bytes 6148
  17.4 71.6 %copy-start.28 = (f32[1,2,2,128]{3,1,2,0:T(2,128)}, f32[1,2,2,128]{3,1,2,0:T(2,128)S(1)}, u32[]{:S(2)}) copy-start(f32[1,2,2,128]{3,1,2,0:T(2,128)S(1)} %copy.95) | copy-start | bytes 6148
  17.4 80.3 %copy-start.22 = (f32[512]{0:T(512)}, f32[512]{0:T(512)S(1)}, u32[]{:S(2)}) copy-start(f32[512]{0:T(512)S(1)} %rsqrt.25) | copy-start | bytes 6148
  89.0 8.6 %copy-start.18 = (f32[768]{0:T(1024)}, f32[768]{0:T(1024)S(1)}, u32[]{:S(2)}) copy-start(f32[768]{0:T(1024)S(1)} %convert_element_type.226) | copy-start | bytes 9220
  89.3 8.4 %copy-start.26 = (f32[2,256,1]{1,2,0:T(1,128)}, f32[2,256,1]{1,2,0:T(1,128)S(1)}, u32[]{:S(2)}) copy-start(f32[2,256,1]{1,2,0:T(1,128)S(1)} %get-tuple-element.67) | copy-start | bytes 6148
  111.0 1.0 copy-start.4
  111.0 2.9 copy-start.15
  114.0 2.7 copy-start.10
  120.9 1.1 copy-start.6
  162.9 66.2 %copy-start.7 = (f32[512,768]{1,0:T(8,128)S(1)}, f32[512,768]{1,0:T(8,128)}, u32[]{:S(2)}) copy-start(f32[512,768]{1,0:T(8,128)} %copy-done.6) | copy-start | bytes 4718596
  208.8 20.3 %copy-start.31 = (bf16[768,3072]{1,0:T(8,128)(2,1)S(1)}, bf16[768,3072]{1,0:T(8,128)(2,1)}, u32[]{:S(2)}) copy-start(bf16[768,3072]{1,0:T(8,128)(2,1)} %all-gather.9.cloned.1.call-done) | copy-start | bytes 14155780
  229.1 3.0 copy-start.32
  229.1 3.0 copy-start.8
  232.1 2.0 copy-start.12
  233.2 0.9 copy-start.13
  244.7 155.2 %reduce-scatter.5.cloned.1.call-start = ((), (), s32[]{:S(2)}) async-start(), calls=%async_computation.8 | async-start | bytes 7520256 | tf_op jit(solution)/shard_map/reduce_scatter | solution.py:253
  249.6 4.5 copy-start.5
  255.2 1.2 copy-start.17
  263.4 1.9 copy-start.11
  263.9 1.4 copy-start.3
  270.3 244.6 %reduce-scatter.9.cloned.1.call-start = ((), (), s32[]{:S(2)}) async-start(), calls=%async_computation.10 | async-start | bytes 10027008 | tf_op jit(solution)/shard_map/reduce_scatter | solution.py:237
  279.7 351.0 %reduce-scatter.11.cloned.1.call-start = ((), (), s32[]{:S(2)}) async-start(), calls=%async_computation.11 | async-start | bytes 10027008 | tf_op jit(solution)/shard_map/reduce_scatter | solution.py:239
  279.7 7.9 %copy-start.16 = (bf16[512,768]{1,0:T(8,128)(2,1)S(1)}, bf16[512,768]{1,0:T(8,128)(2,1)}, u32[]{:S(2)}) copy-start(bf16[512,768]{1,0:T(8,128)(2,1)} %multiply_convert_fusion.4) | copy-start | bytes 2359300
  286.0 1.6 copy-start.14
  292.8 0.7 copy-start.27
  292.8 2.0 copy-start.30
  292.8 2.0 copy-start.25
  292.8 2.3 copy-start.1
  292.8 2.3 copy-start.19
  292.8 2.3 copy-start.21
  292.8 417.6 %all-reduce.24.cloned.1.call-start = ((), (), s32[]{:S(2)}) async-start(), calls=%async_computation.12 | async-start | bytes 1769472 | tf_op jit(solution)/shard_map/psum | solution.py:262
  295.1 5.0 copy-start.29
  295.1 5.0 copy-start.23
  302.7 400.9 %copy-start.9 = (f32[512,768]{1,0:T(8,128)S(1)}, f32[512,768]{1,0:T(8,128)}, u32[]{:S(2)}) copy-start(f32[512,768]{1,0:T(8,128)} %copy-done.6) | copy-start | bytes 4718596
Sparse Core Ops, SparseCore 0:
  10.3 49.8 all-gather.4
  62.5 37.3 all-gather.6
  102.2 52.4 all-gather.8
  156.8 51.9 all-gather.10
  244.8 61.5 reduce-scatter.6
  310.8 89.0 reduce-scatter.4
  404.0 110.8 reduce-scatter.8
  519.5 111.1 reduce-scatter.10
  634.3 36.7 all-reduce.23
where the time goes:
time: 728 us; the launch traced here: 724 us
  waiting for transfers between devices  404 us (55%)
  blocking collectives  130 us (18%)
  matrix products  87.6 us (12%)
  other arithmetic  43.3 us (6%)
  local copies, waits for them, and re-layouts  41.5 us (6%)
  between operations  17.3 us (2%)
    unnamed x2, blocking collectives  124 us
    reduce_scatter x1, waiting for transfers between devices, per_device(): lax.psum_scatter(fc2_grad, 'fsdp', scatter_dimension=0, tiled=True)  114 us
    reduce_scatter x1, waiting for transfers between devices, per_device(): lax.psum_scatter(fc1_grad, 'fsdp', scatter_dimension=0, tiled=True)  113 us
    reduce_scatter x1, waiting for transfers between devices, per_device(): lax.psum_scatter(qkv_grad, 'fsdp', scatter_dimension=0, tiled=True)  91.9 us
    all_gather x1, waiting for transfers between devices, per_device(): lax.all_gather(fc2_weight, 'fsdp', axis=0, tiled=True)  45.9 us
    all_gather x1, waiting for transfers between devices, per_device(): lax.all_gather(fc1_weight, 'fsdp', axis=0, tiled=True)  32.3 us
    dot_general x4, matrix products, times_transpose(): lax.dot_general(left, right, (((1,), (1,)), ((), ())), preferred_element_...  31.4 us
    dot_general x4, matrix products, inner_rows(): lax.dot_general(left, right, (((0,), (0,)), ((), ())), preferred_element_...  21.4 us
  transfers between devices with their start and end apart: 9, of which 6 were waited for; matrix products, arithmetic and copies ran while one was open for 17% of the time, Pallas kernels for 0%

commit v1 on v0

--- a/solution.py
+++ b/solution.py
@@ -1,6 +1,8 @@
 import jax
 import jax.numpy as jnp
 from jax import lax
+from jax.experimental import pallas as pl
+from jax.experimental.pallas import tpu as pltpu
 from jax.sharding import PartitionSpec as P
 
 HEADS = 12
@@ -290,6 +292,564 @@
     )
 
 
+BIT_Z1, BIT_Z0, BIT_Y, BIT_C = 8, 4, 2, 1
+PIECE = 48
+WIDE = 768
+SCALE_ON = 1.0 / 0.9
+VMEM_BYTES = 56 * 1024 * 1024
+f32 = jnp.float32
+bf16 = jnp.bfloat16
+
+
+def hop(array, bit):
+    return lax.ppermute(array, "fsdp", [(i, i ^ bit) for i in range(16)])
+
+
+def swap(array):
+    return lax.ppermute(array, "dp", [(0, 1), (1, 0)])
+
+
+def join(*arrays):
+    return jnp.concatenate(arrays, axis=0)
+
+
+def gather_group(halves, x):
+    mine = jnp.where(x == 0, halves[0], halves[1])
+    pair = jnp.stack([mine, hop(mine, BIT_Z1)], axis=1)
+    far = hop(pair, BIT_Z0)
+    line0 = join(pair[0], far[0])
+    line1 = join(pair[1], far[1])
+    wide0 = join(line0, hop(line0, BIT_Y))
+    wide1 = join(line1, swap(line1))
+    own = (wide0, swap(wide0), wide1, hop(wide1, BIT_Y))
+    other = tuple(hop(part, BIT_C) for part in own)
+    return own + other
+
+
+def plus(left, right):
+    return (left.astype(f32) + right.astype(f32)).astype(bf16)
+
+
+def scatter_group(own, away):
+    came = hop(away, BIT_C)
+    keep0, send0, keep1, send1 = [plus(own[a], came[a]) for a in range(4)]
+    got0 = swap(send0)
+    got1 = hop(send1, BIT_Y)
+    keep0, send0 = plus(keep0[:4], got0[:4]), plus(keep0[4:], got0[4:])
+    keep1, send1 = plus(keep1[:4], got1[:4]), plus(keep1[4:], got1[4:])
+    got0 = hop(send0, BIT_Y)
+    got1 = swap(send1)
+    keep = jnp.stack([plus(keep0[:2], got0[:2]), plus(keep1[:2], got1[:2])])
+    send = jnp.stack([plus(keep0[2:], got0[2:]), plus(keep1[2:], got1[2:])])
+    got = hop(send, BIT_Z0)
+    keep, send = plus(keep[:, 0], got[:, 0]), plus(keep[:, 1], got[:, 1])
+    mine = plus(keep, hop(send, BIT_Z1))
+    return mine, swap(mine)
+
+
+def place(mine, other, x, half, line):
+    return jnp.where(x == half, mine[line], other[line]).astype(f32)
+
+
+def product(left, right, dims):
+    return lax.dot_general(left, right, (dims, ((), ())), preferred_element_type=f32)
+
+
+NN = ((1,), (0,))
+NT = ((1,), (1,))
+TN = ((0,), (0,))
+
+
+def slot(line, xr, yr):
+    return (xr, yr) if line == 0 else (2 + yr, xr)
+
+
+def load_chunk(store, refs, i, line, xr):
+    for m in range(16):
+        c, yr, z0r, z1r = m & 1, (m >> 1) & 1, (m >> 2) & 1, (m >> 3) & 1
+        array, part = slot(line, xr, yr) if isinstance(xr, int) else (2 + yr, xr)
+        row = pl.multiple_of((i ^ m) * PIECE, 16)
+        store[pl.ds(row, PIECE), :] = refs[4 * c + array][part * 4 + z0r * 2 + z1r]
+
+
+def save_chunk(value, outs, i, line, xr):
+    for m in range(16):
+        c, yr, z0r, z1r = m & 1, (m >> 1) & 1, (m >> 2) & 1, (m >> 3) & 1
+        array, part = slot(line, xr, yr) if isinstance(xr, int) else (2 + yr, xr)
+        row = pl.multiple_of((i ^ m) * PIECE, 16)
+        outs[c][array, part * 4 + z0r * 2 + z1r] = value[pl.ds(row, PIECE), :]
+
+
+def row_facts(info, r):
+    first = info[2 + 3 * r]
+    second = first + info[3 + 3 * r]
+    third = second + info[4 + 3 * r]
+
+    def segment(shape, axis):
+        t = lax.broadcasted_iota(jnp.int32, shape, axis)
+        return (t >= first).astype(jnp.int32) + (t >= second).astype(jnp.int32) + (t >= third).astype(jnp.int32)
+
+    column = segment((256, 1), 0)
+
+    def scale(branch):
+        keeps = [info[8 + 6 * r + 2 * j + branch].astype(f32) * SCALE_ON for j in range(3)]
+        return jnp.where(
+            column == 0, keeps[0], jnp.where(column == 1, keeps[1], jnp.where(column == 2, keeps[2], 0.0))
+        )
+
+    inside = jnp.where(column < 3, 1.0, 0.0).astype(f32)
+    return column, segment((1, 256), 1), scale, inside
+
+
+def unit_of(values):
+    center = values - jnp.mean(values, axis=-1, keepdims=True)
+    spread = jnp.mean(center * center, axis=-1, keepdims=True)
+    root = lax.rsqrt(spread + EPSILON)
+    return center * root, root
+
+
+def unit_back(unit, root, gain, incoming):
+    eg = incoming * gain
+    return root * (
+        eg - jnp.mean(eg, axis=-1, keepdims=True) - unit * jnp.mean(eg * unit, axis=-1, keepdims=True)
+    )
+
+
+def sums(values):
+    return jnp.sum(values, axis=0, keepdims=True)
+
+
+def qkv_kernel(info, tok, small, *rest):
+    refs, (packed, normed, weight) = rest[:8], rest[8:]
+    i, x = info[0], info[1]
+    for line in range(2):
+        for xr in range(2):
+            load_chunk(weight.at[line, x ^ xr], refs, i, line, xr)
+    for r in range(2):
+        rows = slice(256 * r, 256 * r + 256)
+        unit, _ = unit_of(tok[rows, :].astype(f32))
+        normed[rows, :] = (unit * small[0:1, :] + small[1:2, :]).astype(bf16)
+    for r in range(2):
+        rows = slice(256 * r, 256 * r + 256)
+        low = normed[rows, :]
+        packed[rows, 0:768] = (product(low, weight[1, 0], NN) + small[2:3, :]).astype(bf16)
+        packed[rows, 768:1536] = product(low, weight[0, 0], NN).astype(bf16)
+        packed[rows, 1536:2304] = (product(low, weight[0, 1], NN) + small[3:4, :]).astype(bf16)
+
+
+def attend_kernel(info, packed, tok, cot, small, *rest):
+    refs, (attended, middle, normed, grad_two, lse, weight) = rest[:8], rest[8:]
+    i, x, r = info[0], info[1], pl.program_id(0)
+
+    @pl.when(r == 0)
+    def _():
+        load_chunk(weight, refs, i, 1, x ^ 1)
+
+    column, across, scale, inside = row_facts(info, r)
+    same = column == across
+    lane = lax.broadcasted_iota(jnp.int32, (256, 128), 1)
+    kept = jnp.zeros((256, 128), f32)
+    for h in range(0, HEADS, 2):
+        pair = []
+        for g in (h, h + 1):
+            query = packed[:, 64 * g : 64 * g + 64] * 0.125
+            scores = product(query, packed[:, 768 + 64 * g : 832 + 64 * g], NT)
+            scores = jnp.where(same, scores, NEGATIVE)
+            top = jnp.max(scores, axis=-1, keepdims=True)
+            raised = jnp.exp(scores - top)
+            total = jnp.sum(raised, axis=-1, keepdims=True)
+            low = (raised / total).astype(bf16)
+            pair.append(product(low, packed[:, 1536 + 64 * g : 1600 + 64 * g], NN).astype(bf16))
+            kept = jnp.where(lane == g, top + jnp.log(total), kept)
+        attended[:, 64 * h : 64 * h + 128] = jnp.concatenate(pair, axis=1)
+    lse[...] = kept
+    branch = product(attended[...], weight[...], NN) + small[4:5, :]
+    after = tok[...].astype(f32) + scale(0) * branch
+    middle[...] = after
+    unit, _ = unit_of(after)
+    normed[...] = (unit * small[5:6, :] + small[6:7, :]).astype(bf16)
+    grad_two[...] = (cot[...].astype(f32) * inside * scale(1)).astype(bf16)
+
+
+def up_kernel(info, normed, grad_two, small, *rest):
+    refs, (hidden, active, own, away, weight, grad) = rest[:8], rest[8:]
+    i, x, t = info[0], info[1], pl.program_id(0)
+    block = ((t & 1) ^ x) * 2 + (t >> 1)
+    for step in range(4):
+
+        @pl.when(t == step)
+        def _():
+            load_chunk(weight, refs, i, step >> 1, step & 1)
+
+    value = product(normed[...], weight[...], NN) + small[pl.ds(8 + block, 1), :]
+    hidden[0] = value
+    low = (0.5 * value * (1.0 + lax.erf(value * (0.5**0.5)))).astype(bf16)
+    active[0] = low
+    grad[...] = product(low, grad_two[...], TN).astype(bf16)
+    far = block ^ (i >> 2)
+    spot = (far & 1) * 2 + (far >> 1)
+    for line in range(2):
+        for xr in range(2):
+            for near in range(4):
+                c, yr = near & 1, near >> 1
+                array, part = slot(line, xr, yr)
+                row = ((i & 3) ^ near) * 192 + ((xr ^ x) * 2 + line) * PIECE
+                (own, away)[c][array, part * 4 + spot] = grad[pl.ds(pl.multiple_of(row, 16), PIECE), :]
+
+
+def down_kernel(info, normed, grad_two, hidden, active, middle, cot, small, *rest):
+    refs1, refs2, outs = rest[:8], rest[8:16], rest[16:]
+    result, grad_middle, grad_one, bias, own, away, weight1, weight2, branch, grad_normed, grad = outs
+    i, x, t = info[0], info[1], pl.program_id(0)
+    block = ((t & 1) ^ x) * 2 + (t >> 1)
+    for step in range(4):
+
+        @pl.when(t == step)
+        def _():
+            load_chunk(weight1, refs1, i, step >> 1, step & 1)
+
+    far = block ^ (i >> 2)
+    spot = (far & 1) * 2 + (far >> 1)
+    for line in range(2):
+        for xr in range(2):
+            for near in range(4):
+                c, yr = near & 1, near >> 1
+                array, part = slot(line, xr, yr)
+                row = ((i & 3) ^ near) * 192 + ((xr ^ x) * 2 + line) * PIECE
+                weight2[pl.ds(pl.multiple_of(row, 16), PIECE), :] = refs2[4 * c + array][part * 4 + spot]
+
+    @pl.when(t == 0)
+    def _():
+        branch[...] = jnp.zeros_like(branch)
+        grad_normed[...] = jnp.zeros_like(grad_normed)
+        bias[...] = jnp.zeros_like(bias)
+        bias[7:8, :] = sums(grad_two[...].astype(f32))
+
+    branch[...] += product(active[0], weight2[...], NN)
+    value = hidden[0]
+    slope = 0.5 * (1.0 + lax.erf(value * (0.5**0.5))) + value * (
+        jnp.exp(-0.5 * value * value) * 0.3989422804014327
+    )
+    low = (product(grad_two[...], weight2[...], NT) * slope).astype(bf16)
+    bias[pl.ds(8 + block, 1), :] = sums(low.astype(f32))
+    grad_normed[...] += product(low, weight1[...], NT)
+    grad[...] = product(normed[...], low, TN).astype(bf16)
+    for step in range(4):
+
+        @pl.when(t == step)
+        def _():
+            save_chunk(grad, (own, away), i, step >> 1, step & 1)
+
+    @pl.when(t == 3)
+    def _():
+        for r in range(2):
+            rows = slice(256 * r, 256 * r + 256)
+            _, _, scale, inside = row_facts(info, r)
+            after = middle[rows, :]
+            result[rows, :] = (
+                (after + scale(1) * (branch[rows, :] + small[7:8, :])) * inside
+            ).astype(bf16)
+            unit, root = unit_of(after)
+            incoming = grad_normed[rows, :]
+            bias[5:6, :] += sums(incoming * unit)
+            bias[6:7, :] += sums(incoming)
+            total = cot[rows, :].astype(f32) * inside + unit_back(unit, root, small[5:6, :], incoming)
+            grad_middle[rows, :] = total
+            low_one = (total * scale(0)).astype(bf16)
+            grad_one[rows, :] = low_one
+            bias[4:5, :] += sums(low_one.astype(f32))
+
+
+def attend_back_kernel(info, packed, lse, attended, grad_one, *rest):
+    refs, (grad_packed, proj_grad, weight, total) = rest[:8], rest[8:]
+    i, x, r = info[0], info[1], pl.program_id(0)
+
+    @pl.when(r == 0)
+    def _():
+        load_chunk(weight, refs, i, 1, x ^ 1)
+        total[...] = jnp.zeros_like(total)
+
+    column, across, _, _ = row_facts(info, r)
+    same = column == across
+    total[...] += product(attended[...], grad_one[...], TN)
+
+    @pl.when(r == 1)
+    def _():
+        proj_grad[...] = total[...].astype(bf16)
+
+    grad_attended = product(grad_one[...], weight[...], NT).astype(bf16)
+    for h in range(0, HEADS, 2):
+        pairs = ([], [], [])
+        for g in (h, h + 1):
+            query = packed[:, 64 * g : 64 * g + 64] * 0.125
+            key = packed[:, 768 + 64 * g : 832 + 64 * g]
+            value = packed[:, 1536 + 64 * g : 1600 + 64 * g]
+            back = grad_attended[:, 64 * g : 64 * g + 64]
+            scores = product(query, key, NT)
+            weighting = jnp.where(same, jnp.exp(scores - lse[:, g : g + 1]), 0.0)
+            grad_weighting = product(back, value, NT)
+            pairs[2].append(product(weighting.astype(bf16), back, TN))
+            inner = jnp.sum(grad_weighting * weighting, axis=-1, keepdims=True)
+            low = (weighting * (grad_weighting - inner)).astype(bf16)
+            pairs[0].append(product(low, key, NN) * 0.125)
+            pairs[1].append(product(low, query, TN))
+        for k in range(3):
+            grad_packed[:, 768 * k + 64 * h : 768 * k + 64 * h + 128] = jnp.concatenate(
+                pairs[k], axis=1
+            ).astype(bf16)
+
+
+def qkv_back_kernel(info, tok, normed, grad_packed, grad_middle, proj_grad, bias_in, small, *rest):
+    refs, (tokens_grad, bias, own, away, weight, grad) = rest[:8], rest[8:]
+    i, x = info[0], info[1]
+    for line in range(2):
+        for xr in range(2):
+            load_chunk(weight.at[line, x ^ xr], refs, i, line, xr)
+    bias[...] = bias_in[...]
+    bias[2:3, :] = sums(grad_packed[:, 0:768].astype(f32))
+    bias[3:4, :] = sums(grad_packed[:, 1536:2304].astype(f32))
+    grad[1, 0] = product(normed[...], grad_packed[:, 0:768], TN).astype(bf16)
+    grad[0, 0] = product(normed[...], grad_packed[:, 768:1536], TN).astype(bf16)
+    grad[0, 1] = product(normed[...], grad_packed[:, 1536:2304], TN).astype(bf16)
+    grad[1, 1] = proj_grad[...]
+    for line in range(2):
+        for xr in range(2):
+            save_chunk(grad.at[line, x ^ xr], (own, away), i, line, xr)
+    bias[0:2, :] = jnp.zeros((2, WIDE), f32)
+    for r in range(2):
+        rows = slice(256 * r, 256 * r + 256)
+        incoming = (
+            product(grad_packed[rows, 0:768], weight[1, 0], NT)
+            + product(grad_packed[rows, 768:1536], weight[0, 0], NT)
+            + product(grad_packed[rows, 1536:2304], weight[0, 1], NT)
+        )
+        unit, root = unit_of(tok[rows, :].astype(f32))
+        bias[0:1, :] += sums(incoming * unit)
+        bias[1:2, :] += sums(incoming)
+        tokens_grad[rows, :] = grad_middle[rows, :] + unit_back(unit, root, small[0:1, :], incoming)
+
+
+def whole(shape):
+    return pl.BlockSpec(shape, lambda *_: (0,) * len(shape))
+
+
+def rowwise(width):
+    return pl.BlockSpec((256, width), lambda r, info: (r, 0))
+
+
+def steps(shape):
+    return pl.BlockSpec((1,) + shape, lambda t, info: (t, 0, 0))
+
+
+def run_kernel(kernel, grid, operands, outs, scratch, flops, moved):
+    info = operands[0]
+    specs = [spec or whole(array.shape) for spec, array in operands[1]]
+    return pl.pallas_call(
+        kernel,
+        grid_spec=pltpu.PrefetchScalarGridSpec(
+            num_scalar_prefetch=1,
+            grid=(grid,),
+            in_specs=specs,
+            out_specs=[spec or whole(shape) for spec, shape, _ in outs],
+            scratch_shapes=[pltpu.VMEM(shape, dtype) for shape, dtype in scratch],
+        ),
+        out_shape=[jax.ShapeDtypeStruct(shape, dtype) for _, shape, dtype in outs],
+        compiler_params=pltpu.CompilerParams(
+            dimension_semantics=("arbitrary",), vmem_limit_bytes=VMEM_BYTES
+        ),
+        cost_estimate=pl.CostEstimate(flops=flops, bytes_accessed=moved, transcendentals=0),
+    )(info, *[array for _, array in operands[1]])
+
+
+def fast_device(
+    tokens,
+    lengths,
+    keep_mask,
+    cotangent,
+    ln1_gain,
+    ln1_bias,
+    qkv_weight,
+    q_bias,
+    v_bias,
+    proj_weight,
+    proj_bias,
+    ln2_gain,
+    ln2_bias,
+    fc1_weight,
+    fc1_bias,
+    fc2_weight,
+    fc2_bias,
+):
+    count = tokens.shape[0] * tokens.shape[1]
+    i = lax.axis_index("fsdp")
+    x = lax.axis_index("dp")
+    info = jnp.concatenate(
+        [jnp.stack([i, x]).astype(jnp.int32), lengths.reshape(-1), keep_mask.reshape(-1)]
+    )
+    tok = tokens.reshape(count, WIDE)
+    cot = cotangent.reshape(count, WIDE)
+
+    line = jnp.concatenate(
+        [ln1_gain, ln1_bias, q_bias, v_bias, proj_bias, ln2_gain, ln2_bias, fc2_bias, fc1_bias]
+    ).reshape(1, 576)
+    line = jnp.pad(line, ((0, 0), (0, WIDE - 576)))
+    for bit in (BIT_Z1, BIT_Z0, BIT_Y, BIT_C):
+        line = join(line, hop(line, bit))
+    order = jnp.array([(m & 1) * 8 + (m >> 1 & 1) * 4 + (m >> 2 & 1) * 2 + (m >> 3) for m in range(16)])
+    turned = jnp.arange(16)[:, None] == (order ^ i)[None, :]
+    line = jnp.dot(turned.astype(bf16), line, preferred_element_type=f32)
+    small = jnp.concatenate(
+        [
+            line[:, :384].reshape(16, 8, 48).transpose(1, 0, 2).reshape(8, WIDE),
+            line[:, 384:576].reshape(4, WIDE),
+            jnp.zeros((4, WIDE), f32),
+        ]
+    )
+
+    query, key, value = (qkv_weight[:, WIDE * k : WIDE * k + WIDE] for k in range(3))
+    first = gather_group(jnp.stack([jnp.stack([key, query]), jnp.stack([value, proj_weight])]), x)
+    up = gather_group(fc1_weight.reshape(PIECE, 2, 2, WIDE).transpose(1, 2, 0, 3), x)
+    down = gather_group(fc2_weight.reshape(2, 2, PIECE, WIDE), x)
+
+    def full(arrays):
+        return [(None, array) for array in arrays]
+
+    parts = (4, 8, PIECE, WIDE)
+    packed, normed_one = run_kernel(
+        qkv_kernel,
+        1,
+        (info, full((tok, small) + first)),
+        [(None, (count, 3 * WIDE), bf16), (None, (count, WIDE), bf16)],
+        [((2, 2, WIDE, WIDE), bf16)],
+        2 * count * WIDE * 3 * WIDE,
+        10 << 20,
+    )
+    attended, middle, normed_two, grad_two, lse = run_kernel(
+        attend_kernel,
+        2,
+        (
+            info,
+            [(rowwise(3 * WIDE), packed), (rowwise(WIDE), tok), (rowwise(WIDE), cot), (None, small)]
+            + full(first),
+        ),
+        [
+            (rowwise(WIDE), (count, WIDE), bf16),
+            (rowwise(WIDE), (count, WIDE), f32),
+            (rowwise(WIDE), (count, WIDE), bf16),
+            (rowwise(WIDE), (count, WIDE), bf16),
+            (rowwise(128), (count, 128), f32),
+        ],
+        [((WIDE, WIDE), bf16)],
+        8 * count * WIDE * WIDE,
+        16 << 20,
+    )
+    hidden, active, fc2_own, fc2_away = run_kernel(
+        up_kernel,
+        4,
+        (info, full((normed_two, grad_two, small) + up)),
+        [
+            (steps((count, WIDE)), (4, count, WIDE), f32),
+            (steps((count, WIDE)), (4, count, WIDE), bf16),
+            (None, parts, bf16),
+            (None, parts, bf16),
+        ],
+        [((WIDE, WIDE), bf16), ((WIDE, WIDE), bf16)],
+        16 * count * WIDE * WIDE,
+        20 << 20,
+    )
+    output, grad_middle, grad_one, bias, fc1_own, fc1_away = run_kernel(
+        down_kernel,
+        4,
+        (
+            info,
+            full((normed_two, grad_two))
+            + [(steps((count, WIDE)), hidden), (steps((count, WIDE)), active)]
+            + full((middle, cot, small) + up + down),
+        ),
+        [
+            (None, (count, WIDE), bf16),
+            (None, (count, WIDE), f32),
+            (None, (count, WIDE), bf16),
+            (None, (16, WIDE), f32),
+            (None, parts, bf16),
+            (None, parts, bf16),
+        ],
+        [
+            ((WIDE, WIDE), bf16),
+            ((WIDE, WIDE), bf16),
+            ((count, WIDE), f32),
+            ((count, WIDE), f32),
+            ((WIDE, WIDE), bf16),
+        ],
+        32 * count * WIDE * WIDE,
+        30 << 20,
+    )
+    grad_packed, proj_grad = run_kernel(
+        attend_back_kernel,
+        2,
+        (
+            info,
+            [
+                (rowwise(3 * WIDE), packed),
+                (rowwise(128), lse),
+                (rowwise(WIDE), attended),
+                (rowwise(WIDE), grad_one),
+            ]
+            + full(first),
+        ),
+        [(rowwise(3 * WIDE), (count, 3 * WIDE), bf16), (None, (WIDE, WIDE), bf16)],
+        [((WIDE, WIDE), bf16), ((WIDE, WIDE), f32)],
+        16 * count * WIDE * WIDE,
+        16 << 20,
+    )
+    tokens_grad, bias, qkv_own, qkv_away = run_kernel(
+        qkv_back_kernel,
+        1,
+        (info, full((tok, normed_one, grad_packed, grad_middle, proj_grad, bias, small) + first)),
+        [
+            (None, (count, WIDE), f32),
+            (None, (16, WIDE), f32),
+            (None, parts, bf16),
+            (None, parts, bf16),
+        ],
+        [((2, 2, WIDE, WIDE), bf16), ((2, 2, WIDE, WIDE), bf16)],
+        12 * count * WIDE * WIDE,
+        20 << 20,
+    )
+
+    down_mine, down_other = scatter_group(fc2_own, fc2_away)
+    up_mine, up_other = scatter_group(fc1_own, fc1_away)
+    qkv_mine, qkv_other = scatter_group(qkv_own, qkv_away)
+    for bit in (BIT_C, BIT_Y, BIT_Z0, BIT_Z1):
+        bias = bias + hop(bias, bit)
+    bias = bias + swap(bias)
+    narrow = lax.dynamic_slice(bias[:8].reshape(8, 16, 48), (0, i, 0), (8, 1, 48)).reshape(8, 48)
+    broad = lax.dynamic_slice(bias[8:12].reshape(3072), (i * 192,), (192,))
+
+    fc1_grad = jnp.concatenate([place(up_mine, up_other, x, k >> 1, k & 1) for k in range(4)], axis=1)
+    fc2_grad = jnp.concatenate([place(down_mine, down_other, x, k >> 1, k & 1) for k in range(4)], axis=0)
+    qkv_grad = jnp.concatenate(
+        [place(qkv_mine, qkv_other, x, half, row) for half, row in ((0, 1), (0, 0), (1, 0))], axis=1
+    )
+    return (
+        output.reshape(tokens.shape),
+        tokens_grad.reshape(tokens.shape),
+        narrow[0],
+        narrow[1],
+        qkv_grad,
+        narrow[2],
+        narrow[3],
+        place(qkv_mine, qkv_other, x, 1, 1),
+        narrow[4],
+        narrow[5],
+        narrow[6],
+        fc1_grad,
+        broad,
+        fc2_grad,
+        narrow[7],
+    )
+
+
 def solution(mesh):
     in_specs = (
         P(("dp", "fsdp"), None, None),
@@ -327,6 +887,7 @@
         P("fsdp", None),
         P("fsdp"),
     )
+    fits = mesh.shape["dp"] == 2 and mesh.shape["fsdp"] == 16
     return jax.shard_map(
-        per_device, mesh=mesh, in_specs=in_specs, out_specs=out_specs, check_vma=False
-    )
+        fast_device if fits else per_device, mesh=mesh, in_specs=in_specs, out_specs=out_specs, check_vma=False
+    )

time: 728 us -> 317 us (0.44)
  waiting for transfers between devices: 404 us -> 129 us
  blocking collectives: 130 us -> 0 us
  Pallas kernels: 0 us -> 89.1 us
  matrix products: 87.6 us -> 0.12 us
  starting transfers between devices: 0.99 us -> 56.6 us
  local copies, waits for them, and re-layouts: 41.5 us -> 17.5 us
  other arithmetic: 43.3 us -> 22.4 us
  between operations: 17.3 us -> 1.42 us
    reduce_scatter x4 -> x0, waiting for transfers between devices: 323 us -> none  [the longest x1 114 us: per_device(): lax.psum_scatter(fc2_grad, 'fsdp', scatter_dimension=0, tiled=True)]
    ppermute x0 -> x63, waiting for transfers between devices: none -> 129 us  [the longest x47 81.9 us: hop(): return lax.ppermute(array, 'fsdp', [(i, i ^ bit) for i in range(16)])]
    unnamed x2 -> x0, blocking collectives: 124 us -> none
    pallas_call x0 -> x6, Pallas kernels: none -> 89.1 us  [run_kernel(): pl.pallas_call(kernel, grid_spec=pltpu.PrefetchScalarGridSpec(num_scalar_...]
    dot_general x18 -> x1, matrix products: 87.6 us -> 0.12 us  [fast_device(): line = jnp.dot(turned.astype(bf16), line, preferred_element_type=f32)]
    all_gather x4 -> x0, waiting for transfers between devices: 78.2 us -> none  [the longest x1 45.9 us: per_device(): lax.all_gather(fc2_weight, 'fsdp', axis=0, tiled=True)]
    ppermute x0 -> x63, starting transfers between devices: none -> 56.6 us  [the longest x47 37.1 us: hop(): return lax.ppermute(array, 'fsdp', [(i, i ^ bit) for i in range(16)])]
    convert_element_type x33 -> x18, other arithmetic: 32.8 us -> 11.6 us  [the longest x15 10.8 us: plus(): return (left.astype(f32) + right.astype(f32)).astype(bf16)]
  transfers between devices with their start and end apart: 9 -> 63, of which waited for: 6 -> 33; matrix products, arithmetic and copies ran while one was open for 17% -> 10% of each run, Pallas kernels for 0% -> 28%
where the time goes in v1:
time: 317 us
  waiting for transfers between devices  129 us (41%)
  Pallas kernels  89.1 us (28%)
  starting transfers between devices  56.6 us (18%)
  other arithmetic  22.4 us (7%)
  local copies, waits for them, and re-layouts  17.5 us (6%)
    pallas_call x6, Pallas kernels, run_kernel(): pl.pallas_call(kernel, grid_spec=pltpu.PrefetchScalarGridSpec(num_scalar_...  89.1 us
    ppermute x47, waiting for transfers between devices, hop(): return lax.ppermute(array, 'fsdp', [(i, i ^ bit) for i in range(16)])  81.9 us
    ppermute x16, waiting for transfers between devices, swap(): return lax.ppermute(array, 'dp', [(0, 1), (1, 0)])  47.5 us
    ppermute x47, starting transfers between devices, hop(): return lax.ppermute(array, 'fsdp', [(i, i ^ bit) for i in range(16)])  37.1 us
    ppermute x16, starting transfers between devices, swap(): return lax.ppermute(array, 'dp', [(0, 1), (1, 0)])  19.5 us
    convert_element_type x15, other arithmetic, plus(): return (left.astype(f32) + right.astype(f32)).astype(bf16)  10.8 us
  transfers between devices with their start and end apart: 63, of which 33 were waited for; matrix products, arithmetic and copies ran while one was open for 10% of the time, Pallas kernels for 28%

profile of v1, /device:TPU:0, one launch (start us, length us, event | category | flops | bytes accessed | tf_op | source)
XLA Modules:
  0.0 316.6 jit_solution(16050925713604143805)
XLA Ops:
  2.7 4.1 %collective-permute-start.4 = (bf16[2,48,768]{2,1,0:T(8,128)(2,1)S(1)}, bf16[2,48,768]{2,1,0:T(8,128)(2,1)S(1)}, u32[]{:S(2)}, u32[]{:S(2)}) collective-permute-start(bf16[2,48,768]{2,1,0:T(8,128)(2,1)S(1)} %maximum_select_fusion.1), channel_id=1, source_target_pairs={{0,8},{1,9},{2,10},{3,11},{4,12},{5,13},{6,14},{7,15},{8,0},{9,1},... | collective-permute-start | bytes 442376 | tf_op jit(solution)/shard_map/ppermute | solution.py:305
  6.8 6.1 %concatenate.99 = bf16[576]{0:T(1024)(128)(2,1)S(1)} concatenate(bf16[48]{0:T(256)(128)(2,1)} %param.22, bf16[48]{0:T(256)(128)(2,1)} %param.23, bf16[48]{0:T(256)(128)(2,1)} %param.25, bf16[48]{0:T(256)(128)(2,1)} %param.26, bf16[48]{0:T(256)(128)(2,1)} %param.28, bf16[48]{0:T(256)(128)(2,1)} %param.29, bf16[48]{0:T(256)(128)(2,1)} %param.30, bf16[48]{0:T(256)(128)(2,1)} %param.34, ...), dimensions={0} | concatenate | bytes 2304 | tf_op jit(solution)/shard_map/concatenate | solution.py:692
  13.3 3.0 collective-permute-start.14
  16.2 2.9 collective-permute-done
  19.5 3.5 %collective-permute-done.1 = bf16[2,768]{1,0:T(2,128)(2,1)S(1)} collective-permute-done((bf16[2,768]{1,0:T(2,128)(2,1)S(1)}, bf16[2,768]{1,0:T(2,128)(2,1)S(1)}, u32[]{:S(2)}, u32[]{:S(2)}) %collective-permute-start.1) | collective-permute-done | bytes 3104 | tf_op jit(solution)/shard_map/ppermute | solution.py:305
  24.7 2.1 collective-permute-done.2
  27.1 2.1 collective-permute-start.15
  29.9 6.9 %collective-permute-done.5 = bf16[2,2,48,768]{3,2,1,0:T(8,128)(2,1)S(1)} collective-permute-done((bf16[2,2,48,768]{3,2,1,0:T(8,128)(2,1)S(1)}, bf16[2,2,48,768]{3,2,1,0:T(8,128)(2,1)S(1)}, u32[]{:S(2)}, u32[]{:S(2)}) %collective-permute-start.5) | collective-permute-done | bytes 294944 | tf_op jit(solution)/shard_map/ppermute | solution.py:305
  40.1 3.1 collective-permute-done.15
  44.8 4.2 %collective-permute-done.25 = bf16[2,2,48,768]{3,2,1,0:T(8,128)(2,1)S(1)} collective-permute-done((bf16[2,2,48,768]{3,2,1,0:T(8,128)(2,1)S(1)}, bf16[2,2,48,768]{3,2,1,0:T(8,128)(2,1)S(1)}, u32[]{:S(2)}, u32[]{:S(2)}) %collective-permute-start.25) | collective-permute-done | bytes 294944 | tf_op jit(solution)/shard_map/ppermute | solution.py:305
  53.6 5.4 %collective-permute-done.18 = bf16[4,48,768]{2,1,0:T(8,128)(2,1)S(1)} collective-permute-done((bf16[4,48,768]{2,1,0:T(8,128)(2,1)S(1)}, bf16[4,48,768]{2,1,0:T(8,128)(2,1)S(1)}, u32[]{:S(2)}, u32[]{:S(2)}) %collective-permute-start.18) | collective-permute-done | bytes 294944 | tf_op jit(solution)/shard_map/ppermute | solution.py:309
  63.9 12.8 %collective-permute-done.28 = bf16[4,48,768]{2,1,0:T(8,128)(2,1)} collective-permute-done((bf16[4,48,768]{2,1,0:T(8,128)(2,1)}, bf16[4,48,768]{2,1,0:T(8,128)(2,1)}, u32[]{:S(2)}, u32[]{:S(2)}) %collective-permute-start.28) | collective-permute-done | bytes 294944 | tf_op jit(solution)/shard_map/ppermute | solution.py:309
  83.4 7.5 %collective-permute-done.17.rest_1_ = bf16[8,48,768]{2,1,0:T(8,128)(2,1)} collective-permute-done((bf16[8,48,768]{2,1,0:T(8,128)(2,1)S(1)}, bf16[8,48,768]{2,1,0:T(8,128)(2,1)}, u32[]{:S(2)}, u32[]{:S(2)}) %collective-permute-start.17) | collective-permute-done | bytes 589856 | tf_op jit(solution)/shard_map/ppermute | solution.py:309
  90.9 3.2 %collective-permute-done.19.rest_3_ = bf16[8,48,768]{2,1,0:T(8,128)(2,1)} collective-permute-done((bf16[8,48,768]{2,1,0:T(8,128)(2,1)S(1)}, bf16[8,48,768]{2,1,0:T(8,128)(2,1)}, u32[]{:S(2)}, u32[]{:S(2)}) %collective-permute-start.19) | collective-permute-done | bytes 589856 | tf_op jit(solution)/shard_map/ppermute | solution.py:305
  97.8 7.1 %shard_map.289 = (bf16[512,2304]{1,0:T(8,128)(2,1)}, bf16[512,768]{1,0:T(8,128)(2,1)}) custom-call(s32[20]{0:T(128)} %pad_add_fusion.info, bf16[512,768]{1,0:T(8,128)(2,1)} %bitcast.248, f32[16,768]{1,0:T(8,128)} %maximum_maximum_fusion.small, bf16[8,48,768]{2,1,0:T(8,128)(2,1)} %copy-done.4, bf16[8,48,768]{2,1,0:T(8,128)(2,1)} %collective-permute-done.7.rest_1_, ...), custom_call_target="tpu_custom_call" | custom-call | flops 1811939328 | bytes 10485760 | tf_op jit(solution)/shard_map/pallas_call | solution.py:647
  105.0 4.1 %collective-permute-done.27.rest_9_ = bf16[8,48,768]{2,1,0:T(8,128)(2,1)} collective-permute-done((bf16[8,48,768]{2,1,0:T(8,128)(2,1)S(1)}, bf16[8,48,768]{2,1,0:T(8,128)(2,1)}, u32[]{:S(2)}, u32[]{:S(2)}) %collective-permute-start.27) | collective-permute-done | bytes 589856 | tf_op jit(solution)/shard_map/ppermute | solution.py:309
  109.9 14.5 %shard_map.290 = (bf16[512,768]{1,0:T(8,128)(2,1)}, f32[512,768]{1,0:T(8,128)}, bf16[512,768]{1,0:T(8,128)(2,1)}, bf16[512,768]{1,0:T(8,128)(2,1)}, f32[512,128]{1,0:T(8,128)}) custom-call(s32[20]{0:T(128)} %pad_add_fusion.info, bf16[512,2304]{1,0:T(8,128)(2,1)} %get-tuple-element.38.packed, bf16[512,768]{1,0:T(8,128)(2,1)} %bitcast.249, ...), custom_call_target="tpu_custom_call" | custom-call | flops 2415919104 | bytes 16777216 | tf_op jit(solution)/shard_map/pallas_call | solution.py:647
  125.2 13.8 %shard_map.291 = (f32[4,512,768]{2,1,0:T(8,128)}, bf16[4,512,768]{2,1,0:T(8,128)(2,1)}, bf16[4,8,48,768]{3,2,1,0:T(8,128)(2,1)}, bf16[4,8,48,768]{3,2,1,0:T(8,128)(2,1)}) custom-call(s32[20]{0:T(128)} %pad_add_fusion.info, bf16[512,768]{1,0:T(8,128)(2,1)} %get-tuple-element.39.normed, bf16[512,768]{1,0:T(8,128)(2,1)} %get-tuple-element.40.grad_two, ...), custom_call_target="tpu_custom_call" | custom-call | flops 4831838208 | bytes 20971520 | tf_op jit(solution)/shard_map/pallas_call | solution.py:647
  140.7 24.3 %shard_map.292 = (bf16[512,768]{1,0:T(8,128)(2,1)}, f32[512,768]{1,0:T(8,128)}, bf16[512,768]{1,0:T(8,128)(2,1)}, f32[16,768]{1,0:T(8,128)}, bf16[4,8,48,768]{3,...) custom-call(s32[20]{0:T(128)} %pad_add_fusion.info, bf16[512,768]{1,0:T(8,128)(2,1)} %get-tuple-element.39.normed, ...), custom_call_target="tpu_custom_call" | custom-call | flops 9663676416 | bytes 31457280 | tf_op jit(solution)/shard_map/pallas_call | solution.py:647
  165.3 17.6 %shard_map.293 = (bf16[512,2304]{1,0:T(8,128)(2,1)}, bf16[768,768]{1,0:T(8,128)(2,1)}) custom-call(s32[20]{0:T(128)} %pad_add_fusion.info, bf16[512,2304]{1,0:T(8,128)(2,1)} %get-tuple-element.38.packed, f32[512,128]{1,0:T(8,128)} %get-tuple-element.46.lse, bf16[512,768]{1,0:T(8,128)(2,1)} %get-tuple-element.47.attended, ...), custom_call_target="tpu_custom_call" | custom-call | flops 4831838208 | bytes 16777216 | tf_op jit(solution)/shard_map/pallas_call | solution.py:647
  182.9 11.8 %shard_map.294 = (f32[512,768]{1,0:T(8,128)}, f32[16,768]{1,0:T(8,128)}, bf16[4,8,48,768]{3,2,1,0:T(8,128)(2,1)}, bf16[4,8,48,768]{3,2,1,0:T(8,128)(2,1)}) custom-call(s32[20]{0:T(128)} %pad_add_fusion.info, bf16[512,768]{1,0:T(8,128)(2,1)} %bitcast.250, bf16[512,768]{1,0:T(8,128)(2,1)} %get-tuple-element.45.normed, ...), custom_call_target="tpu_custom_call" | custom-call | flops 3623878656 | bytes 20971520 | tf_op jit(solution)/shard_map/pallas_call | solution.py:647
  195.2 3.5 %collective-permute-done.34 = f32[16,768]{1,0:T(8,128)S(1)} collective-permute-done((f32[16,768]{1,0:T(8,128)}, f32[16,768]{1,0:T(8,128)S(1)}, u32[]{:S(2)}, u32[]{:S(2)}) %collective-permute-start.34) | collective-permute-done | bytes 49184 | tf_op jit(solution)/shard_map/ppermute | solution.py:305
  201.1 2.6 collective-permute-done.35
  204.3 3.5 %collective-permute-done.36 = f32[16,768]{1,0:T(8,128)S(1)} collective-permute-done((f32[16,768]{1,0:T(8,128)S(1)}, f32[16,768]{1,0:T(8,128)S(1)}, u32[]{:S(2)}, u32[]{:S(2)}) %collective-permute-start.36) | collective-permute-done | bytes 49184 | tf_op jit(solution)/shard_map/ppermute | solution.py:305
  209.2 4.2 %collective-permute-done.37 = f32[16,768]{1,0:T(8,128)S(1)} collective-permute-done((f32[16,768]{1,0:T(8,128)S(1)}, f32[16,768]{1,0:T(8,128)S(1)}, u32[]{:S(2)}, u32[]{:S(2)}) %collective-permute-start.37) | collective-permute-done | bytes 49184 | tf_op jit(solution)/shard_map/ppermute | solution.py:305
  215.4 2.2 collective-permute-done.38
  220.4 4.1 %add_convert_fusion.3 = (bf16[1,8,48,768]{3,2,1,0:T(8,128)(2,1)S(1)}, bf16[8,48,768]{2,1,0:T(8,128)(2,1)}, bf16[1,8,48,768]{3,2,1,0:T(8,128)(2,1)S(1)}, bf16[8,48,768]{2,1,0:T(8,128)(2,1)}) fusion(bf16[4,8,48,768]{3,2,1,0:T(8,128)(2,1)} %copy-done.2, bf16[4,8,48,768]{3,2,1,0:T(8,128)(2,1)} %get-tuple-element.59), kind=kLoop, calls=%fused_computation.3 | loop fusion | flops 4718592 | bytes 7077888 | tf_op jit(solution)/shard_map/convert_element_type | solution.py:330
  231.2 2.3 add_convert_fusion.7
  234.2 2.3 add_convert_fusion.11
  236.5 2.0 collective-permute-start.40
  238.4 2.1 collective-permute-done.56
  240.5 2.0 collective-permute-start.42
  243.7 2.4 collective-permute-done.58
  247.8 5.2 %collective-permute-done.48 = bf16[8,48,768]{2,1,0:T(8,128)(2,1)S(1)} collective-permute-done((bf16[8,48,768]{2,1,0:T(8,128)(2,1)S(1)}, bf16[8,48,768]{2,1,0:T(8,128)(2,1)S(1)}, u32[]{:S(2)}, u32[]{:S(2)}) %collective-permute-start.48) | collective-permute-done | bytes 589856 | tf_op jit(solution)/shard_map/ppermute | solution.py:309
  253.0 2.4 collective-permute-start.59
  255.6 3.1 collective-permute-done.50
  260.4 5.2 %collective-permute-done.40 = bf16[8,48,768]{2,1,0:T(8,128)(2,1)S(1)} collective-permute-done((bf16[8,48,768]{2,1,0:T(8,128)(2,1)S(1)}, bf16[8,48,768]{2,1,0:T(8,128)(2,1)S(1)}, u32[]{:S(2)}, u32[]{:S(2)}) %collective-permute-start.40) | collective-permute-done | bytes 589856 | tf_op jit(solution)/shard_map/ppermute | solution.py:309
  265.7 2.4 collective-permute-start.51
  268.3 3.1 collective-permute-done.42
  273.1 4.7 %collective-permute-done.57 = bf16[4,48,768]{2,1,0:T(8,128)(2,1)S(1)} collective-permute-done((bf16[4,48,768]{2,1,0:T(8,128)(2,1)S(1)}, bf16[4,48,768]{2,1,0:T(8,128)(2,1)S(1)}, u32[]{:S(2)}, u32[]{:S(2)}) %collective-permute-start.57) | collective-permute-done | bytes 294944 | tf_op jit(solution)/shard_map/ppermute | solution.py:305
  278.2 3.6 %collective-permute-done.49 = bf16[4,48,768]{2,1,0:T(8,128)(2,1)S(1)} collective-permute-done((bf16[4,48,768]{2,1,0:T(8,128)(2,1)S(1)}, bf16[4,48,768]{2,1,0:T(8,128)(2,1)S(1)}, u32[]{:S(2)}, u32[]{:S(2)}) %collective-permute-start.49) | collective-permute-done | bytes 294944 | tf_op jit(solution)/shard_map/ppermute | solution.py:305
  282.3 2.7 collective-permute-done.41
  285.5 4.8 %collective-permute-done.60 = bf16[2,2,48,768]{3,2,0,1:T(8,128)(2,1)S(1)} collective-permute-done((bf16[2,2,48,768]{3,2,0,1:T(8,128)(2,1)S(1)}, bf16[2,2,48,768]{3,2,0,1:T(8,128)(2,1)S(1)}, u32[]{:S(2)}, u32[]{:S(2)}) %collective-permute-start.60) | collective-permute-done | bytes 294944 | tf_op jit(solution)/shard_map/ppermute | solution.py:305
  290.5 3.8 %collective-permute-done.52 = bf16[2,2,48,768]{3,2,0,1:T(8,128)(2,1)S(1)} collective-permute-done((bf16[2,2,48,768]{3,2,0,1:T(8,128)(2,1)S(1)}, bf16[2,2,48,768]{3,2,0,1:T(8,128)(2,1)S(1)}, u32[]{:S(2)}, u32[]{:S(2)}) %collective-permute-start.52) | collective-permute-done | bytes 294944 | tf_op jit(solution)/shard_map/ppermute | solution.py:305
  294.8 5.1 %collective-permute-done.44 = bf16[2,2,48,768]{3,2,1,0:T(8,128)(2,1)S(1)} collective-permute-done((bf16[2,2,48,768]{3,2,1,0:T(8,128)(2,1)S(1)}, bf16[2,2,48,768]{3,2,1,0:T(8,128)(2,1)S(1)}, u32[]{:S(2)}, u32[]{:S(2)}) %collective-permute-start.44) | collective-permute-done | bytes 294944 | tf_op jit(solution)/shard_map/ppermute | solution.py:305
  300.3 2.5 collective-permute-done.61
  303.0 5.1 %collective-permute-done.45 = bf16[2,48,768]{2,1,0:T(8,128)(2,1)S(1)} collective-permute-done((bf16[2,48,768]{2,1,0:T(8,128)(2,1)S(1)}, bf16[2,48,768]{2,1,0:T(8,128)(2,1)S(1)}, u32[]{:S(2)}, u32[]{:S(2)}) %collective-permute-start.45) | collective-permute-done | bytes 147488 | tf_op jit(solution)/shard_map/ppermute | solution.py:305
  310.4 3.0 collective-permute-done.46
  (242 shorter events, 65.2 us)
Async XLA Ops:
  2.7 24.2 %collective-permute-start.4 = (bf16[2,48,768]{2,1,0:T(8,128)(2,1)S(1)}, bf16[2,48,768]{2,1,0:T(8,128)(2,1)S(1)}, u32[]{:S(2)}, u32[]{:S(2)}) collective-permute-start(bf16[2,48,768]{2,1,0:T(8,128)(2,1)S(1)} %maximum_select_fusion.1), channel_id=1, source_target_pairs={{0,8},{1,9},{2,10},{3,11},{4,12},{5,13},{6,14},{7,15},{8,0},{9,1},... | collective-permute-start | bytes 442376 | tf_op jit(solution)/shard_map/ppermute | solution.py:305
  13.3 13.8 %collective-permute-start.14 = (bf16[2,48,768]{2,1,0:T(8,128)(2,1)S(1)}, bf16[2,48,768]{2,1,0:T(8,128)(2,1)S(1)}, u32[]{:S(2)}, u32[]{:S(2)}) collective-permute-start(bf16[2,48,768]{2,1,0:T(8,128)(2,1)S(1)} %get-tuple-element.118), channel_id=1, source_target_pairs={{0,8},{1,9},{2,10},{3,11},{4,12},{5,13},{6,14},{7,15},{8,0},{9,1},... | collective-permute-start | bytes 442376 | tf_op jit(solution)/shard_map/ppermute | solution.py:305
  26.8 26.1 %collective-permute-start.3 = (bf16[8,768]{1,0:T(8,128)(2,1)S(1)}, bf16[8,768]{1,0:T(8,128)(2,1)S(1)}, u32[]{:S(2)}, u32[]{:S(2)}) collective-permute-start(bf16[8,768]{1,0:T(8,128)(2,1)S(1)} %pad_maximum_fusion.21), channel_id=1, source_target_pairs={{0,1},{1,0},{2,3},{3,2},{4,5},{5,4},{6,7},{7,6},{8,9},{9,8},{10,11... | collective-permute-start | bytes 36872 | tf_op jit(solution)/shard_map/ppermute | solution.py:305
  27.1 16.1 %collective-permute-start.15 = (bf16[2,2,48,768]{3,2,1,0:T(8,128)(2,1)S(1)}, bf16[2,2,48,768]{3,2,1,0:T(8,128)(2,1)S(1)}, u32[]{:S(2)}, u32[]{:S(2)}) collective-permute-start(bf16[2,2,48,768]{3,2,1,0:T(8,128)(2,1)S(1)} %pad_maximum_fusion.7), channel_id=1, source_target_pairs={{0,4},{1,5},{2,6},{3,7},{4,0},{5,1},{6,2},{7,3},{8,12},{9,13},{10,... | collective-permute-start | bytes 884744 | tf_op jit(solution)/shard_map/ppermute | solution.py:305
  29.2 19.8 %collective-permute-start.25 = (bf16[2,2,48,768]{3,2,1,0:T(8,128)(2,1)S(1)}, bf16[2,2,48,768]{3,2,1,0:T(8,128)(2,1)S(1)}, u32[]{:S(2)}, u32[]{:S(2)}) collective-permute-start(bf16[2,2,48,768]{3,2,1,0:T(8,128)(2,1)S(1)} %pad_maximum_fusion.8), channel_id=1, source_target_pairs={{0,4},{1,5},{2,6},{3,7},{4,0},{5,1},{6,2},{7,3},{8,12},{9,13},{10,... | collective-permute-start | bytes 884744 | tf_op jit(solution)/shard_map/ppermute | solution.py:305
  36.9 13.7 %collective-permute-start.8 = (bf16[4,48,768]{2,1,0:T(8,128)(2,1)S(1)}, bf16[4,48,768]{2,1,0:T(8,128)(2,1)S(1)}, u32[]{:S(2)}, u32[]{:S(2)}) collective-permute-start(bf16[4,48,768]{2,1,0:T(8,128)(2,1)S(1)} %pad_maximum_fusion.10), channel_id=1, source_target_pairs={{0,16},{16,0},{1,17},{17,1},{2,18},{18,2},{3,19},{19,3},{4,20},{20... | collective-permute-start | bytes 884744 | tf_op jit(solution)/shard_map/ppermute | solution.py:309
  38.5 13.8 %collective-permute-start.6 = (bf16[4,48,768]{2,1,0:T(8,128)(2,1)S(1)}, bf16[4,48,768]{2,1,0:T(8,128)(2,1)S(1)}, u32[]{:S(2)}, u32[]{:S(2)}) collective-permute-start(bf16[4,48,768]{2,1,0:T(8,128)(2,1)S(1)} %pad_maximum_fusion.9), channel_id=1, source_target_pairs={{0,2},{1,3},{2,0},{3,1},{4,6},{5,7},{6,4},{7,5},{8,10},{9,11},{10,... | collective-permute-start | bytes 884744 | tf_op jit(solution)/shard_map/ppermute | solution.py:305
  43.2 10.4 %collective-permute-start.16 = (bf16[4,48,768]{2,1,0:T(8,128)(2,1)S(1)}, bf16[4,48,768]{2,1,0:T(8,128)(2,1)S(1)}, u32[]{:S(2)}, u32[]{:S(2)}) collective-permute-start(bf16[4,48,768]{2,1,0:T(8,128)(2,1)S(1)} %pad_maximum_fusion.11), channel_id=1, source_target_pairs={{0,2},{1,3},{2,0},{3,1},{4,6},{5,7},{6,4},{7,5},{8,10},{9,11},{10,... | collective-permute-start | bytes 884744 | tf_op jit(solution)/shard_map/ppermute | solution.py:305
  50.6 10.1 %collective-permute-start.26 = (bf16[4,48,768]{2,1,0:T(8,128)(2,1)S(1)}, bf16[4,48,768]{2,1,0:T(8,128)(2,1)}, u32[]{:S(2)}, u32[]{:S(2)}) collective-permute-start(bf16[4,48,768]{2,1,0:T(8,128)(2,1)S(1)} %pad_maximum_fusion.13), channel_id=1, source_target_pairs={{0,2},{1,3},{2,0},{3,1},{4,6},{5,7},{6,4},{7,5},{8,10},{9,11},{10,... | collective-permute-start | bytes 884744 | tf_op jit(solution)/shard_map/ppermute | solution.py:305
  52.3 25.9 %collective-permute-start.9 = (bf16[8,48,768]{2,1,0:T(8,128)(2,1)S(1)}, bf16[8,48,768]{2,1,0:T(8,128)(2,1)}, u32[]{:S(2)}, u32[]{:S(2)}) collective-permute-start(bf16[8,48,768]{2,1,0:T(8,128)(2,1)S(1)} %pad_maximum_fusion.1.rest_2_), channel_id=1, source_target_pairs={{0,2},{1,3},{2,0},{3,1},{4,6},{5,7},{6,4},{7,5},{8,10},{9,11},{10,... | collective-permute-start | bytes 1769480 | tf_op jit(solution)/shard_map/ppermute | solution.py:305
  53.0 25.3 %collective-permute-start.7 = (bf16[8,48,768]{2,1,0:T(8,128)(2,1)S(1)}, bf16[8,48,768]{2,1,0:T(8,128)(2,1)}, u32[]{:S(2)}, u32[]{:S(2)}) collective-permute-start(bf16[8,48,768]{2,1,0:T(8,128)(2,1)S(1)} %pad_maximum_fusion.rest_0_), channel_id=1, source_target_pairs={{0,16},{16,0},{1,17},{17,1},{2,18},{18,2},{3,19},{19,3},{4,20},{20... | collective-permute-start | bytes 1769480 | tf_op jit(solution)/shard_map/ppermute | solution.py:309
  53.6 26.2 %collective-permute-start.12 = (bf16[8,48,768]{2,1,0:T(8,128)(2,1)S(1)}, bf16[8,48,768]{2,1,0:T(8,128)(2,1)}, u32[]{:S(2)}, u32[]{:S(2)}) collective-permute-start(bf16[8,48,768]{2,1,0:T(8,128)(2,1)S(1)} %pad_maximum_fusion.1.rest_2_), channel_id=1, source_target_pairs={{0,1},{1,0},{2,3},{3,2},{4,5},{5,4},{6,7},{7,6},{8,9},{9,8},{10,11... | collective-permute-start | bytes 1769480 | tf_op jit(solution)/shard_map/ppermute | solution.py:305
  59.0 21.0 %collective-permute-start.10 = (bf16[8,48,768]{2,1,0:T(8,128)(2,1)S(1)}, bf16[8,48,768]{2,1,0:T(8,128)(2,1)}, u32[]{:S(2)}, u32[]{:S(2)}) collective-permute-start(bf16[8,48,768]{2,1,0:T(8,128)(2,1)S(1)} %pad_maximum_fusion.rest_0_), channel_id=1, source_target_pairs={{0,1},{1,0},{2,3},{3,2},{4,5},{5,4},{6,7},{7,6},{8,9},{9,8},{10,11... | collective-permute-start | bytes 1769480 | tf_op jit(solution)/shard_map/ppermute | solution.py:305
  60.7 16.0 %collective-permute-start.28 = (bf16[4,48,768]{2,1,0:T(8,128)(2,1)}, bf16[4,48,768]{2,1,0:T(8,128)(2,1)}, u32[]{:S(2)}, u32[]{:S(2)}) collective-permute-start(bf16[4,48,768]{2,1,0:T(8,128)(2,1)} %pad_maximum_fusion.14), channel_id=1, source_target_pairs={{0,16},{16,0},{1,17},{17,1},{2,18},{18,2},{3,19},{19,3},{4,20},{20... | collective-permute-start | bytes 884744 | tf_op jit(solution)/shard_map/ppermute | solution.py:309
  76.7 14.2 %collective-permute-start.17 = (bf16[8,48,768]{2,1,0:T(8,128)(2,1)S(1)}, bf16[8,48,768]{2,1,0:T(8,128)(2,1)}, u32[]{:S(2)}, u32[]{:S(2)}) collective-permute-start(bf16[8,48,768]{2,1,0:T(8,128)(2,1)S(1)} %pad_maximum_fusion.2.rest_0_), channel_id=1, source_target_pairs={{0,16},{16,0},{1,17},{17,1},{2,18},{18,2},{3,19},{19,3},{4,20},{20... | collective-permute-start | bytes 1769480 | tf_op jit(solution)/shard_map/ppermute | solution.py:309
  78.2 16.4 %collective-permute-start.20 = (bf16[8,48,768]{2,1,0:T(8,128)(2,1)S(1)}, bf16[8,48,768]{2,1,0:T(8,128)(2,1)}, u32[]{:S(2)}, u32[]{:S(2)}) collective-permute-start(bf16[8,48,768]{2,1,0:T(8,128)(2,1)S(1)} %pad_maximum_fusion.2.rest_0_), channel_id=1, source_target_pairs={{0,1},{1,0},{2,3},{3,2},{4,5},{5,4},{6,7},{7,6},{8,9},{9,8},{10,11... | collective-permute-start | bytes 1769480 | tf_op jit(solution)/shard_map/ppermute | solution.py:305
  78.2 15.8 %collective-permute-start.19 = (bf16[8,48,768]{2,1,0:T(8,128)(2,1)S(1)}, bf16[8,48,768]{2,1,0:T(8,128)(2,1)}, u32[]{:S(2)}, u32[]{:S(2)}) collective-permute-start(bf16[8,48,768]{2,1,0:T(8,128)(2,1)S(1)} %pad_maximum_fusion.3.rest_2_), channel_id=1, source_target_pairs={{0,2},{1,3},{2,0},{3,1},{4,6},{5,7},{6,4},{7,5},{8,10},{9,11},{10,... | collective-permute-start | bytes 1769480 | tf_op jit(solution)/shard_map/ppermute | solution.py:305
  79.8 16.3 %collective-permute-start.13 = (bf16[8,48,768]{2,1,0:T(8,128)(2,1)}, bf16[8,48,768]{2,1,0:T(8,128)(2,1)}, u32[]{:S(2)}, u32[]{:S(2)}) collective-permute-start(bf16[8,48,768]{2,1,0:T(8,128)(2,1)} %collective-permute-done.9.rest_3_), channel_id=1, source_target_pairs={{0,1},{1,0},{2,3},{3,2},{4,5},{5,4},{6,7},{7,6},{8,9},{9,8},{10,11... | collective-permute-start | bytes 1769480 | tf_op jit(solution)/shard_map/ppermute | solution.py:305
  80.0 16.6 %collective-permute-start.11 = (bf16[8,48,768]{2,1,0:T(8,128)(2,1)}, bf16[8,48,768]{2,1,0:T(8,128)(2,1)}, u32[]{:S(2)}, u32[]{:S(2)}) collective-permute-start(bf16[8,48,768]{2,1,0:T(8,128)(2,1)} %collective-permute-done.7.rest_1_), channel_id=1, source_target_pairs={{0,1},{1,0},{2,3},{3,2},{4,5},{5,4},{6,7},{7,6},{8,9},{9,8},{10,11... | collective-permute-start | bytes 1769480 | tf_op jit(solution)/shard_map/ppermute | solution.py:305
  90.9 14.0 %collective-permute-start.22 = (bf16[8,48,768]{2,1,0:T(8,128)(2,1)S(1)}, bf16[8,48,768]{2,1,0:T(8,128)(2,1)S(1)}, u32[]{:S(2)}, u32[]{:S(2)}) collective-permute-start(bf16[8,48,768]{2,1,0:T(8,128)(2,1)S(1)} %pad_maximum_fusion.3.rest_2_), channel_id=1, source_target_pairs={{0,1},{1,0},{2,3},{3,2},{4,5},{5,4},{6,7},{7,6},{8,9},{9,8},{10,11... | collective-permute-start | bytes 1769480 | tf_op jit(solution)/shard_map/ppermute | solution.py:305
  94.1 15.0 %collective-permute-start.27 = (bf16[8,48,768]{2,1,0:T(8,128)(2,1)S(1)}, bf16[8,48,768]{2,1,0:T(8,128)(2,1)}, u32[]{:S(2)}, u32[]{:S(2)}) collective-permute-start(bf16[8,48,768]{2,1,0:T(8,128)(2,1)S(1)} %pad_maximum_fusion.4.rest_8_), channel_id=1, source_target_pairs={{0,16},{16,0},{1,17},{17,1},{2,18},{18,2},{3,19},{19,3},{4,20},{20... | collective-permute-start | bytes 1769480 | tf_op jit(solution)/shard_map/ppermute | solution.py:309
  94.6 14.7 %collective-permute-start.29 = (bf16[8,48,768]{2,1,0:T(8,128)(2,1)S(1)}, bf16[8,48,768]{2,1,0:T(8,128)(2,1)}, u32[]{:S(2)}, u32[]{:S(2)}) collective-permute-start(bf16[8,48,768]{2,1,0:T(8,128)(2,1)S(1)} %pad_maximum_fusion.5.rest_10_), channel_id=1, source_target_pairs={{0,2},{1,3},{2,0},{3,1},{4,6},{5,7},{6,4},{7,5},{8,10},{9,11},{10,... | collective-permute-start | bytes 1769480 | tf_op jit(solution)/shard_map/ppermute | solution.py:305
  96.1 13.4 %collective-permute-start.21 = (bf16[8,48,768]{2,1,0:T(8,128)(2,1)}, bf16[8,48,768]{2,1,0:T(8,128)(2,1)S(1)}, u32[]{:S(2)}, u32[]{:S(2)}) collective-permute-start(bf16[8,48,768]{2,1,0:T(8,128)(2,1)} %collective-permute-done.17.rest_1_), channel_id=1, source_target_pairs={{0,1},{1,0},{2,3},{3,2},{4,5},{5,4},{6,7},{7,6},{8,9},{9,8},{10,11... | collective-permute-start | bytes 1769480 | tf_op jit(solution)/shard_map/ppermute | solution.py:305
  96.6 27.8 %collective-permute-start.23 = (bf16[8,48,768]{2,1,0:T(8,128)(2,1)}, bf16[8,48,768]{2,1,0:T(8,128)(2,1)S(1)}, u32[]{:S(2)}, u32[]{:S(2)}) collective-permute-start(bf16[8,48,768]{2,1,0:T(8,128)(2,1)} %collective-permute-done.19.rest_3_), channel_id=1, source_target_pairs={{0,1},{1,0},{2,3},{3,2},{4,5},{5,4},{6,7},{7,6},{8,9},{9,8},{10,11... | collective-permute-start | bytes 1769480 | tf_op jit(solution)/shard_map/ppermute | solution.py:305
  104.9 34.4 %collective-permute-start.30 = (bf16[8,48,768]{2,1,0:T(8,128)(2,1)S(1)}, bf16[8,48,768]{2,1,0:T(8,128)(2,1)S(1)}, u32[]{:S(2)}, u32[]{:S(2)}) collective-permute-start(bf16[8,48,768]{2,1,0:T(8,128)(2,1)S(1)} %pad_maximum_fusion.4.rest_8_), channel_id=1, source_target_pairs={{0,1},{1,0},{2,3},{3,2},{4,5},{5,4},{6,7},{7,6},{8,9},{9,8},{10,11... | collective-permute-start | bytes 1769480 | tf_op jit(solution)/shard_map/ppermute | solution.py:305
  109.1 30.3 %collective-permute-start.32 = (bf16[8,48,768]{2,1,0:T(8,128)(2,1)S(1)}, bf16[8,48,768]{2,1,0:T(8,128)(2,1)S(1)}, u32[]{:S(2)}, u32[]{:S(2)}) collective-permute-start(bf16[8,48,768]{2,1,0:T(8,128)(2,1)S(1)} %pad_maximum_fusion.5.rest_10_), channel_id=1, source_target_pairs={{0,1},{1,0},{2,3},{3,2},{4,5},{5,4},{6,7},{7,6},{8,9},{9,8},{10,11... | collective-permute-start | bytes 1769480 | tf_op jit(solution)/shard_map/ppermute | solution.py:305
  109.3 30.0 %collective-permute-start.31 = (bf16[8,48,768]{2,1,0:T(8,128)(2,1)}, bf16[8,48,768]{2,1,0:T(8,128)(2,1)S(1)}, u32[]{:S(2)}, u32[]{:S(2)}) collective-permute-start(bf16[8,48,768]{2,1,0:T(8,128)(2,1)} %collective-permute-done.27.rest_9_), channel_id=1, source_target_pairs={{0,1},{1,0},{2,3},{3,2},{4,5},{5,4},{6,7},{7,6},{8,9},{9,8},{10,11... | collective-permute-start | bytes 1769480 | tf_op jit(solution)/shard_map/ppermute | solution.py:305
  109.6 29.8 %collective-permute-start.33 = (bf16[8,48,768]{2,1,0:T(8,128)(2,1)}, bf16[8,48,768]{2,1,0:T(8,128)(2,1)S(1)}, u32[]{:S(2)}, u32[]{:S(2)}) collective-permute-start(bf16[8,48,768]{2,1,0:T(8,128)(2,1)} %collective-permute-done.29.rest_11_), channel_id=1, source_target_pairs={{0,1},{1,0},{2,3},{3,2},{4,5},{5,4},{6,7},{7,6},{8,9},{9,8},{10,11... | collective-permute-start | bytes 1769480 | tf_op jit(solution)/shard_map/ppermute | solution.py:305
  139.0 79.9 %collective-permute-start.55 = (bf16[4,8,48,768]{3,2,1,0:T(8,128)(2,1)}, bf16[4,8,48,768]{3,2,1,0:T(8,128)(2,1)S(1)}, u32[]{:S(2)}, u32[]{:S(2)}) collective-permute-start(bf16[4,8,48,768]{3,2,1,0:T(8,128)(2,1)} %get-tuple-element.60), channel_id=1, source_target_pairs={{0,1},{1,0},{2,3},{3,2},{4,5},{5,4},{6,7},{7,6},{8,9},{9,8},{10,11... | collective-permute-start | bytes 7077896 | tf_op jit(solution)/shard_map/ppermute | solution.py:305
  165.0 66.2 %collective-permute-start.47 = (bf16[4,8,48,768]{3,2,1,0:T(8,128)(2,1)}, bf16[4,8,48,768]{3,2,1,0:T(8,128)(2,1)}, u32[]{:S(2)}, u32[]{:S(2)}) collective-permute-start(bf16[4,8,48,768]{3,2,1,0:T(8,128)(2,1)} %get-tuple-element.58), channel_id=1, source_target_pairs={{0,1},{1,0},{2,3},{3,2},{4,5},{5,4},{6,7},{7,6},{8,9},{9,8},{10,11... | collective-permute-start | bytes 7077896 | tf_op jit(solution)/shard_map/ppermute | solution.py:305
  194.7 39.5 %collective-permute-start.39 = (bf16[4,8,48,768]{3,2,1,0:T(8,128)(2,1)}, bf16[4,8,48,768]{3,2,1,0:T(8,128)(2,1)}, u32[]{:S(2)}, u32[]{:S(2)}) collective-permute-start(bf16[4,8,48,768]{3,2,1,0:T(8,128)(2,1)} %get-tuple-element.56), channel_id=1, source_target_pairs={{0,1},{1,0},{2,3},{3,2},{4,5},{5,4},{6,7},{7,6},{8,9},{9,8},{10,11... | collective-permute-start | bytes 7077896 | tf_op jit(solution)/shard_map/ppermute | solution.py:305
  224.4 16.1 %collective-permute-start.56 = (bf16[8,48,768]{2,1,0:T(8,128)(2,1)}, bf16[8,48,768]{2,1,0:T(8,128)(2,1)}, u32[]{:S(2)}, u32[]{:S(2)}) collective-permute-start(bf16[8,48,768]{2,1,0:T(8,128)(2,1)} %get-tuple-element.64), channel_id=1, source_target_pairs={{0,16},{16,0},{1,17},{17,1},{2,18},{18,2},{3,19},{19,3},{4,20},{20... | collective-permute-start | bytes 1769480 | tf_op jit(solution)/shard_map/ppermute | solution.py:309
  229.7 16.5 %collective-permute-start.58 = (bf16[8,48,768]{2,1,0:T(8,128)(2,1)}, bf16[8,48,768]{2,1,0:T(8,128)(2,1)S(1)}, u32[]{:S(2)}, u32[]{:S(2)}) collective-permute-start(bf16[8,48,768]{2,1,0:T(8,128)(2,1)} %get-tuple-element.62), channel_id=1, source_target_pairs={{0,2},{1,3},{2,0},{3,1},{4,6},{5,7},{6,4},{7,5},{8,10},{9,11},{10,... | collective-permute-start | bytes 1769480 | tf_op jit(solution)/shard_map/ppermute | solution.py:305
  233.5 19.5 %collective-permute-start.48 = (bf16[8,48,768]{2,1,0:T(8,128)(2,1)S(1)}, bf16[8,48,768]{2,1,0:T(8,128)(2,1)S(1)}, u32[]{:S(2)}, u32[]{:S(2)}) collective-permute-start(bf16[8,48,768]{2,1,0:T(8,128)(2,1)S(1)} %get-tuple-element.68), channel_id=1, source_target_pairs={{0,16},{16,0},{1,17},{17,1},{2,18},{18,2},{3,19},{19,3},{4,20},{20... | collective-permute-start | bytes 1769480 | tf_op jit(solution)/shard_map/ppermute | solution.py:309
  233.7 25.1 %collective-permute-start.50 = (bf16[8,48,768]{2,1,0:T(8,128)(2,1)S(1)}, bf16[8,48,768]{2,1,0:T(8,128)(2,1)S(1)}, u32[]{:S(2)}, u32[]{:S(2)}) collective-permute-start(bf16[8,48,768]{2,1,0:T(8,128)(2,1)S(1)} %get-tuple-element.66), channel_id=1, source_target_pairs={{0,2},{1,3},{2,0},{3,1},{4,6},{5,7},{6,4},{7,5},{8,10},{9,11},{10,... | collective-permute-start | bytes 1769480 | tf_op jit(solution)/shard_map/ppermute | solution.py:305
  236.5 29.2 %collective-permute-start.40 = (bf16[8,48,768]{2,1,0:T(8,128)(2,1)S(1)}, bf16[8,48,768]{2,1,0:T(8,128)(2,1)S(1)}, u32[]{:S(2)}, u32[]{:S(2)}) collective-permute-start(bf16[8,48,768]{2,1,0:T(8,128)(2,1)S(1)} %get-tuple-element.72), channel_id=1, source_target_pairs={{0,16},{16,0},{1,17},{17,1},{2,18},{18,2},{3,19},{19,3},{4,20},{20... | collective-permute-start | bytes 1769480 | tf_op jit(solution)/shard_map/ppermute | solution.py:309
  240.5 30.9 %collective-permute-start.42 = (bf16[8,48,768]{2,1,0:T(8,128)(2,1)S(1)}, bf16[8,48,768]{2,1,0:T(8,128)(2,1)S(1)}, u32[]{:S(2)}, u32[]{:S(2)}) collective-permute-start(bf16[8,48,768]{2,1,0:T(8,128)(2,1)S(1)} %get-tuple-element.70), channel_id=1, source_target_pairs={{0,2},{1,3},{2,0},{3,1},{4,6},{5,7},{6,4},{7,5},{8,10},{9,11},{10,... | collective-permute-start | bytes 1769480 | tf_op jit(solution)/shard_map/ppermute | solution.py:305
  246.1 31.6 %collective-permute-start.57 = (bf16[4,48,768]{2,1,0:T(8,128)(2,1)S(1)}, bf16[4,48,768]{2,1,0:T(8,128)(2,1)S(1)}, u32[]{:S(2)}, u32[]{:S(2)}) collective-permute-start(bf16[4,48,768]{2,1,0:T(8,128)(2,1)S(1)} %get-tuple-element.74), channel_id=1, source_target_pairs={{0,2},{1,3},{2,0},{3,1},{4,6},{5,7},{6,4},{7,5},{8,10},{9,11},{10,... | collective-permute-start | bytes 884744 | tf_op jit(solution)/shard_map/ppermute | solution.py:305
  253.0 24.9 %collective-permute-start.59 = (bf16[4,48,768]{2,1,0:T(8,128)(2,1)S(1)}, bf16[4,48,768]{2,1,0:T(8,128)(2,1)S(1)}, u32[]{:S(2)}, u32[]{:S(2)}) collective-permute-start(bf16[4,48,768]{2,1,0:T(8,128)(2,1)S(1)} %get-tuple-element.76), channel_id=1, source_target_pairs={{0,16},{16,0},{1,17},{17,1},{2,18},{18,2},{3,19},{19,3},{4,20},{20... | collective-permute-start | bytes 884744 | tf_op jit(solution)/shard_map/ppermute | solution.py:309
  258.8 23.1 %collective-permute-start.49 = (bf16[4,48,768]{2,1,0:T(8,128)(2,1)S(1)}, bf16[4,48,768]{2,1,0:T(8,128)(2,1)S(1)}, u32[]{:S(2)}, u32[]{:S(2)}) collective-permute-start(bf16[4,48,768]{2,1,0:T(8,128)(2,1)S(1)} %get-tuple-element.78), channel_id=1, source_target_pairs={{0,2},{1,3},{2,0},{3,1},{4,6},{5,7},{6,4},{7,5},{8,10},{9,11},{10,... | collective-permute-start | bytes 884744 | tf_op jit(solution)/shard_map/ppermute | solution.py:305
  265.7 16.3 %collective-permute-start.51 = (bf16[4,48,768]{2,1,0:T(8,128)(2,1)S(1)}, bf16[4,48,768]{2,1,0:T(8,128)(2,1)S(1)}, u32[]{:S(2)}, u32[]{:S(2)}) collective-permute-start(bf16[4,48,768]{2,1,0:T(8,128)(2,1)S(1)} %get-tuple-element.80), channel_id=1, source_target_pairs={{0,16},{16,0},{1,17},{17,1},{2,18},{18,2},{3,19},{19,3},{4,20},{20... | collective-permute-start | bytes 884744 | tf_op jit(solution)/shard_map/ppermute | solution.py:309
  271.4 13.6 %collective-permute-start.41 = (bf16[4,48,768]{2,1,0:T(8,128)(2,1)S(1)}, bf16[4,48,768]{2,1,0:T(8,128)(2,1)S(1)}, u32[]{:S(2)}, u32[]{:S(2)}) collective-permute-start(bf16[4,48,768]{2,1,0:T(8,128)(2,1)S(1)} %get-tuple-element.82), channel_id=1, source_target_pairs={{0,2},{1,3},{2,0},{3,1},{4,6},{5,7},{6,4},{7,5},{8,10},{9,11},{10,... | collective-permute-start | bytes 884744 | tf_op jit(solution)/shard_map/ppermute | solution.py:305
  278.1 12.2 %collective-permute-start.60 = (bf16[2,2,48,768]{3,2,0,1:T(8,128)(2,1)S(1)}, bf16[2,2,48,768]{3,2,0,1:T(8,128)(2,1)S(1)}, u32[]{:S(2)}, u32[]{:S(2)}) collective-permute-start(bf16[2,2,48,768]{3,2,0,1:T(8,128)(2,1)S(1)} %copy.51), channel_id=1, source_target_pairs={{0,4},{1,5},{2,6},{3,7},{4,0},{5,1},{6,2},{7,3},{8,12},{9,13},{10,... | collective-permute-start | bytes 884744 | tf_op jit(solution)/shard_map/ppermute | solution.py:305
  282.1 12.3 %collective-permute-start.52 = (bf16[2,2,48,768]{3,2,0,1:T(8,128)(2,1)S(1)}, bf16[2,2,48,768]{3,2,0,1:T(8,128)(2,1)S(1)}, u32[]{:S(2)}, u32[]{:S(2)}) collective-permute-start(bf16[2,2,48,768]{3,2,0,1:T(8,128)(2,1)S(1)} %copy.49), channel_id=1, source_target_pairs={{0,4},{1,5},{2,6},{3,7},{4,0},{5,1},{6,2},{7,3},{8,12},{9,13},{10,... | collective-permute-start | bytes 884744 | tf_op jit(solution)/shard_map/ppermute | solution.py:305
  285.2 14.7 %collective-permute-start.44 = (bf16[2,2,48,768]{3,2,1,0:T(8,128)(2,1)S(1)}, bf16[2,2,48,768]{3,2,1,0:T(8,128)(2,1)S(1)}, u32[]{:S(2)}, u32[]{:S(2)}) collective-permute-start(bf16[2,2,48,768]{3,2,1,0:T(8,128)(2,1)S(1)} %pad_maximum_fusion.15), channel_id=1, source_target_pairs={{0,4},{1,5},{2,6},{3,7},{4,0},{5,1},{6,2},{7,3},{8,12},{9,13},{10,... | collective-permute-start | bytes 884744 | tf_op jit(solution)/shard_map/ppermute | solution.py:305
  290.3 12.5 %collective-permute-start.61 = (bf16[2,48,768]{2,1,0:T(8,128)(2,1)S(1)}, bf16[2,48,768]{2,1,0:T(8,128)(2,1)S(1)}, u32[]{:S(2)}, u32[]{:S(2)}) collective-permute-start(bf16[2,48,768]{2,1,0:T(8,128)(2,1)S(1)} %fusion.38), channel_id=1, source_target_pairs={{0,8},{1,9},{2,10},{3,11},{4,12},{5,13},{6,14},{7,15},{8,0},{9,1},... | collective-permute-start | bytes 442376 | tf_op jit(solution)/shard_map/ppermute | solution.py:305
  294.4 15.0 %collective-permute-start.53 = (bf16[2,48,768]{2,1,0:T(8,128)(2,1)S(1)}, bf16[2,48,768]{2,1,0:T(8,128)(2,1)S(1)}, u32[]{:S(2)}, u32[]{:S(2)}) collective-permute-start(bf16[2,48,768]{2,1,0:T(8,128)(2,1)S(1)} %fusion.32), channel_id=1, source_target_pairs={{0,8},{1,9},{2,10},{3,11},{4,12},{5,13},{6,14},{7,15},{8,0},{9,1},... | collective-permute-start | bytes 442376 | tf_op jit(solution)/shard_map/ppermute | solution.py:305
  302.9 11.9 %collective-permute-start.62 = (bf16[2,48,768]{2,1,0:T(8,128)(2,1)S(1)}, bf16[2,48,768]{2,1,0:T(8,128)(2,1)S(1)}, u32[]{:S(2)}, u32[]{:S(2)}) collective-permute-start(bf16[2,48,768]{2,1,0:T(8,128)(2,1)S(1)} %fusion.18), channel_id=1, source_target_pairs={{0,16},{16,0},{1,17},{17,1},{2,18},{18,2},{3,19},{19,3},{4,20},{20... | collective-permute-start | bytes 442376 | tf_op jit(solution)/shard_map/ppermute | solution.py:309
  (48 other events, 447.7 us)

commit v2 on v0

--- a/solution.py
+++ b/solution.py
@@ -1,6 +1,10 @@
+import functools
+
 import jax
 import jax.numpy as jnp
 from jax import lax
+from jax.experimental import pallas as pl
+from jax.experimental.pallas import tpu as pltpu
 from jax.sharding import PartitionSpec as P
 
 HEADS = 12
@@ -290,6 +294,780 @@
     )
 
 
+BIT_Z1, BIT_Z0, BIT_Y, BIT_C = 8, 4, 2, 1
+PIECE = 48
+WIDE = 768
+SCALE_ON = 1.0 / 0.9
+VMEM_BYTES = 56 * 1024 * 1024
+f32 = jnp.float32
+bf16 = jnp.bfloat16
+
+
+def hop(array, bit):
+    return lax.ppermute(array, "fsdp", [(i, i ^ bit) for i in range(16)])
+
+
+def swap(array):
+    return lax.ppermute(array, "dp", [(0, 1), (1, 0)])
+
+
+def join(*arrays):
+    return jnp.concatenate(arrays, axis=0)
+
+
+def tie(array, *before):
+    return lax.optimization_barrier((array,) + before)[0]
+
+
+def to_other_core(own):
+    return own + tuple(hop(part, BIT_C) for part in own)
+
+
+def plus(left, right):
+    return (left.astype(f32) + right.astype(f32)).astype(bf16)
+
+
+def core_sums(own, came):
+    return tuple(plus(own[a], came[a]) for a in range(4))
+
+
+def first_hops(parts):
+    return swap(parts[1]), hop(parts[3], BIT_Y)
+
+
+def first_sums(parts, got):
+    return (
+        plus(parts[0][:4], got[0][:4]),
+        plus(parts[0][4:], got[0][4:]),
+        plus(parts[2][:4], got[1][:4]),
+        plus(parts[2][4:], got[1][4:]),
+    )
+
+
+def second_hops(parts):
+    return hop(parts[1], BIT_Y), swap(parts[3])
+
+
+def second_sums(parts, got):
+    return tuple(
+        jnp.stack([plus(parts[0][half], got[0][half]), plus(parts[2][half], got[1][half])])
+        for half in (slice(0, 2), slice(2, 4))
+    )
+
+
+def third_hops(parts):
+    return (hop(parts[1], BIT_Z0),)
+
+
+def third_sums(parts, got):
+    return plus(parts[0][:, 0], got[0][:, 0]), plus(parts[0][:, 1], got[0][:, 1])
+
+
+def fourth_hops(parts):
+    return (hop(parts[1], BIT_Z1),)
+
+
+def fourth_sums(parts, got):
+    return plus(parts[0], got[0])
+
+
+def place(mine, other, x, half, line):
+    return jnp.where(x == half, mine[line], other[line]).astype(f32)
+
+
+def product(left, right, dims):
+    return lax.dot_general(left, right, (dims, ((), ())), preferred_element_type=f32)
+
+
+NN = ((1,), (0,))
+NT = ((1,), (1,))
+TN = ((0,), (0,))
+
+
+def slot(line, xr, yr):
+    return (xr, yr) if line == 0 else (2 + yr, xr)
+
+
+def load_chunk(store, refs, i, line, xr):
+    for m in range(16):
+        c, yr, z0r, z1r = m & 1, (m >> 1) & 1, (m >> 2) & 1, (m >> 3) & 1
+        array, part = slot(line, xr, yr) if isinstance(xr, int) else (2 + yr, xr)
+        row = pl.multiple_of((i ^ m) * PIECE, 16)
+        store[pl.ds(row, PIECE), :] = refs[4 * c + array][part * 4 + z0r * 2 + z1r]
+
+
+def save_chunk(value, outs, i, line, xr):
+    for m in range(16):
+        c, yr, z0r, z1r = m & 1, (m >> 1) & 1, (m >> 2) & 1, (m >> 3) & 1
+        array, part = slot(line, xr, yr) if isinstance(xr, int) else (2 + yr, xr)
+        row = pl.multiple_of((i ^ m) * PIECE, 16)
+        outs[c][array, part * 4 + z0r * 2 + z1r] = value[pl.ds(row, PIECE), :]
+
+
+def row_facts(info, r):
+    first = info[2 + 3 * r]
+    second = first + info[3 + 3 * r]
+    third = second + info[4 + 3 * r]
+
+    def segment(shape, axis):
+        t = lax.broadcasted_iota(jnp.int32, shape, axis)
+        return (t >= first).astype(jnp.int32) + (t >= second).astype(jnp.int32) + (t >= third).astype(jnp.int32)
+
+    column = segment((256, 1), 0)
+
+    def scale(branch):
+        keeps = [info[8 + 6 * r + 2 * j + branch].astype(f32) * SCALE_ON for j in range(3)]
+        return jnp.where(
+            column == 0, keeps[0], jnp.where(column == 1, keeps[1], jnp.where(column == 2, keeps[2], 0.0))
+        )
+
+    inside = jnp.where(column < 3, 1.0, 0.0).astype(f32)
+    return column, segment((1, 256), 1), scale, inside
+
+
+def unit_of(values):
+    center = values - jnp.mean(values, axis=-1, keepdims=True)
+    spread = jnp.mean(center * center, axis=-1, keepdims=True)
+    root = lax.rsqrt(spread + EPSILON)
+    return center * root, root
+
+
+def unit_back(unit, root, gain, incoming):
+    eg = incoming * gain
+    return root * (
+        eg - jnp.mean(eg, axis=-1, keepdims=True) - unit * jnp.mean(eg * unit, axis=-1, keepdims=True)
+    )
+
+
+def sums(values):
+    return jnp.sum(values, axis=0, keepdims=True)
+
+
+def load_direct(store, own, other, i, spots):
+    for m in range(16):
+        spot = spots[0] * (m >> 3) + spots[1] * (m >> 2 & 1) + spots[2] * (m >> 1 & 1)
+        row = pl.multiple_of((i ^ m) * PIECE, 16)
+        store[pl.ds(row, PIECE), :] = (other if m & 1 else own)[spot, 0:PIECE, :]
+
+
+def prepare_kernel(info, qkv, fc1, fc2, *rest):
+    vectors, (pair, ahead, up, down) = rest[:9], rest[9:]
+    x = info[1]
+    ahead[0, 0:PIECE, :] = qkv[:, 0:WIDE]
+    rows = [jnp.pad(v[...].astype(f32).reshape(1, -1), ((0, 0), (0, 256 - v.shape[0]))) for v in vectors]
+    ahead[0, PIECE : PIECE + 16, 0:256] = jnp.concatenate(rows + [jnp.zeros((7, 256), f32)]).astype(bf16)
+    ahead[0, PIECE : PIECE + 16, 256:WIDE] = jnp.zeros((16, WIDE - 256), bf16)
+    for line in range(2):
+        at = pl.multiple_of(WIDE + WIDE * x + 384 * line, 128)
+        pair[line] = qkv[:, pl.ds(at, 384)]
+        up[line] = fc1[:, pl.ds(pl.multiple_of((2 * x + line) * WIDE, 128), WIDE)]
+        down[line] = fc2[pl.ds(pl.multiple_of((2 * x + line) * PIECE, 16), PIECE), :]
+
+
+def load_qkv(weight, refs, query_own, query_other, i, x):
+    load_direct(weight.at[0], query_own, query_other, i, (2, 4, 1))
+    for line in range(2):
+        for xr in range(2):
+            load_chunk(weight.at[1 + (x ^ xr), :, 384 * line : 384 * line + 384], refs, i, line, xr)
+
+
+def qkv_kernel(info, tok, small, *rest):
+    refs, (query_own, query_other, packed, normed, weight) = rest[:8], rest[8:]
+    i, x = info[0], info[1]
+    load_qkv(weight, refs, query_own, query_other, i, x)
+    for r in range(2):
+        rows = slice(256 * r, 256 * r + 256)
+        unit, _ = unit_of(tok[rows, :].astype(f32))
+        normed[rows, :] = (unit * small[0:1, :] + small[1:2, :]).astype(bf16)
+    for r in range(2):
+        rows = slice(256 * r, 256 * r + 256)
+        low = normed[rows, :]
+        packed[rows, 0:768] = (product(low, weight[0], NN) + small[2:3, :]).astype(bf16)
+        packed[rows, 768:1536] = product(low, weight[1], NN).astype(bf16)
+        packed[rows, 1536:2304] = (product(low, weight[2], NN) + small[3:4, :]).astype(bf16)
+
+
+def attend_kernel(info, packed, cot, attended, grad_two, lse):
+    r = pl.program_id(0)
+    column, across, scale, inside = row_facts(info, r)
+    same = column == across
+    lane = lax.broadcasted_iota(jnp.int32, (256, 128), 1)
+    kept = jnp.zeros((256, 128), f32)
+    for h in range(0, HEADS, 2):
+        pair = []
+        for g in (h, h + 1):
+            query = packed[:, 64 * g : 64 * g + 64] * 0.125
+            scores = product(query, packed[:, 768 + 64 * g : 832 + 64 * g], NT)
+            scores = jnp.where(same, scores, NEGATIVE)
+            top = jnp.max(scores, axis=-1, keepdims=True)
+            raised = jnp.exp(scores - top)
+            total = jnp.sum(raised, axis=-1, keepdims=True)
+            low = (raised / total).astype(bf16)
+            pair.append(product(low, packed[:, 1536 + 64 * g : 1600 + 64 * g], NN).astype(bf16))
+            kept = jnp.where(lane == g, top + jnp.log(total), kept)
+        attended[:, 64 * h : 64 * h + 128] = jnp.concatenate(pair, axis=1)
+    lse[...] = kept
+    grad_two[...] = (cot[...].astype(f32) * inside * scale(1)).astype(bf16)
+
+
+def up_kernel(info, attended, tok, grad_two, small, proj_own, proj_other, *rest):
+    refs, (middle, normed, hidden, active, own, away, proj, weight, grad) = rest[:8], rest[8:]
+    i, x, t = info[0], info[1], pl.program_id(0)
+    block = ((t & 1) ^ x) * 2 + (t >> 1)
+
+    @pl.when(t == 0)
+    def _():
+        load_direct(proj, proj_own, proj_other, i, (1, 2, 4))
+        for r in range(2):
+            rows = slice(256 * r, 256 * r + 256)
+            _, _, scale, _ = row_facts(info, r)
+            branch = product(attended[rows, :], proj[...], NN) + small[4:5, :]
+            after = tok[rows, :].astype(f32) + scale(0) * branch
+            middle[rows, :] = after
+            unit, _ = unit_of(after)
+            normed[rows, :] = (unit * small[5:6, :] + small[6:7, :]).astype(bf16)
+
+    for step in range(4):
+
+        @pl.when(t == step)
+        def _():
+            load_chunk(weight, refs, i, step >> 1, step & 1)
+
+    value = product(normed[...], weight[...], NN) + small[pl.ds(8 + block, 1), :]
+    hidden[0] = value
+    low = (0.5 * value * (1.0 + lax.erf(value * (0.5**0.5)))).astype(bf16)
+    active[0] = low
+    grad[...] = product(low, grad_two[...], TN).astype(bf16)
+    far = block ^ (i >> 2)
+    spot = (far & 1) * 2 + (far >> 1)
+    for line in range(2):
+        for xr in range(2):
+            for near in range(4):
+                c, yr = near & 1, near >> 1
+                array, part = slot(line, xr, yr)
+                row = ((i & 3) ^ near) * 192 + ((xr ^ x) * 2 + line) * PIECE
+                (own, away)[c][array, part * 4 + spot] = grad[pl.ds(pl.multiple_of(row, 16), PIECE), :]
+
+
+def down_kernel(line, info, normed, grad_two, hidden, active, small, *rest):
+    refs1 = [None] * 8
+    refs1[2 * line], refs1[2 * line + 1], refs1[4 + 2 * line], refs1[5 + 2 * line] = rest[:4]
+    refs2, rest = rest[4:12], rest[12:]
+    if line == 0:
+        branch, grad_normed, bias, own, away, weight1, weight2, grad = rest
+    else:
+        branch_in, grad_normed_in, bias_in, middle, cot, result, grad_middle, grad_one, bias = rest[:9]
+        own, away, weight1, weight2, grad, branch, grad_normed = rest[9:]
+    i, x, t = info[0], info[1], pl.program_id(0)
+    block = (t ^ x) * 2 + line
+
+    @pl.when(t == 0)
+    def _():
+        if line == 0:
+            branch[...] = jnp.zeros_like(branch)
+            grad_normed[...] = jnp.zeros_like(grad_normed)
+            bias[...] = jnp.zeros_like(bias)
+            bias[7:8, :] = sums(grad_two[...].astype(f32))
+        else:
+            branch[...] = branch_in[...]
+            grad_normed[...] = grad_normed_in[...]
+            bias[...] = bias_in[...]
+
+    for step in range(2):
+
+        @pl.when(t == step)
+        def _():
+            load_chunk(weight1, refs1, i, line, step)
+
+    far = block ^ (i >> 2)
+    spot = (far & 1) * 2 + (far >> 1)
+    for row_line in range(2):
+        for xr in range(2):
+            for near in range(4):
+                c, yr = near & 1, near >> 1
+                array, part = slot(row_line, xr, yr)
+                row = ((i & 3) ^ near) * 192 + ((xr ^ x) * 2 + row_line) * PIECE
+                weight2[pl.ds(pl.multiple_of(row, 16), PIECE), :] = refs2[4 * c + array][part * 4 + spot]
+
+    branch[...] += product(active[0], weight2[...], NN)
+    value = hidden[0]
+    slope = 0.5 * (1.0 + lax.erf(value * (0.5**0.5))) + value * (
+        jnp.exp(-0.5 * value * value) * 0.3989422804014327
+    )
+    low = (product(grad_two[...], weight2[...], NT) * slope).astype(bf16)
+    bias[pl.ds(8 + block, 1), :] = sums(low.astype(f32))
+    grad_normed[...] += product(low, weight1[...], NT)
+    grad[...] = product(normed[...], low, TN).astype(bf16)
+    for m in range(16):
+        c, yr, z0r, z1r = m & 1, (m >> 1) & 1, (m >> 2) & 1, (m >> 3) & 1
+        array, part = (t, yr) if line == 0 else (yr, t)
+        row = pl.multiple_of((i ^ m) * PIECE, 16)
+        (own, away)[c][array, part * 4 + z0r * 2 + z1r] = grad[pl.ds(row, PIECE), :]
+
+    if line == 1:
+
+        @pl.when(t == 1)
+        def _():
+            for r in range(2):
+                rows = slice(256 * r, 256 * r + 256)
+                _, _, scale, inside = row_facts(info, r)
+                after = middle[rows, :]
+                result[rows, :] = (
+                    (after + scale(1) * (branch[rows, :] + small[7:8, :])) * inside
+                ).astype(bf16)
+                unit, root = unit_of(after)
+                incoming = grad_normed[rows, :]
+                bias[5:6, :] += sums(incoming * unit)
+                bias[6:7, :] += sums(incoming)
+                total = cot[rows, :].astype(f32) * inside + unit_back(unit, root, small[5:6, :], incoming)
+                grad_middle[rows, :] = total
+                low_one = (total * scale(0)).astype(bf16)
+                grad_one[rows, :] = low_one
+                bias[4:5, :] += sums(low_one.astype(f32))
+
+
+def attend_back_kernel(group, info, queries, keys, values, lse, attended, grad_one, normed, *rest):
+    if group == 0:
+        proj_own, proj_other, grad_packed, own, away, weight, proj_rest, grad, total = rest
+    else:
+        weight, proj_rest, grad_packed, own, away, grad = rest
+    i, x, r = info[0], info[1], pl.program_id(0)
+    if group == 0:
+
+        @pl.when(r == 0)
+        def _():
+            load_direct(weight, proj_own, proj_other, i, (1, 2, 4))
+            total[...] = jnp.zeros_like(total)
+
+        total[...] += product(attended[...], grad_one[...], TN)
+
+    column, across, _, _ = row_facts(info, r)
+    same = column == across
+    grad_attended = product(grad_one[...], weight[384 * group : 384 * group + 384, :], NT).astype(bf16)
+    rows = pl.ds(pl.multiple_of(r * 256, 256), 256)
+    for h in range(0, 6, 2):
+        pairs = ([], [], [])
+        for g in (h, h + 1):
+            here = slice(64 * g, 64 * g + 64)
+            query = queries[:, here] * 0.125
+            key = keys[:, here]
+            value = values[:, here]
+            back = grad_attended[:, here]
+            scores = product(query, key, NT)
+            head = 6 * group + g
+            weighting = jnp.where(same, jnp.exp(scores - lse[:, head : head + 1]), 0.0)
+            grad_weighting = product(back, value, NT)
+            pairs[2].append(product(weighting.astype(bf16), back, TN))
+            inner = jnp.sum(grad_weighting * weighting, axis=-1, keepdims=True)
+            low = (weighting * (grad_weighting - inner)).astype(bf16)
+            pairs[0].append(product(low, key, NN) * 0.125)
+            pairs[1].append(product(low, query, TN))
+        for k in range(3):
+            grad_packed[rows, 384 * k + 64 * h : 384 * k + 64 * h + 128] = jnp.concatenate(
+                pairs[k], axis=1
+            ).astype(bf16)
+
+    @pl.when(r == 1)
+    def _():
+        low = normed[...]
+        grad[1, 0] = product(low, grad_packed[:, 0:384], TN).astype(bf16)
+        grad[0, 0] = product(low, grad_packed[:, 384:768], TN).astype(bf16)
+        grad[0, 1] = product(low, grad_packed[:, 768:1152], TN).astype(bf16)
+        if group == 0:
+            grad[1, 1] = total[:, 0:384].astype(bf16)
+            proj_rest[...] = total[:, 384:768].astype(bf16)
+        else:
+            grad[1, 1] = proj_rest[...]
+        for line in range(2):
+            for xr in range(2):
+                save_chunk(grad.at[line, x ^ xr], (own, away), i, line, xr)
+
+
+def tokens_back_kernel(r, info, tok, back0, back1, grad_middle, bias_in, small, *rest):
+    refs, (query_own, query_other), (tokens_grad, bias, weight) = rest[:8], rest[8:10], rest[-3:]
+    i, x = info[0], info[1]
+    load_qkv(weight, refs, query_own, query_other, i, x)
+    bias[...] = bias_in[...]
+    for part, back in ((0, back0), (1, back1)):
+        columns = slice(384 * part, 384 * part + 384)
+        bias[2:3, columns] += sums(back[:, 0:384].astype(f32))
+        bias[3:4, columns] += sums(back[:, 768:1152].astype(f32))
+    incoming = jnp.zeros((256, WIDE), f32)
+    for k in range(3):
+        here = slice(384 * k, 384 * k + 384)
+        joined = jnp.concatenate([back0[:, here], back1[:, here]], axis=1)
+        incoming += product(joined, weight[k], NT)
+    unit, root = unit_of(tok[...].astype(f32))
+    bias[0:1, :] += sums(incoming * unit)
+    bias[1:2, :] += sums(incoming)
+    tokens_grad[...] = grad_middle[...] + unit_back(unit, root, small[0:1, :], incoming)
+
+
+def results_kernel(info, mine0, other0, mine1, other1, bias, qkv, proj, *vectors):
+    i, x = info[0], info[1]
+    for group, mine, other in ((0, mine0, other0), (1, mine1, other1)):
+        for line, half, column in ((1, 0, 0), (0, 0, 768), (0, 1, 1536), (1, 1, None)):
+            a, b = mine[line].astype(f32), other[line].astype(f32)
+            value = jnp.where(x == half, a, b)
+            if column is None:
+                proj[:, 384 * group : 384 * group + 384] = value
+            else:
+                qkv[:, column + 384 * group : column + 384 * group + 384] = value
+
+    def cut(rows, start, width):
+        feature = lax.broadcasted_iota(jnp.int32, (WIDE, width), 0)
+        lane = lax.broadcasted_iota(jnp.int32, (WIDE, width), 1)
+        chosen = (feature == lane + start).astype(f32)
+        return lax.dot_general(
+            rows, chosen, (NN, ((), ())), precision=lax.Precision.HIGHEST, preferred_element_type=f32
+        )
+
+    narrow = cut(bias[0:8, :], i * 48, 128)
+    for k in range(8):
+        vectors[k][...] = narrow[k, 0:48]
+    wide = cut(bias[8:16, :], (i & 3) * 192, 256)
+    chosen = lax.broadcasted_iota(jnp.int32, (8, 256), 0) == (i >> 2)
+    vectors[8][...] = jnp.sum(jnp.where(chosen, wide, 0.0), axis=0)[0:192]
+
+
+def whole(shape):
+    return pl.BlockSpec(shape, lambda *_: (0,) * len(shape))
+
+
+def rowwise(width):
+    return pl.BlockSpec((256, width), lambda r, info: (r, 0))
+
+
+def steps(shape):
+    return pl.BlockSpec((1,) + shape, lambda t, info: (t, 0, 0))
+
+
+def run_kernel(kernel, grid, info, operands, outs, scratch, microseconds, alias=None):
+    return pl.pallas_call(
+        kernel,
+        grid_spec=pltpu.PrefetchScalarGridSpec(
+            num_scalar_prefetch=1,
+            grid=(grid,),
+            in_specs=[spec or whole(array.shape) for spec, array in operands],
+            out_specs=[spec or whole(shape) for spec, shape, _ in outs],
+            scratch_shapes=[pltpu.VMEM(shape, dtype) for shape, dtype in scratch],
+        ),
+        out_shape=[jax.ShapeDtypeStruct(shape, dtype) for _, shape, dtype in outs],
+        input_output_aliases=alias or {},
+        compiler_params=pltpu.CompilerParams(
+            dimension_semantics=("arbitrary",), vmem_limit_bytes=VMEM_BYTES
+        ),
+        cost_estimate=pl.CostEstimate(
+            flops=int(microseconds * 1.15e9), bytes_accessed=1 << 20, transcendentals=0
+        ),
+    )(info, *[array for _, array in operands])
+
+
+def fast_device(
+    tokens,
+    lengths,
+    keep_mask,
+    cotangent,
+    ln1_gain,
+    ln1_bias,
+    qkv_weight,
+    q_bias,
+    v_bias,
+    proj_weight,
+    proj_bias,
+    ln2_gain,
+    ln2_bias,
+    fc1_weight,
+    fc1_bias,
+    fc2_weight,
+    fc2_bias,
+):
+    count = tokens.shape[0] * tokens.shape[1]
+    i = lax.axis_index("fsdp")
+    x = lax.axis_index("dp")
+    info = jnp.concatenate(
+        [jnp.stack([i, x]).astype(jnp.int32), lengths.reshape(-1), keep_mask.reshape(-1)]
+    )
+    tok = tokens.reshape(count, WIDE)
+    cot = cotangent.reshape(count, WIDE)
+
+    def full(*arrays):
+        return [(None, array) for array in arrays]
+
+    vectors = (ln1_gain, ln1_bias, q_bias, v_bias, proj_bias, ln2_gain, ln2_bias, fc2_bias, fc1_bias)
+    pair, ahead, up, down = run_kernel(
+        prepare_kernel,
+        1,
+        info,
+        full(qkv_weight, fc1_weight, fc2_weight, *vectors),
+        [
+            (None, (2, PIECE, 384), bf16),
+            (None, (1, 64, WIDE), bf16),
+            (None, (2, PIECE, WIDE), bf16),
+            (None, (2, PIECE, WIDE), bf16),
+        ],
+        [],
+        2,
+    )
+
+    far = hop(pair, BIT_Z1)
+    ahead = join(ahead, hop(ahead, BIT_Y))
+    pair = jnp.stack([pair, far], axis=1)
+    far = hop(pair, BIT_Z0)
+    ahead_far = hop(ahead, BIT_Z1)
+    ahead = join(ahead, ahead_far)
+    line0, line1 = join(pair[0], far[0]), join(pair[1], far[1])
+    wide0 = join(line0, hop(line0, BIT_Y))
+    wide1 = join(line1, swap(line1))
+    line0, line1, up = lax.optimization_barrier((line0, line1, up))
+    got0, got1 = hop(line0, BIT_Y), swap(line1)
+    up_far = hop(up, BIT_Z1)
+    got0, got1, up_far = lax.optimization_barrier((got0, got1, up_far))
+    wide0, wide1 = join(line0, got0), join(line1, got1)
+    got0, got1, ahead_far = swap(wide0), hop(wide1, BIT_Y), hop(ahead, BIT_Z0)
+    up = jnp.stack([up, up_far], axis=1)
+    up_far = hop(up, BIT_Z0)
+    down = tie(join(down, proj_weight[None]), got0, got1)
+    ahead = join(ahead, ahead_far)
+    got0, got1, up_far = lax.optimization_barrier((got0, got1, up_far))
+    first = to_other_core((wide0, got0, wide1, got1))
+    ahead_other = hop(ahead, BIT_C)
+
+    up_line0, up_line1 = join(up[0], up_far[0]), join(up[1], up_far[1])
+    up_got0, up_got1 = hop(up_line0, BIT_Y), swap(up_line1)
+    down_far = hop(down, BIT_Z1)
+
+    vectors = jnp.concatenate([ahead[:, PIECE : PIECE + 9, :192], ahead_other[:, PIECE : PIECE + 9, :192]])
+    origin = jnp.array([(p >> 1 & 1) * 8 + (p >> 2 & 1) * 4 + (p & 1) * 2 + (p >> 3) for p in range(16)])
+    turned = jnp.arange(16)[:, None] == (origin ^ i)[None, :]
+    vectors = jnp.einsum("mp,pkl->kml", turned.astype(bf16), vectors, preferred_element_type=f32)
+    small = jnp.concatenate(
+        [vectors[:8, :, :48].reshape(8, WIDE), vectors[8].reshape(4, WIDE), jnp.zeros((4, WIDE), f32)]
+    )
+
+    packed, normed_one = run_kernel(
+        qkv_kernel,
+        1,
+        info,
+        full(tok, small, *first, ahead, ahead_other),
+        [(None, (count, 3 * WIDE), bf16), (None, (count, WIDE), bf16)],
+        [((3, WIDE, WIDE), bf16)],
+        7,
+    )
+
+    up_got0, up_got1, down_far, _ = lax.optimization_barrier((up_got0, up_got1, down_far, packed))
+    up_wide0, up_wide1 = join(up_line0, up_got0), join(up_line1, up_got1)
+    up_got0, up_got1 = swap(up_wide0), hop(up_wide1, BIT_Y)
+    down = jnp.stack([down, down_far], axis=1)
+    down_far = hop(down, BIT_Z0)
+
+    attended, grad_two, lse = run_kernel(
+        attend_kernel,
+        2,
+        tie(info, up_wide0, up_wide1, down),
+        [(rowwise(3 * WIDE), packed), (rowwise(WIDE), cot)],
+        [
+            (rowwise(WIDE), (count, WIDE), bf16),
+            (rowwise(WIDE), (count, WIDE), bf16),
+            (rowwise(128), (count, 128), f32),
+        ],
+        [],
+        12,
+    )
+
+    up_got0, up_got1, down_far, _ = lax.optimization_barrier((up_got0, up_got1, down_far, lse))
+    up = to_other_core((up_wide0, up_got0, up_wide1, up_got1))
+    down_line0, down_line1, proj = (join(down[k], down_far[k]) for k in range(3))
+    down_got0, down_got1 = hop(down_line0, BIT_Y), swap(down_line1)
+    proj = join(proj, hop(proj, BIT_Y))
+    proj_other = hop(proj, BIT_C)
+    down_wide0, down_wide1 = join(down_line0, down_got0), join(down_line1, down_got1)
+    down_got0, down_got1 = swap(down_wide0), hop(down_wide1, BIT_Y)
+
+    parts = (4, 8, PIECE, WIDE)
+    middle, normed_two, hidden, active, fc2_own, fc2_away = run_kernel(
+        up_kernel,
+        4,
+        tie(info, down_wide0, down_wide1),
+        full(attended, tok, grad_two, small, proj, proj_other, *up),
+        [
+            (None, (count, WIDE), f32),
+            (None, (count, WIDE), bf16),
+            (steps((count, WIDE)), (4, count, WIDE), f32),
+            (steps((count, WIDE)), (4, count, WIDE), bf16),
+            (None, parts, bf16),
+            (None, parts, bf16),
+        ],
+        [((WIDE, WIDE), bf16)] * 3,
+        16,
+    )
+
+    down_got0, down_got1, _ = lax.optimization_barrier((down_got0, down_got1, normed_two))
+    down = to_other_core((down_wide0, down_got0, down_wide1, down_got1))
+    fc2_came = hop(fc2_away, BIT_C)
+    half = (2, 8, PIECE, WIDE)
+    whole_f32 = (None, (count, WIDE), f32)
+    whole_bf16 = (None, (count, WIDE), bf16)
+
+    def down_back(line, info, more, outs, scratch):
+        block = pl.BlockSpec((1, count, WIDE), lambda t, _: (2 * line + t, 0, 0))
+        return run_kernel(
+            functools.partial(down_kernel, line),
+            2,
+            info,
+            full(normed_two, grad_two)
+            + [(block, hidden), (block, active)]
+            + full(small, *up[2 * line : 2 * line + 2], *up[4 + 2 * line : 6 + 2 * line], *down, *more),
+            outs + [(None, (16, WIDE), f32), (None, half, bf16), (None, half, bf16)],
+            [((WIDE, WIDE), bf16)] * 3 + scratch,
+            13,
+        )
+
+    branch, grad_normed, bias, fc1_own0, fc1_away0 = down_back(0, info, (), [whole_f32] * 2, [])
+    fc2_came, bias = lax.optimization_barrier((fc2_came, bias))
+    two = core_sums(fc2_own, fc2_came)
+    two_got = first_hops(two)
+    one_came0 = hop(fc1_away0, BIT_C)
+    output, grad_middle, grad_one, bias, fc1_own1, fc1_away1 = down_back(
+        1,
+        tie(info, *two),
+        (branch, grad_normed, bias, middle, cot),
+        [whole_bf16, whole_f32, whole_bf16],
+        [((count, WIDE), f32)] * 2,
+    )
+
+    def attend_back(group, info, more, outs, scratch):
+        def columns(k):
+            return pl.BlockSpec((256, 384), lambda r, _, at=2 * k + group: (r, at))
+
+        narrow = (4, 8, PIECE, 384)
+        return run_kernel(
+            functools.partial(attend_back_kernel, group),
+            2,
+            info,
+            [(columns(k), packed) for k in range(3)]
+            + [(rowwise(128), lse), (rowwise(WIDE), attended), (rowwise(WIDE), grad_one)]
+            + full(normed_one, *more),
+            [(None, (count, 1152), bf16), (None, narrow, bf16), (None, narrow, bf16)] + outs,
+            [((2, 2, WIDE, 384), bf16)] + scratch,
+            14,
+        )
+
+    two_got, one_came0, bias = lax.optimization_barrier((two_got, one_came0, bias))
+    two = first_sums(two, two_got)
+    two_got, one_came1 = second_hops(two), hop(fc1_away1, BIT_C)
+    back0, head_own0, head_away0, proj_full, proj_rest = attend_back(
+        0,
+        tie(info, *two),
+        (proj, proj_other),
+        [(None, (WIDE, WIDE), bf16), (None, (WIDE, 384), bf16)],
+        [((WIDE, WIDE), f32)],
+    )
+
+    two_got, one_came1, _ = lax.optimization_barrier((two_got, one_came1, proj_rest))
+    two = second_sums(two, two_got)
+    one = tuple(
+        plus(own[k], came[k])
+        for own, came in ((fc1_own0, one_came0), (fc1_own1, one_came1))
+        for k in range(2)
+    )
+    one_got, two_got, zero_came = first_hops(one), third_hops(two), hop(head_away0, BIT_C)
+    back1, head_own1, head_away1 = attend_back(1, tie(info, *two, *one), (proj_full, proj_rest), [], [])
+
+    two_got, one_got, zero_came, _ = lax.optimization_barrier((two_got, one_got, zero_came, back1))
+    two, one, zero = third_sums(two, two_got), first_sums(one, one_got), core_sums(head_own0, zero_came)
+    last_came = hop(head_away1, BIT_C)
+    two_got, one_got, zero_got = fourth_hops(two), second_hops(one), first_hops(zero)
+
+    def tokens_back(r, info, more, alias):
+        def row(width):
+            return pl.BlockSpec((256, width), lambda _, __: (r, 0))
+
+        return run_kernel(
+            functools.partial(tokens_back_kernel, r),
+            1,
+            info,
+            [(row(WIDE), tok), (row(1152), back0), (row(1152), back1), (row(WIDE), grad_middle)]
+            + full(bias, small, *first, ahead, ahead_other)
+            + more,
+            [(row(WIDE), (count, WIDE), f32), (None, (16, WIDE), f32)],
+            [((3, WIDE, WIDE), bf16)],
+            6,
+            alias,
+        )
+
+    tokens_grad, bias = tokens_back(0, tie(info, *two, *one, *zero), [], {})
+
+    two_got, one_got, zero_got, last_came, bias = lax.optimization_barrier(
+        (two_got, one_got, zero_got, last_came, bias)
+    )
+    last, two, one, zero = (
+        core_sums(head_own1, last_came),
+        fourth_sums(two, two_got),
+        second_sums(one, one_got),
+        first_sums(zero, zero_got),
+    )
+    last_got, one_got, zero_got, two_other = first_hops(last), third_hops(one), second_hops(zero), swap(two)
+    tokens_grad, bias = tokens_back(
+        1, tie(info, *last, two, *one, *zero), [(pl.BlockSpec(memory_space=pl.ANY), tokens_grad)], {17: 0}
+    )
+
+    last_got, one_got, zero_got, two_other, bias = lax.optimization_barrier(
+        (last_got, one_got, zero_got, two_other, bias)
+    )
+    last, one, zero = first_sums(last, last_got), third_sums(one, one_got), second_sums(zero, zero_got)
+    last_got, one_got, zero_got, bias_got = lax.optimization_barrier(
+        (
+            second_hops(last),
+            fourth_hops(one),
+            third_hops(zero),
+            (hop(bias, BIT_C), hop(bias, BIT_Y), hop(bias, BIT_C | BIT_Y)),
+        )
+    )
+    last, one, zero = second_sums(last, last_got), fourth_sums(one, one_got), third_sums(zero, zero_got)
+    bias = (bias + bias_got[0]) + (bias_got[1] + bias_got[2])
+    last_got, one_other, zero_got, bias_got = lax.optimization_barrier(
+        (third_hops(last), swap(one), fourth_hops(zero), hop(bias, BIT_Z0))
+    )
+    last, zero, bias = third_sums(last, last_got), fourth_sums(zero, zero_got), bias + bias_got
+    last_got, zero_other, bias_got = lax.optimization_barrier(
+        (fourth_hops(last), swap(zero), hop(bias, BIT_Z1))
+    )
+    last, bias = fourth_sums(last, last_got), bias + bias_got
+    last_other, bias_got = swap(last), swap(bias)
+    bias = bias + bias_got
+    qkv_grad, proj_grad, *narrow = run_kernel(
+        results_kernel,
+        1,
+        info,
+        full(zero, zero_other, last, last_other, bias),
+        [(None, (PIECE, 3 * WIDE), f32), (None, (PIECE, WIDE), f32)]
+        + [(None, (48,), f32)] * 8
+        + [(None, (192,), f32)],
+        [],
+        3,
+    )
+    fc1_grad = jnp.concatenate([place(one, one_other, x, k >> 1, k & 1) for k in range(4)], axis=1)
+    fc2_grad = jnp.concatenate([place(two, two_other, x, k >> 1, k & 1) for k in range(4)], axis=0)
+    return (
+        output.reshape(tokens.shape),
+        tokens_grad.reshape(tokens.shape),
+        narrow[0],
+        narrow[1],
+        qkv_grad,
+        narrow[2],
+        narrow[3],
+        proj_grad,
+        narrow[4],
+        narrow[5],
+        narrow[6],
+        fc1_grad,
+        narrow[8],
+        fc2_grad,
+        narrow[7],
+    )
+
+
 def solution(mesh):
     in_specs = (
         P(("dp", "fsdp"), None, None),
@@ -327,6 +1105,7 @@
         P("fsdp", None),
         P("fsdp"),
     )
+    fits = mesh.shape["dp"] == 2 and mesh.shape["fsdp"] == 16
     return jax.shard_map(
-        per_device, mesh=mesh, in_specs=in_specs, out_specs=out_specs, check_vma=False
-    )
+        fast_device if fits else per_device, mesh=mesh, in_specs=in_specs, out_specs=out_specs, check_vma=False
+    )

time: 728 us -> 273 us (0.38)
  waiting for transfers between devices: 404 us -> 73.2 us
  blocking collectives: 130 us -> 0 us
  Pallas kernels: 0 us -> 108 us
  matrix products: 87.6 us -> 0.15 us
  starting transfers between devices: 0.99 us -> 68.1 us
  local copies, waits for them, and re-layouts: 41.5 us -> 6.1 us
  other arithmetic: 43.3 us -> 11.5 us
  between operations: 17.3 us -> 2.06 us
    reduce_scatter x4 -> x0, waiting for transfers between devices: 323 us -> none  [the longest x1 114 us: per_device(): lax.psum_scatter(fc2_grad, 'fsdp', scatter_dimension=0, tiled=True)]
    unnamed x2 -> x0, blocking collectives: 124 us -> none
    pallas_call x0 -> x11, Pallas kernels: none -> 108 us  [run_kernel(): pl.pallas_call(kernel, grid_spec=pltpu.PrefetchScalarGridSpec(num_scalar_...]
    dot_general x18 -> x1, matrix products: 87.6 us -> 0.15 us  [fast_device(): jnp.einsum('mp,pkl->kml', turned.astype(bf16), vectors, preferred_element...]
    all_gather x4 -> x0, waiting for transfers between devices: 78.2 us -> none  [the longest x1 45.9 us: per_device(): lax.all_gather(fc2_weight, 'fsdp', axis=0, tiled=True)]
    ppermute x0 -> x75, waiting for transfers between devices: none -> 73.2 us  [the longest x56 67.7 us: hop(): return lax.ppermute(array, 'fsdp', [(i, i ^ bit) for i in range(16)])]
    ppermute x0 -> x75, starting transfers between devices: none -> 68.1 us  [the longest x56 44 us: hop(): return lax.ppermute(array, 'fsdp', [(i, i ^ bit) for i in range(16)])]
    convert_element_type x33 -> x23, other arithmetic: 32.8 us -> 3.01 us  [the longest x21 2.96 us: plus(): return (left.astype(f32) + right.astype(f32)).astype(bf16)]
  transfers between devices with their start and end apart: 9 -> 75, of which waited for: 6 -> 27; matrix products, arithmetic and copies ran while one was open for 17% -> 4% of each run, Pallas kernels for 0% -> 38%
where the time goes in v2:
time: 273 us; the launch traced here: 269 us
  Pallas kernels  108 us (40%)
  waiting for transfers between devices  73.2 us (27%)
  starting transfers between devices  68.1 us (25%)
  other arithmetic  11.5 us (4%)
  local copies, waits for them, and re-layouts  6.1 us (2%)
    pallas_call x11, Pallas kernels, run_kernel(): pl.pallas_call(kernel, grid_spec=pltpu.PrefetchScalarGridSpec(num_scalar_...  108 us
    ppermute x56, waiting for transfers between devices, hop(): return lax.ppermute(array, 'fsdp', [(i, i ^ bit) for i in range(16)])  67.7 us
    ppermute x56, starting transfers between devices, hop(): return lax.ppermute(array, 'fsdp', [(i, i ^ bit) for i in range(16)])  44 us
    ppermute x19, starting transfers between devices, swap(): return lax.ppermute(array, 'dp', [(0, 1), (1, 0)])  24.1 us
    ppermute x19, waiting for transfers between devices, swap(): return lax.ppermute(array, 'dp', [(0, 1), (1, 0)])  5.5 us
  transfers between devices with their start and end apart: 75, of which 27 were waited for; matrix products, arithmetic and copies ran while one was open for 4% of the time, Pallas kernels for 38%

profile of v2, /device:TPU:0, one launch (start us, length us, event | category | flops | bytes accessed | tf_op | source)
XLA Modules:
  0.0 268.9 jit_solution(10487311136578049813)
XLA Ops:
  2.9 2.8 %shard_map.289 = (bf16[2,48,384]{2,1,0:T(8,128)(2,1)}, bf16[1,64,768]{2,1,0:T(8,128)(2,1)}, bf16[2,48,768]{2,1,0:T(8,128)(2,1)}, bf16[2,48,768]{2,1,0:T(8,128)(2,1)}) custom-call(s32[20]{0:T(128)} %pad_add_fusion.info, bf16[48,2304]{1,0:T(8,128)(2,1)} %qkv.1, bf16[48,3072]{1,0:T(8,128)(2,1)} %fc1.1, bf16[192,768]{1,0:T(8,128)(2,1)} %fc2.1, ...), custom_call_target="tpu_custom_call" | custom-call | flops 2300000000 | bytes 1048576 | tf_op jit(solution)/shard_map/pallas_call | solution.py:746
  5.7 3.0 %collective-permute-start.11 = (bf16[1,64,768]{2,1,0:T(8,128)(2,1)}, bf16[1,64,768]{2,1,0:T(8,128)(2,1)S(1)}, u32[]{:S(2)}, u32[]{:S(2)}) collective-permute-start(bf16[1,64,768]{2,1,0:T(8,128)(2,1)} %get-tuple-element.141), channel_id=1, source_target_pairs={{0,2},{1,3},{2,0},{3,1},{4,6},{5,7},{6,4},{7,5},{8,10},{9,11},{10,... | collective-permute-start | bytes 294920 | tf_op jit(solution)/shard_map/ppermute | solution.py:307
  8.7 2.6 collective-permute-start
  13.3 2.1 collective-permute-done
  17.7 3.3 %collective-permute-start.12 = (bf16[2,64,768]{2,1,0:T(8,128)(2,1)S(1)}, bf16[2,64,768]{2,1,0:T(8,128)(2,1)S(1)}, u32[]{:S(2)}, u32[]{:S(2)}) collective-permute-start(bf16[2,64,768]{2,1,0:T(8,128)(2,1)S(1)} %pad_maximum_fusion.18), channel_id=1, source_target_pairs={{0,8},{1,9},{2,10},{3,11},{4,12},{5,13},{6,14},{7,15},{8,0},{9,1},... | collective-permute-start | bytes 589832 | tf_op jit(solution)/shard_map/ppermute | solution.py:307
  23.1 1.5 collective-permute-start.3
  24.6 2.4 collective-permute-start.4
  27.1 6.6 %collective-permute-done.12 = bf16[2,64,768]{2,1,0:T(8,128)(2,1)S(1)} collective-permute-done((bf16[2,64,768]{2,1,0:T(8,128)(2,1)S(1)}, bf16[2,64,768]{2,1,0:T(8,128)(2,1)S(1)}, u32[]{:S(2)}, u32[]{:S(2)}) %collective-permute-start.12) | collective-permute-done | bytes 196640 | tf_op jit(solution)/shard_map/ppermute | solution.py:307
  33.9 1.9 collective-permute-done.4
  36.8 1.5 collective-permute-start.5
  38.2 7.7 %collective-permute-done.13 = bf16[4,64,768]{2,1,0:T(8,128)(2,1)S(1)} collective-permute-done((bf16[4,64,768]{2,1,0:T(8,128)(2,1)S(1)}, bf16[4,64,768]{2,1,0:T(8,128)(2,1)S(1)}, u32[]{:S(2)}, u32[]{:S(2)}) %collective-permute-start.13) | collective-permute-done | bytes 393248 | tf_op jit(solution)/shard_map/ppermute | solution.py:307
  46.6 3.9 %collective-permute-done.7 = bf16[2,2,48,768]{3,2,1,0:T(8,128)(2,1)S(1)} collective-permute-done((bf16[2,2,48,768]{3,2,1,0:T(8,128)(2,1)S(1)}, bf16[2,2,48,768]{3,2,1,0:T(8,128)(2,1)S(1)}, u32[]{:S(2)}, u32[]{:S(2)}) %collective-permute-start.7) | collective-permute-done | bytes 294944 | tf_op jit(solution)/shard_map/ppermute | solution.py:307
  53.0 1.5 collective-permute-start.9
  55.0 6.9 %shard_map.290 = (bf16[512,2304]{1,0:T(8,128)(2,1)}, bf16[512,768]{1,0:T(8,128)(2,1)}) custom-call(s32[20]{0:T(128)} %pad_add_fusion.info, bf16[512,768]{1,0:T(8,128)(2,1)} %bitcast.243, f32[16,768]{1,0:T(8,128)} %maximum_maximum_fusion.small, bf16[8,48,384]{2,1,0:T(8,128)(2,1)} %copy-done.12, bf16[8,48,384]{2,1,0:T(8,128)(2,1)} %collective-permute-done.5.rest_1_, ...), custom_call_target="tpu_custom_call" | custom-call | flops 8049999872 | bytes 1048576 | tf_op jit(solution)/shard_map/pallas_call | solution.py:746
  62.0 2.5 collective-permute-done.10
  66.9 10.4 %shard_map.291 = (bf16[512,768]{1,0:T(8,128)(2,1)}, bf16[512,768]{1,0:T(8,128)(2,1)}, f32[512,128]{1,0:T(8,128)}) custom-call(s32[20]{0:T(128)} %pad_add_fusion.info, bf16[512,2304]{1,0:T(8,128)(2,1)} %get-tuple-element.144.packed.queries.keys.values, bf16[512,768]{1,0:T(8,128)(2,1)} %bitcast.241), custom_call_target="tpu_custom_call" | custom-call | flops 13799999488 | bytes 1048576 | tf_op jit(solution)/shard_map/pallas_call | solution.py:746
  77.4 2.8 %collective-permute-done.20.rest_3_.rest_1_ = bf16[8,48,768]{2,1,0:T(8,128)(2,1)S(1)} collective-permute-done((bf16[8,48,768]{2,1,0:T(8,128)(2,1)S(1)}, bf16[8,48,768]{2,1,0:T(8,128)(2,1)S(1)}, u32[]{:S(2)}, u32[]{:S(2)}) %collective-permute-start.20) | collective-permute-done | bytes 589856 | tf_op jit(solution)/shard_map/ppermute | solution.py:307
  80.5 1.5 collective-permute-start.24
  82.1 1.6 collective-permute-start.23
  84.7 5.4 %collective-permute-done.24 = bf16[4,48,768]{2,1,0:T(8,128)(2,1)S(1)} collective-permute-done((bf16[4,48,768]{2,1,0:T(8,128)(2,1)S(1)}, bf16[4,48,768]{2,1,0:T(8,128)(2,1)S(1)}, u32[]{:S(2)}, u32[]{:S(2)}) %collective-permute-start.24) | collective-permute-done | bytes 294944 | tf_op jit(solution)/shard_map/ppermute | solution.py:307
  90.9 2.8 %collective-permute-done.22 = bf16[4,48,768]{2,1,0:T(8,128)(2,1)S(1)} collective-permute-done((bf16[4,48,768]{2,1,0:T(8,128)(2,1)S(1)}, bf16[4,48,768]{2,1,0:T(8,128)(2,1)S(1)}, u32[]{:S(2)}, u32[]{:S(2)}) %collective-permute-start.22) | collective-permute-done | bytes 294944 | tf_op jit(solution)/shard_map/ppermute | solution.py:307
  96.2 2.5 collective-permute-start.31
  99.8 15.4 %shard_map.292 = (f32[512,768]{1,0:T(8,128)}, bf16[512,768]{1,0:T(8,128)(2,1)}, f32[4,512,768]{2,1,0:T(8,128)}, bf16[4,512,768]{2,1,0:T(8,128)(2,1)}, bf16[4,8,4...) custom-call(s32[20]{0:T(128)} %pad_add_fusion.info, bf16[512,768]{1,0:T(8,128)(2,1)} %get-tuple-element.152.attended, ...), custom_call_target="tpu_custom_call" | custom-call | flops 18400000000 | bytes 1048576 | tf_op jit(solution)/shard_map/pallas_call | solution.py:746
  116.5 4.8 %collective-permute-done.35.rest_10_ = bf16[8,48,768]{2,1,0:T(8,128)(2,1)} collective-permute-done((bf16[8,48,768]{2,1,0:T(8,128)(2,1)S(1)}, bf16[8,48,768]{2,1,0:T(8,128)(2,1)}, u32[]{:S(2)}, u32[]{:S(2)}) %collective-permute-start.35) | collective-permute-done | bytes 589856 | tf_op jit(solution)/shard_map/ppermute | solution.py:307
  123.6 13.0 %shard_map.293 = (f32[512,768]{1,0:T(8,128)}, f32[512,768]{1,0:T(8,128)}, f32[16,768]{1,0:T(8,128)}, bf16[2,8,48,768]{3,2,1,0:T(8,128)(2,1)}, bf16[2,8,48,768]{3,2,1,0:T(8,128)(2,1)}) custom-call(s32[20]{0:T(128)} %pad_add_fusion.info, bf16[512,768]{1,0:T(8,128)(2,1)} %get-tuple-element.158.normed, bf16[512,768]{1,0:T(8,128)(2,1)} %get-tuple-element.153.grad_two, ...), custom_call_target="tpu_custom_call" | custom-call | flops 14949999616 | bytes 1048576 | tf_op jit(solution)/shard_map/pallas_call | solution.py:746
  138.3 17.4 %shard_map.294 = (bf16[512,768]{1,0:T(8,128)(2,1)}, f32[512,768]{1,0:T(8,128)}, bf16[512,768]{1,0:T(8,128)(2,1)}, f32[16,768]{1,0:T(8,128)}, bf16[2,8,48,768]{3,...) custom-call(s32[20]{0:T(128)} %pad_add_fusion.info, bf16[512,768]{1,0:T(8,128)(2,1)} %get-tuple-element.158.normed, ...), custom_call_target="tpu_custom_call" | custom-call | flops 14949999616 | bytes 1048576 | tf_op jit(solution)/shard_map/pallas_call | solution.py:746
  156.0 1.8 collective-permute-start.41
  160.0 13.5 %shard_map.295 = (bf16[512,1152]{1,0:T(8,128)(2,1)}, bf16[4,8,48,384]{3,2,1,0:T(8,128)(2,1)}, bf16[4,8,48,384]{3,2,1,0:T(8,128)(2,1)}, bf16[768,768]{1,0:T(8,128)(2,1)}, bf16[768,384]{1,0:T(8,128)(2,1)}) custom-call(s32[20]{0:T(128)} %pad_add_fusion.info, bf16[512,2304]{1,0:T(8,128)(2,1)} %get-tuple-element.144.packed.queries.keys.values, ...), custom_call_target="tpu_custom_call" | custom-call | flops 16099999744 | bytes 1048576 | tf_op jit(solution)/shard_map/pallas_call | solution.py:746
  176.0 1.7 collective-permute-start.43
  177.7 12.8 %shard_map.296 = (bf16[512,1152]{1,0:T(8,128)(2,1)}, bf16[4,8,48,384]{3,2,1,0:T(8,128)(2,1)}, bf16[4,8,48,384]{3,2,1,0:T(8,128)(2,1)}) custom-call(s32[20]{0:T(128)} %pad_add_fusion.info, bf16[512,2304]{1,0:T(8,128)(2,1)} %get-tuple-element.144.packed.queries.keys.values, bf16[512,2304]{1,0:T(8,128)(2,1)} %get-tuple-element.144.packed.queries.keys.values, ...), custom_call_target="tpu_custom_call" | custom-call | flops 16099999744 | bytes 1048576 | tf_op jit(solution)/shard_map/pallas_call | solution.py:746
  190.9 1.6 collective-permute-start.50
  195.9 8.1 %collective-permute-done.47 = bf16[2,48,768]{2,1,0:T(8,128)(2,1)S(1)} collective-permute-done((bf16[2,48,768]{2,1,0:T(8,128)(2,1)S(1)}, bf16[2,48,768]{2,1,0:T(8,128)(2,1)S(1)}, u32[]{:S(2)}, u32[]{:S(2)}) %collective-permute-start.47) | collective-permute-done | bytes 147488 | tf_op jit(solution)/shard_map/ppermute | solution.py:307
  204.7 6.1 %shard_map.297 = (f32[512,768]{1,0:T(8,128)}, f32[16,768]{1,0:T(8,128)}) custom-call(s32[20]{0:T(128)} %pad_add_fusion.info, bf16[512,768]{1,0:T(8,128)(2,1)} %bitcast.245, bf16[512,1152]{1,0:T(8,128)(2,1)} %get-tuple-element.198.back0, bf16[512,1152]{1,0:T(8,128)(2,1)} %get-tuple-element.190.back1, f32[512,768]{1,0:T(8,128)} %get-tuple-element.199.grad_middle, ...), custom_call_target="tpu_custom_call" | custom-call | flops 6899999744 | bytes 1048576 | tf_op jit(solution)/shard_map/pallas_call | solution.py:746
  210.8 2.1 collective-permute-done.48
  213.2 1.7 collective-permute-start.57
  218.0 1.5 collective-permute-done.57
  219.5 2.2 collective-permute-start.58
  221.7 6.1 %shard_map.298 = (f32[512,768]{1,0:T(8,128)}, f32[16,768]{1,0:T(8,128)}) custom-call(s32[20]{0:T(128)} %pad_add_fusion.info, bf16[512,768]{1,0:T(8,128)(2,1)} %bitcast.246, bf16[512,1152]{1,0:T(8,128)(2,1)} %get-tuple-element.198.back0, bf16[512,1152]{1,0:T(8,128)(2,1)} %get-tuple-element.190.back1, ...), custom_call_target="tpu_custom_call", output_to_operand_aliasing={{0}: (17, {})} | custom-call | flops 6899999744 | bytes 1048576 | tf_op jit(solution)/shard_map/pallas_call | solution.py:746
  230.8 1.7 collective-permute-start.61
  234.8 3.2 %collective-permute-done.62 = bf16[2,2,48,384]{3,2,0,1:T(8,128)(2,1)S(1)} collective-permute-done((bf16[2,2,48,384]{3,2,0,1:T(8,128)(2,1)S(1)}, bf16[2,2,48,384]{3,2,0,1:T(8,128)(2,1)S(1)}, u32[]{:S(2)}, u32[]{:S(2)}) %collective-permute-start.62) | collective-permute-done | bytes 147488 | tf_op jit(solution)/shard_map/ppermute | solution.py:307
  238.0 2.8 %collective-permute-done.61 = bf16[2,48,768]{2,1,0:T(8,128)(2,1)S(1)} collective-permute-done((bf16[2,48,768]{2,1,0:T(8,128)(2,1)S(1)}, bf16[2,48,768]{2,1,0:T(8,128)(2,1)S(1)}, u32[]{:S(2)}, u32[]{:S(2)}) %collective-permute-start.61) | collective-permute-done | bytes 147488 | tf_op jit(solution)/shard_map/ppermute | solution.py:307
  242.2 2.1 collective-permute-start.66
  245.5 4.9 %collective-permute-done.68 = bf16[2,48,384]{2,1,0:T(8,128)(2,1)S(1)} collective-permute-done((bf16[2,48,384]{2,1,0:T(8,128)(2,1)S(1)}, bf16[2,48,384]{2,1,0:T(8,128)(2,1)S(1)}, u32[]{:S(2)}, u32[]{:S(2)}) %collective-permute-start.68) | collective-permute-done | bytes 73760 | tf_op jit(solution)/shard_map/ppermute | solution.py:307
  251.6 1.9 collective-permute-start.70
  253.6 1.5 collective-permute-start.71
  255.5 1.8 collective-permute-done.70
  258.7 1.5 collective-permute-start.74
  265.3 3.1 %shard_map.299 = (f32[48,2304]{1,0:T(8,128)}, f32[48,768]{1,0:T(8,128)}, f32[48]{0:T(128)}, f32[48]{0:T(128)}, f32[48]{0:T(128)}, /*index=5*/f32[48]{0:T(128)}, ...) custom-call(s32[20]{0:T(128)} %pad_add_fusion.info, bf16[2,48,384]{2,1,0:T(8,128)(2,1)} %copy-done.14, ...), custom_call_target="tpu_custom_call" | custom-call | flops 3449999872 | bytes 1048576 | tf_op jit(solution)/shard_map/pallas_call | solution.py:746
  (264 shorter events, 54.9 us)
Async XLA Ops:
  5.7 12.0 %collective-permute-start.11 = (bf16[1,64,768]{2,1,0:T(8,128)(2,1)}, bf16[1,64,768]{2,1,0:T(8,128)(2,1)S(1)}, u32[]{:S(2)}, u32[]{:S(2)}) collective-permute-start(bf16[1,64,768]{2,1,0:T(8,128)(2,1)} %get-tuple-element.141), channel_id=1, source_target_pairs={{0,2},{1,3},{2,0},{3,1},{4,6},{5,7},{6,4},{7,5},{8,10},{9,11},{10,... | collective-permute-start | bytes 294920 | tf_op jit(solution)/shard_map/ppermute | solution.py:307
  17.7 16.0 %collective-permute-start.12 = (bf16[2,64,768]{2,1,0:T(8,128)(2,1)S(1)}, bf16[2,64,768]{2,1,0:T(8,128)(2,1)S(1)}, u32[]{:S(2)}, u32[]{:S(2)}) collective-permute-start(bf16[2,64,768]{2,1,0:T(8,128)(2,1)S(1)} %pad_maximum_fusion.18), channel_id=1, source_target_pairs={{0,8},{1,9},{2,10},{3,11},{4,12},{5,13},{6,14},{7,15},{8,0},{9,1},... | collective-permute-start | bytes 589832 | tf_op jit(solution)/shard_map/ppermute | solution.py:307
  22.6 11.3 %collective-permute-start.2 = (bf16[4,48,384]{2,1,0:T(8,128)(2,1)S(1)}, bf16[4,48,384]{2,1,0:T(8,128)(2,1)S(1)}, u32[]{:S(2)}, u32[]{:S(2)}) collective-permute-start(bf16[4,48,384]{2,1,0:T(8,128)(2,1)S(1)} %get-tuple-element.133), channel_id=1, source_target_pairs={{0,2},{1,3},{2,0},{3,1},{4,6},{5,7},{6,4},{7,5},{8,10},{9,11},{10,... | collective-permute-start | bytes 442376 | tf_op jit(solution)/shard_map/ppermute | solution.py:307
  23.1 10.8 %collective-permute-start.3 = (bf16[4,48,384]{2,1,0:T(8,128)(2,1)S(1)}, bf16[4,48,384]{2,1,0:T(8,128)(2,1)S(1)}, u32[]{:S(2)}, u32[]{:S(2)}) collective-permute-start(bf16[4,48,384]{2,1,0:T(8,128)(2,1)S(1)} %get-tuple-element.134), channel_id=1, source_target_pairs={{0,16},{16,0},{1,17},{17,1},{2,18},{18,2},{3,19},{19,3},{4,20},{20... | collective-permute-start | bytes 442376 | tf_op jit(solution)/shard_map/ppermute | solution.py:311
  24.6 11.2 %collective-permute-start.4 = (bf16[2,48,768]{2,1,0:T(8,128)(2,1)S(1)}, bf16[2,48,768]{2,1,0:T(8,128)(2,1)S(1)}, u32[]{:S(2)}, u32[]{:S(2)}) collective-permute-start(bf16[2,48,768]{2,1,0:T(8,128)(2,1)S(1)} %copy-done.10), channel_id=1, source_target_pairs={{0,8},{1,9},{2,10},{3,11},{4,12},{5,13},{6,14},{7,15},{8,0},{9,1},... | collective-permute-start | bytes 442376 | tf_op jit(solution)/shard_map/ppermute | solution.py:307
  33.8 12.1 %collective-permute-start.13 = (bf16[4,64,768]{2,1,0:T(8,128)(2,1)S(1)}, bf16[4,64,768]{2,1,0:T(8,128)(2,1)S(1)}, u32[]{:S(2)}, u32[]{:S(2)}) collective-permute-start(bf16[4,64,768]{2,1,0:T(8,128)(2,1)S(1)} %pad_maximum_fusion.6), channel_id=1, source_target_pairs={{0,4},{1,5},{2,6},{3,7},{4,0},{5,1},{6,2},{7,3},{8,12},{9,13},{10,... | collective-permute-start | bytes 1179656 | tf_op jit(solution)/shard_map/ppermute | solution.py:307
  35.9 14.6 %collective-permute-start.7 = (bf16[2,2,48,768]{3,2,1,0:T(8,128)(2,1)S(1)}, bf16[2,2,48,768]{3,2,1,0:T(8,128)(2,1)S(1)}, u32[]{:S(2)}, u32[]{:S(2)}) collective-permute-start(bf16[2,2,48,768]{3,2,1,0:T(8,128)(2,1)S(1)} %pad_maximum_fusion.7), channel_id=1, source_target_pairs={{0,4},{1,5},{2,6},{3,7},{4,0},{5,1},{6,2},{7,3},{8,12},{9,13},{10,... | collective-permute-start | bytes 884744 | tf_op jit(solution)/shard_map/ppermute | solution.py:307
  36.1 14.4 %collective-permute-start.6 = (bf16[8,48,384]{2,1,0:T(8,128)(2,1)S(1)}, bf16[8,48,384]{2,1,0:T(8,128)(2,1)}, u32[]{:S(2)}, u32[]{:S(2)}) collective-permute-start(bf16[8,48,384]{2,1,0:T(8,128)(2,1)S(1)} %constant_dynamic-update-slice_fusion.2.rest_2_), channel_id=1, source_target_pairs={{0,2},{1,3},{2,0},{3,1},{4,6},{5,7},{6,4},{7,5},{8,10},{9,11},{10,... | collective-permute-start | bytes 884744 | tf_op jit(solution)/shard_map/ppermute | solution.py:307
  36.8 13.7 %collective-permute-start.5 = (bf16[8,48,384]{2,1,0:T(8,128)(2,1)S(1)}, bf16[8,48,384]{2,1,0:T(8,128)(2,1)}, u32[]{:S(2)}, u32[]{:S(2)}) collective-permute-start(bf16[8,48,384]{2,1,0:T(8,128)(2,1)S(1)} %constant_dynamic-update-slice_fusion.rest_0_), channel_id=1, source_target_pairs={{0,16},{16,0},{1,17},{17,1},{2,18},{18,2},{3,19},{19,3},{4,20},{20... | collective-permute-start | bytes 884744 | tf_op jit(solution)/shard_map/ppermute | solution.py:311
  51.2 13.3 %collective-permute-start.10 = (bf16[3,48,768]{2,1,0:T(8,128)(2,1)S(1)}, bf16[3,48,768]{2,1,0:T(8,128)(2,1)S(1)}, u32[]{:S(2)}, u32[]{:S(2)}) collective-permute-start(bf16[3,48,768]{2,1,0:T(8,128)(2,1)S(1)} %pad_maximum_fusion.17), channel_id=1, source_target_pairs={{0,8},{1,9},{2,10},{3,11},{4,12},{5,13},{6,14},{7,15},{8,0},{9,1},... | collective-permute-start | bytes 663560 | tf_op jit(solution)/shard_map/ppermute | solution.py:307
  53.0 11.5 %collective-permute-start.9 = (bf16[4,48,768]{2,1,0:T(8,128)(2,1)S(1)}, bf16[4,48,768]{2,1,0:T(8,128)(2,1)S(1)}, u32[]{:S(2)}, u32[]{:S(2)}) collective-permute-start(bf16[4,48,768]{2,1,0:T(8,128)(2,1)S(1)} %pad_maximum_fusion.11), channel_id=1, source_target_pairs={{0,16},{16,0},{1,17},{17,1},{2,18},{18,2},{3,19},{19,3},{4,20},{20... | collective-permute-start | bytes 884744 | tf_op jit(solution)/shard_map/ppermute | solution.py:311
  54.5 10.0 %collective-permute-start.8 = (bf16[4,48,768]{2,1,0:T(8,128)(2,1)S(1)}, bf16[4,48,768]{2,1,0:T(8,128)(2,1)S(1)}, u32[]{:S(2)}, u32[]{:S(2)}) collective-permute-start(bf16[4,48,768]{2,1,0:T(8,128)(2,1)S(1)} %pad_maximum_fusion.10), channel_id=1, source_target_pairs={{0,2},{1,3},{2,0},{3,1},{4,6},{5,7},{6,4},{7,5},{8,10},{9,11},{10,... | collective-permute-start | bytes 884744 | tf_op jit(solution)/shard_map/ppermute | solution.py:307
  64.7 12.6 %collective-permute-start.21 = (bf16[3,2,48,768]{3,2,1,0:T(8,128)(2,1)S(1)}, bf16[3,2,48,768]{3,2,1,0:T(8,128)(2,1)S(1)}, u32[]{:S(2)}, u32[]{:S(2)}) collective-permute-start(bf16[3,2,48,768]{3,2,1,0:T(8,128)(2,1)S(1)} %pad_maximum_fusion), channel_id=1, source_target_pairs={{0,4},{1,5},{2,6},{3,7},{4,0},{5,1},{6,2},{7,3},{8,12},{9,13},{10,... | collective-permute-start | bytes 1327112 | tf_op jit(solution)/shard_map/ppermute | solution.py:307
  65.9 14.2 %collective-permute-start.20 = (bf16[8,48,768]{2,1,0:T(8,128)(2,1)S(1)}, bf16[8,48,768]{2,1,0:T(8,128)(2,1)S(1)}, u32[]{:S(2)}, u32[]{:S(2)}) collective-permute-start(bf16[8,48,768]{2,1,0:T(8,128)(2,1)S(1)} %pad_maximum_fusion.2.rest_2_.rest_0_), channel_id=1, source_target_pairs={{0,2},{1,3},{2,0},{3,1},{4,6},{5,7},{6,4},{7,5},{8,10},{9,11},{10,... | collective-permute-start | bytes 1769480 | tf_op jit(solution)/shard_map/ppermute | solution.py:307
  66.5 14.0 %collective-permute-start.19 = (bf16[8,48,768]{2,1,0:T(8,128)(2,1)S(1)}, bf16[8,48,768]{2,1,0:T(8,128)(2,1)S(1)}, u32[]{:S(2)}, u32[]{:S(2)}) collective-permute-start(bf16[8,48,768]{2,1,0:T(8,128)(2,1)S(1)} %pad_maximum_fusion.1.rest_0_), channel_id=1, source_target_pairs={{0,16},{16,0},{1,17},{17,1},{2,18},{18,2},{3,19},{19,3},{4,20},{20... | collective-permute-start | bytes 1769480 | tf_op jit(solution)/shard_map/ppermute | solution.py:311
  80.5 9.7 %collective-permute-start.24 = (bf16[4,48,768]{2,1,0:T(8,128)(2,1)S(1)}, bf16[4,48,768]{2,1,0:T(8,128)(2,1)S(1)}, u32[]{:S(2)}, u32[]{:S(2)}) collective-permute-start(bf16[4,48,768]{2,1,0:T(8,128)(2,1)S(1)} %pad_maximum_fusion.14), channel_id=1, source_target_pairs={{0,2},{1,3},{2,0},{3,1},{4,6},{5,7},{6,4},{7,5},{8,10},{9,11},{10,... | collective-permute-start | bytes 884744 | tf_op jit(solution)/shard_map/ppermute | solution.py:307
  83.7 10.0 %collective-permute-start.22 = (bf16[4,48,768]{2,1,0:T(8,128)(2,1)S(1)}, bf16[4,48,768]{2,1,0:T(8,128)(2,1)S(1)}, u32[]{:S(2)}, u32[]{:S(2)}) collective-permute-start(bf16[4,48,768]{2,1,0:T(8,128)(2,1)S(1)} %pad_maximum_fusion.12), channel_id=1, source_target_pairs={{0,2},{1,3},{2,0},{3,1},{4,6},{5,7},{6,4},{7,5},{8,10},{9,11},{10,... | collective-permute-start | bytes 884744 | tf_op jit(solution)/shard_map/ppermute | solution.py:307
  84.2 10.5 %collective-permute-start.28 = (bf16[8,48,768]{2,1,0:T(8,128)(2,1)S(1)}, bf16[8,48,768]{2,1,0:T(8,128)(2,1)S(1)}, u32[]{:S(2)}, u32[]{:S(2)}) collective-permute-start(bf16[8,48,768]{2,1,0:T(8,128)(2,1)S(1)} %pad_maximum_fusion.2.rest_2_.rest_0_), channel_id=1, source_target_pairs={{0,1},{1,0},{2,3},{3,2},{4,5},{5,4},{6,7},{7,6},{8,9},{9,8},{10,11... | collective-permute-start | bytes 1769480 | tf_op jit(solution)/shard_map/ppermute | solution.py:307
  84.2 11.9 %collective-permute-start.26 = (bf16[8,48,768]{2,1,0:T(8,128)(2,1)S(1)}, bf16[8,48,768]{2,1,0:T(8,128)(2,1)S(1)}, u32[]{:S(2)}, u32[]{:S(2)}) collective-permute-start(bf16[8,48,768]{2,1,0:T(8,128)(2,1)S(1)} %pad_maximum_fusion.1.rest_0_), channel_id=1, source_target_pairs={{0,1},{1,0},{2,3},{3,2},{4,5},{5,4},{6,7},{7,6},{8,9},{9,8},{10,11... | collective-permute-start | bytes 1769480 | tf_op jit(solution)/shard_map/ppermute | solution.py:307
  90.2 8.4 %collective-permute-start.27 = (bf16[8,48,768]{2,1,0:T(8,128)(2,1)S(1)}, bf16[8,48,768]{2,1,0:T(8,128)(2,1)S(1)}, u32[]{:S(2)}, u32[]{:S(2)}) collective-permute-start(bf16[8,48,768]{2,1,0:T(8,128)(2,1)S(1)} %collective-permute-done.19.rest_1_), channel_id=1, source_target_pairs={{0,1},{1,0},{2,3},{3,2},{4,5},{5,4},{6,7},{7,6},{8,9},{9,8},{10,11... | collective-permute-start | bytes 1769480 | tf_op jit(solution)/shard_map/ppermute | solution.py:307
  90.3 8.3 %collective-permute-start.29 = (bf16[8,48,768]{2,1,0:T(8,128)(2,1)S(1)}, bf16[8,48,768]{2,1,0:T(8,128)(2,1)S(1)}, u32[]{:S(2)}, u32[]{:S(2)}) collective-permute-start(bf16[8,48,768]{2,1,0:T(8,128)(2,1)S(1)} %collective-permute-done.20.rest_3_.rest_1_), channel_id=1, source_target_pairs={{0,1},{1,0},{2,3},{3,2},{4,5},{5,4},{6,7},{7,6},{8,9},{9,8},{10,11... | collective-permute-start | bytes 1769480 | tf_op jit(solution)/shard_map/ppermute | solution.py:307
  94.7 21.2 %collective-permute-start.32 = (bf16[8,48,768]{2,1,0:T(8,128)(2,1)S(1)}, bf16[8,48,768]{2,1,0:T(8,128)(2,1)}, u32[]{:S(2)}, u32[]{:S(2)}) collective-permute-start(bf16[8,48,768]{2,1,0:T(8,128)(2,1)S(1)} %pad_maximum_fusion.4.rest_6_), channel_id=1, source_target_pairs={{0,2},{1,3},{2,0},{3,1},{4,6},{5,7},{6,4},{7,5},{8,10},{9,11},{10,... | collective-permute-start | bytes 1769480 | tf_op jit(solution)/shard_map/ppermute | solution.py:307
  96.2 19.8 %collective-permute-start.31 = (bf16[8,48,768]{2,1,0:T(8,128)(2,1)}, bf16[8,48,768]{2,1,0:T(8,128)(2,1)S(1)}, u32[]{:S(2)}, u32[]{:S(2)}) collective-permute-start(bf16[8,48,768]{2,1,0:T(8,128)(2,1)} %pad_maximum_fusion.3.rest_4_), channel_id=1, source_target_pairs={{0,16},{16,0},{1,17},{17,1},{2,18},{18,2},{3,19},{19,3},{4,20},{20... | collective-permute-start | bytes 1769480 | tf_op jit(solution)/shard_map/ppermute | solution.py:311
  115.3 21.4 %collective-permute-start.30 = (bf16[4,8,48,768]{3,2,1,0:T(8,128)(2,1)}, bf16[4,8,48,768]{3,2,1,0:T(8,128)(2,1)S(1)}, u32[]{:S(2)}, u32[]{:S(2)}) collective-permute-start(bf16[4,8,48,768]{3,2,1,0:T(8,128)(2,1)} %get-tuple-element.157), channel_id=1, source_target_pairs={{0,1},{1,0},{2,3},{3,2},{4,5},{5,4},{6,7},{7,6},{8,9},{9,8},{10,11... | collective-permute-start | bytes 7077896 | tf_op jit(solution)/shard_map/ppermute | solution.py:307
  136.6 19.2 %collective-permute-start.39 = (bf16[2,8,48,768]{3,2,1,0:T(8,128)(2,1)}, bf16[2,8,48,768]{3,2,1,0:T(8,128)(2,1)S(1)}, u32[]{:S(2)}, u32[]{:S(2)}) collective-permute-start(bf16[2,8,48,768]{3,2,1,0:T(8,128)(2,1)} %get-tuple-element.171), channel_id=1, source_target_pairs={{0,1},{1,0},{2,3},{3,2},{4,5},{5,4},{6,7},{7,6},{8,9},{9,8},{10,11... | collective-permute-start | bytes 3538952 | tf_op jit(solution)/shard_map/ppermute | solution.py:307
  137.3 18.5 %collective-permute-start.37 = (bf16[8,48,768]{2,1,0:T(8,128)(2,1)S(1)}, bf16[8,48,768]{2,1,0:T(8,128)(2,1)S(1)}, u32[]{:S(2)}, u32[]{:S(2)}) collective-permute-start(bf16[8,48,768]{2,1,0:T(8,128)(2,1)S(1)} %get-tuple-element.248), channel_id=1, source_target_pairs={{0,16},{16,0},{1,17},{17,1},{2,18},{18,2},{3,19},{19,3},{4,20},{20... | collective-permute-start | bytes 1769480 | tf_op jit(solution)/shard_map/ppermute | solution.py:311
  137.6 18.2 %collective-permute-start.38 = (bf16[8,48,768]{2,1,0:T(8,128)(2,1)S(1)}, bf16[8,48,768]{2,1,0:T(8,128)(2,1)S(1)}, u32[]{:S(2)}, u32[]{:S(2)}) collective-permute-start(bf16[8,48,768]{2,1,0:T(8,128)(2,1)S(1)} %get-tuple-element.247), channel_id=1, source_target_pairs={{0,2},{1,3},{2,0},{3,1},{4,6},{5,7},{6,4},{7,5},{8,10},{9,11},{10,... | collective-permute-start | bytes 1769480 | tf_op jit(solution)/shard_map/ppermute | solution.py:307
  155.7 18.0 %collective-permute-start.42 = (bf16[2,8,48,768]{3,2,1,0:T(8,128)(2,1)}, bf16[2,8,48,768]{3,2,1,0:T(8,128)(2,1)S(1)}, u32[]{:S(2)}, u32[]{:S(2)}) collective-permute-start(bf16[2,8,48,768]{3,2,1,0:T(8,128)(2,1)} %get-tuple-element.175), channel_id=1, source_target_pairs={{0,1},{1,0},{2,3},{3,2},{4,5},{5,4},{6,7},{7,6},{8,9},{9,8},{10,11... | collective-permute-start | bytes 3538952 | tf_op jit(solution)/shard_map/ppermute | solution.py:307
  156.0 17.7 %collective-permute-start.41 = (bf16[4,48,768]{2,1,0:T(8,128)(2,1)S(1)}, bf16[4,48,768]{2,1,0:T(8,128)(2,1)S(1)}, u32[]{:S(2)}, u32[]{:S(2)}) collective-permute-start(bf16[4,48,768]{2,1,0:T(8,128)(2,1)S(1)} %get-tuple-element.266), channel_id=1, source_target_pairs={{0,16},{16,0},{1,17},{17,1},{2,18},{18,2},{3,19},{19,3},{4,20},{20... | collective-permute-start | bytes 884744 | tf_op jit(solution)/shard_map/ppermute | solution.py:311
  157.9 15.7 %collective-permute-start.40 = (bf16[4,48,768]{2,1,0:T(8,128)(2,1)S(1)}, bf16[4,48,768]{2,1,0:T(8,128)(2,1)S(1)}, u32[]{:S(2)}, u32[]{:S(2)}) collective-permute-start(bf16[4,48,768]{2,1,0:T(8,128)(2,1)S(1)} %get-tuple-element.267), channel_id=1, source_target_pairs={{0,2},{1,3},{2,0},{3,1},{4,6},{5,7},{6,4},{7,5},{8,10},{9,11},{10,... | collective-permute-start | bytes 884744 | tf_op jit(solution)/shard_map/ppermute | solution.py:307
  159.7 30.9 %collective-permute-start.44 = (bf16[8,48,768]{2,1,0:T(8,128)(2,1)S(1)}, bf16[8,48,768]{2,1,0:T(8,128)(2,1)S(1)}, u32[]{:S(2)}, u32[]{:S(2)}) collective-permute-start(bf16[8,48,768]{2,1,0:T(8,128)(2,1)S(1)} %get-tuple-element.260), channel_id=1, source_target_pairs={{0,16},{16,0},{1,17},{17,1},{2,18},{18,2},{3,19},{19,3},{4,20},{20... | collective-permute-start | bytes 1769480 | tf_op jit(solution)/shard_map/ppermute | solution.py:311
  173.6 17.0 %collective-permute-start.46 = (bf16[4,8,48,384]{3,2,1,0:T(8,128)(2,1)}, bf16[4,8,48,384]{3,2,1,0:T(8,128)(2,1)S(1)}, u32[]{:S(2)}, u32[]{:S(2)}) collective-permute-start(bf16[4,8,48,384]{3,2,1,0:T(8,128)(2,1)} %get-tuple-element.189), channel_id=1, source_target_pairs={{0,1},{1,0},{2,3},{3,2},{4,5},{5,4},{6,7},{7,6},{8,9},{9,8},{10,11... | collective-permute-start | bytes 3538952 | tf_op jit(solution)/shard_map/ppermute | solution.py:307
  175.1 15.4 %collective-permute-start.45 = (bf16[8,48,768]{2,1,0:T(8,128)(2,1)S(1)}, bf16[8,48,768]{2,1,0:T(8,128)(2,1)S(1)}, u32[]{:S(2)}, u32[]{:S(2)}) collective-permute-start(bf16[8,48,768]{2,1,0:T(8,128)(2,1)S(1)} %get-tuple-element.258), channel_id=1, source_target_pairs={{0,2},{1,3},{2,0},{3,1},{4,6},{5,7},{6,4},{7,5},{8,10},{9,11},{10,... | collective-permute-start | bytes 1769480 | tf_op jit(solution)/shard_map/ppermute | solution.py:307
  176.0 14.6 %collective-permute-start.43 = (bf16[2,2,48,768]{3,2,0,1:T(8,128)(2,1)S(1)}, bf16[2,2,48,768]{3,2,0,1:T(8,128)(2,1)S(1)}, u32[]{:S(2)}, u32[]{:S(2)}) collective-permute-start(bf16[2,2,48,768]{3,2,0,1:T(8,128)(2,1)S(1)} %copy.49), channel_id=1, source_target_pairs={{0,4},{1,5},{2,6},{3,7},{4,0},{5,1},{6,2},{7,3},{8,12},{9,13},{10,... | collective-permute-start | bytes 884744 | tf_op jit(solution)/shard_map/ppermute | solution.py:307
  190.6 22.4 %collective-permute-start.52 = (bf16[4,8,48,384]{3,2,1,0:T(8,128)(2,1)}, bf16[4,8,48,384]{3,2,1,0:T(8,128)(2,1)S(1)}, u32[]{:S(2)}, u32[]{:S(2)}) collective-permute-start(bf16[4,8,48,384]{3,2,1,0:T(8,128)(2,1)} %get-tuple-element.196), channel_id=1, source_target_pairs={{0,1},{1,0},{2,3},{3,2},{4,5},{5,4},{6,7},{7,6},{8,9},{9,8},{10,11... | collective-permute-start | bytes 3538952 | tf_op jit(solution)/shard_map/ppermute | solution.py:307
  190.9 19.9 %collective-permute-start.50 = (bf16[8,48,384]{2,1,0:T(8,128)(2,1)S(1)}, bf16[8,48,384]{2,1,0:T(8,128)(2,1)S(1)}, u32[]{:S(2)}, u32[]{:S(2)}) collective-permute-start(bf16[8,48,384]{2,1,0:T(8,128)(2,1)S(1)} %get-tuple-element.256), channel_id=1, source_target_pairs={{0,16},{16,0},{1,17},{17,1},{2,18},{18,2},{3,19},{19,3},{4,20},{20... | collective-permute-start | bytes 884744 | tf_op jit(solution)/shard_map/ppermute | solution.py:311
  192.5 18.3 %collective-permute-start.51 = (bf16[8,48,384]{2,1,0:T(8,128)(2,1)S(1)}, bf16[8,48,384]{2,1,0:T(8,128)(2,1)S(1)}, u32[]{:S(2)}, u32[]{:S(2)}) collective-permute-start(bf16[8,48,384]{2,1,0:T(8,128)(2,1)S(1)} %get-tuple-element.255), channel_id=1, source_target_pairs={{0,2},{1,3},{2,0},{3,1},{4,6},{5,7},{6,4},{7,5},{8,10},{9,11},{10,... | collective-permute-start | bytes 884744 | tf_op jit(solution)/shard_map/ppermute | solution.py:307
  194.0 16.8 %collective-permute-start.49 = (bf16[4,48,768]{2,1,0:T(8,128)(2,1)S(1)}, bf16[4,48,768]{2,1,0:T(8,128)(2,1)S(1)}, u32[]{:S(2)}, u32[]{:S(2)}) collective-permute-start(bf16[4,48,768]{2,1,0:T(8,128)(2,1)S(1)} %get-tuple-element.262), channel_id=1, source_target_pairs={{0,16},{16,0},{1,17},{17,1},{2,18},{18,2},{3,19},{19,3},{4,20},{20... | collective-permute-start | bytes 884744 | tf_op jit(solution)/shard_map/ppermute | solution.py:311
  194.7 9.3 %collective-permute-start.47 = (bf16[2,48,768]{2,1,0:T(8,128)(2,1)S(1)}, bf16[2,48,768]{2,1,0:T(8,128)(2,1)S(1)}, u32[]{:S(2)}, u32[]{:S(2)}) collective-permute-start(bf16[2,48,768]{2,1,0:T(8,128)(2,1)S(1)} %get-tuple-element.282), channel_id=1, source_target_pairs={{0,8},{1,9},{2,10},{3,11},{4,12},{5,13},{6,14},{7,15},{8,0},{9,1},... | collective-permute-start | bytes 442376 | tf_op jit(solution)/shard_map/ppermute | solution.py:307
  204.0 8.9 %collective-permute-start.48 = (bf16[4,48,768]{2,1,0:T(8,128)(2,1)S(1)}, bf16[4,48,768]{2,1,0:T(8,128)(2,1)S(1)}, u32[]{:S(2)}, u32[]{:S(2)}) collective-permute-start(bf16[4,48,768]{2,1,0:T(8,128)(2,1)S(1)} %get-tuple-element.264), channel_id=1, source_target_pairs={{0,2},{1,3},{2,0},{3,1},{4,6},{5,7},{6,4},{7,5},{8,10},{9,11},{10,... | collective-permute-start | bytes 884744 | tf_op jit(solution)/shard_map/ppermute | solution.py:307
  215.0 12.8 %collective-permute-start.56 = (bf16[4,48,384]{2,1,0:T(8,128)(2,1)S(1)}, bf16[4,48,384]{2,1,0:T(8,128)(2,1)S(1)}, u32[]{:S(2)}, u32[]{:S(2)}) collective-permute-start(bf16[4,48,384]{2,1,0:T(8,128)(2,1)S(1)} %get-tuple-element.279), channel_id=1, source_target_pairs={{0,2},{1,3},{2,0},{3,1},{4,6},{5,7},{6,4},{7,5},{8,10},{9,11},{10,... | collective-permute-start | bytes 442376 | tf_op jit(solution)/shard_map/ppermute | solution.py:307
  215.7 12.1 %collective-permute-start.55 = (bf16[2,2,48,768]{3,2,1,0:T(8,128)(2,1)S(1)}, bf16[2,2,48,768]{3,2,1,0:T(8,128)(2,1)S(1)}, u32[]{:S(2)}, u32[]{:S(2)}) collective-permute-start(bf16[2,2,48,768]{3,2,1,0:T(8,128)(2,1)S(1)} %pad_maximum_fusion.16), channel_id=1, source_target_pairs={{0,4},{1,5},{2,6},{3,7},{4,0},{5,1},{6,2},{7,3},{8,12},{9,13},{10,... | collective-permute-start | bytes 884744 | tf_op jit(solution)/shard_map/ppermute | solution.py:307
  216.1 11.7 %collective-permute-start.53 = (bf16[8,48,384]{2,1,0:T(8,128)(2,1)S(1)}, bf16[8,48,384]{2,1,0:T(8,128)(2,1)S(1)}, u32[]{:S(2)}, u32[]{:S(2)}) collective-permute-start(bf16[8,48,384]{2,1,0:T(8,128)(2,1)S(1)} %get-tuple-element.252), channel_id=1, source_target_pairs={{0,16},{16,0},{1,17},{17,1},{2,18},{18,2},{3,19},{19,3},{4,20},{20... | collective-permute-start | bytes 884744 | tf_op jit(solution)/shard_map/ppermute | solution.py:311
  216.6 11.3 %collective-permute-start.54 = (bf16[8,48,384]{2,1,0:T(8,128)(2,1)S(1)}, bf16[8,48,384]{2,1,0:T(8,128)(2,1)S(1)}, u32[]{:S(2)}, u32[]{:S(2)}) collective-permute-start(bf16[8,48,384]{2,1,0:T(8,128)(2,1)S(1)} %get-tuple-element.251), channel_id=1, source_target_pairs={{0,2},{1,3},{2,0},{3,1},{4,6},{5,7},{6,4},{7,5},{8,10},{9,11},{10,... | collective-permute-start | bytes 884744 | tf_op jit(solution)/shard_map/ppermute | solution.py:307
  219.5 8.4 %collective-permute-start.58 = (bf16[2,48,768]{2,1,0:T(8,128)(2,1)S(1)}, bf16[2,48,768]{2,1,0:T(8,128)(2,1)S(1)}, u32[]{:S(2)}, u32[]{:S(2)}) collective-permute-start(bf16[2,48,768]{2,1,0:T(8,128)(2,1)S(1)} %add_convert_fusion.21), channel_id=1, source_target_pairs={{0,16},{16,0},{1,17},{17,1},{2,18},{18,2},{3,19},{19,3},{4,20},{20... | collective-permute-start | bytes 442376 | tf_op jit(solution)/shard_map/ppermute | solution.py:311
  230.8 10.0 %collective-permute-start.61 = (bf16[2,48,768]{2,1,0:T(8,128)(2,1)S(1)}, bf16[2,48,768]{2,1,0:T(8,128)(2,1)S(1)}, u32[]{:S(2)}, u32[]{:S(2)}) collective-permute-start(bf16[2,48,768]{2,1,0:T(8,128)(2,1)S(1)} %fusion.36), channel_id=1, source_target_pairs={{0,8},{1,9},{2,10},{3,11},{4,12},{5,13},{6,14},{7,15},{8,0},{9,1},... | collective-permute-start | bytes 442376 | tf_op jit(solution)/shard_map/ppermute | solution.py:307
  241.0 9.5 %collective-permute-start.67 = (bf16[2,48,768]{2,1,0:T(8,128)(2,1)S(1)}, bf16[2,48,768]{2,1,0:T(8,128)(2,1)S(1)}, u32[]{:S(2)}, u32[]{:S(2)}) collective-permute-start(bf16[2,48,768]{2,1,0:T(8,128)(2,1)S(1)} %fusion.16), channel_id=1, source_target_pairs={{0,16},{16,0},{1,17},{17,1},{2,18},{18,2},{3,19},{19,3},{4,20},{20... | collective-permute-start | bytes 442376 | tf_op jit(solution)/shard_map/ppermute | solution.py:311
  242.2 8.2 %collective-permute-start.66 = (bf16[2,2,48,384]{3,2,0,1:T(8,128)(2,1)S(1)}, bf16[2,2,48,384]{3,2,0,1:T(8,128)(2,1)S(1)}, u32[]{:S(2)}, u32[]{:S(2)}) collective-permute-start(bf16[2,2,48,384]{3,2,0,1:T(8,128)(2,1)S(1)} %copy.53), channel_id=1, source_target_pairs={{0,4},{1,5},{2,6},{3,7},{4,0},{5,1},{6,2},{7,3},{8,12},{9,13},{10,... | collective-permute-start | bytes 442376 | tf_op jit(solution)/shard_map/ppermute | solution.py:307
  (57 other events, 405.6 us)

commit v3 on v2

--- a/solution.py
+++ b/solution.py
@@ -311,6 +311,11 @@
     return lax.ppermute(array, "dp", [(0, 1), (1, 0)])
 
 
+def cross(array):
+    axes = ("dp", "fsdp")
+    return lax.ppermute(array, axes, [(i, i ^ 16 ^ BIT_C) for i in range(32)])
+
+
 def join(*arrays):
     return jnp.concatenate(arrays, axis=0)
 
@@ -333,6 +338,19 @@
 
 def first_hops(parts):
     return swap(parts[1]), hop(parts[3], BIT_Y)
+
+
+def together(move, *arrays):
+    flat = [array.reshape(-1, PIECE, 384) for array in arrays]
+    came, at, out = move(join(*flat)), 0, []
+    for array, part in zip(arrays, flat):
+        out.append(came[at : at + part.shape[0]].reshape(array.shape))
+        at += part.shape[0]
+    return out
+
+
+def hop_y(array):
+    return hop(array, BIT_Y)
 
 
 def first_sums(parts, got):
@@ -371,10 +389,6 @@
     return plus(parts[0], got[0])
 
 
-def place(mine, other, x, half, line):
-    return jnp.where(x == half, mine[line], other[line]).astype(f32)
-
-
 def product(left, right, dims):
     return lax.dot_general(left, right, (dims, ((), ())), preferred_element_type=f32)
 
@@ -388,12 +402,18 @@
     return (xr, yr) if line == 0 else (2 + yr, xr)
 
 
-def load_chunk(store, refs, i, line, xr):
-    for m in range(16):
-        c, yr, z0r, z1r = m & 1, (m >> 1) & 1, (m >> 2) & 1, (m >> 3) & 1
-        array, part = slot(line, xr, yr) if isinstance(xr, int) else (2 + yr, xr)
-        row = pl.multiple_of((i ^ m) * PIECE, 16)
-        store[pl.ds(row, PIECE), :] = refs[4 * c + array][part * 4 + z0r * 2 + z1r]
+def rel_places():
+    return [(m, m & 1, (m >> 1) & 1, ((m >> 2) & 1) * 2 + (m >> 3)) for m in range(16)]
+
+
+def rows_of(i, m):
+    return pl.ds(pl.multiple_of((i ^ m) * PIECE, 16), PIECE)
+
+
+def load_line(store, halves, i, columns=slice(None)):
+    for m, c, yr, z in rel_places():
+        ref, first = halves[c][yr]
+        store[rows_of(i, m), columns] = ref[first + z, 0:PIECE, :]
 
 
 def save_chunk(value, outs, i, line, xr):
@@ -451,30 +471,42 @@
 
 
 def prepare_kernel(info, qkv, fc1, fc2, *rest):
-    vectors, (pair, ahead, up, down) = rest[:9], rest[9:]
+    vectors, (lead, *groups) = rest[:9], rest[9:]
     x = info[1]
-    ahead[0, 0:PIECE, :] = qkv[:, 0:WIDE]
-    rows = [jnp.pad(v[...].astype(f32).reshape(1, -1), ((0, 0), (0, 256 - v.shape[0]))) for v in vectors]
-    ahead[0, PIECE : PIECE + 16, 0:256] = jnp.concatenate(rows + [jnp.zeros((7, 256), f32)]).astype(bf16)
-    ahead[0, PIECE : PIECE + 16, 256:WIDE] = jnp.zeros((16, WIDE - 256), bf16)
-    for line in range(2):
-        at = pl.multiple_of(WIDE + WIDE * x + 384 * line, 128)
-        pair[line] = qkv[:, pl.ds(at, 384)]
-        up[line] = fc1[:, pl.ds(pl.multiple_of((2 * x + line) * WIDE, 128), WIDE)]
-        down[line] = fc2[pl.ds(pl.multiple_of((2 * x + line) * PIECE, 16), PIECE), :]
-
-
-def load_qkv(weight, refs, query_own, query_other, i, x):
-    load_direct(weight.at[0], query_own, query_other, i, (2, 4, 1))
-    for line in range(2):
-        for xr in range(2):
-            load_chunk(weight.at[1 + (x ^ xr), :, 384 * line : 384 * line + 384], refs, i, line, xr)
+    at = pl.multiple_of(WIDE + WIDE * x, 128)
+    lead[0, 0:48, :] = qkv[:, pl.ds(at + 384, 384)]
+    lead[0, 48:96, :] = qkv[:, pl.ds(pl.multiple_of(384 * x, 128), 384)]
+    lead[0, 96:144, :] = qkv[:, pl.ds(at, 384)]
+    rows = [v[...].astype(f32).reshape(1, -1) for v in vectors]
+    rows = rows[:8] + [rows[8][:, 48 * k : 48 * k + 48] for k in range(4)]
+    rows = [jnp.pad(row, ((0, 0), (0, 336))) for row in rows]
+    lead[0, 144:160, :] = jnp.concatenate(rows + [jnp.zeros((4, 384), f32)]).astype(bf16)
+    for half in range(2):
+
+        @pl.when(x == half)
+        def _():
+            for s in range(2):
+                first = 48 * (2 * half + s)
+                cuts = [fc1[:, 192 * j + first : 192 * j + first + 48] for j in range(16)]
+                groups[s][0] = jnp.concatenate(cuts, axis=1)
+                groups[s][1] = fc2[first : first + 48, :]
+
+
+def load_qkv(weight, refs, i, x):
+    for xr in range(2):
+        h = x ^ xr
+        a = [[(refs[6 * c + xr], 4 * yr) for yr in range(2)] for c in range(2)]
+        b = [[(refs[6 * c + 2 + yr], 4 * xr) for yr in range(2)] for c in range(2)]
+        q = [[(refs[6 * c + 4 + xr], 4 * yr) for yr in range(2)] for c in range(2)]
+        load_line(weight.at[1 + h], a, i, slice(0, 384))
+        load_line(weight.at[1 + h], b, i, slice(384, 768))
+        load_line(weight.at[0], q, i, pl.ds(pl.multiple_of(384 * h, 128), 384))
 
 
 def qkv_kernel(info, tok, small, *rest):
-    refs, (query_own, query_other, packed, normed, weight) = rest[:8], rest[8:]
+    refs, (packed, normed, weight) = rest[:12], rest[12:]
     i, x = info[0], info[1]
-    load_qkv(weight, refs, query_own, query_other, i, x)
+    load_qkv(weight, refs, i, x)
     for r in range(2):
         rows = slice(256 * r, 256 * r + 256)
         unit, _ = unit_of(tok[rows, :].astype(f32))
@@ -487,156 +519,144 @@
         packed[rows, 1536:2304] = (product(low, weight[2], NN) + small[3:4, :]).astype(bf16)
 
 
-def attend_kernel(info, packed, cot, attended, grad_two, lse):
+def attend_kernel(info, packed, cot, attended, grad_two, lse, scores, weighting):
     r = pl.program_id(0)
     column, across, scale, inside = row_facts(info, r)
     same = column == across
     lane = lax.broadcasted_iota(jnp.int32, (256, 128), 1)
     kept = jnp.zeros((256, 128), f32)
+    for g in range(HEADS):
+        query = packed[:, 64 * g : 64 * g + 64] * 0.125
+        scores[g] = product(query, packed[:, 768 + 64 * g : 832 + 64 * g], NT)
+    for g in range(HEADS):
+        masked = jnp.where(same, scores[g], NEGATIVE)
+        top = jnp.max(masked, axis=-1, keepdims=True)
+        raised = jnp.exp(masked - top)
+        total = jnp.sum(raised, axis=-1, keepdims=True)
+        weighting[g] = (raised * (1.0 / total)).astype(bf16)
+        kept = jnp.where(lane == g, top + jnp.log(total), kept)
+    lse[...] = kept
     for h in range(0, HEADS, 2):
-        pair = []
-        for g in (h, h + 1):
-            query = packed[:, 64 * g : 64 * g + 64] * 0.125
-            scores = product(query, packed[:, 768 + 64 * g : 832 + 64 * g], NT)
-            scores = jnp.where(same, scores, NEGATIVE)
-            top = jnp.max(scores, axis=-1, keepdims=True)
-            raised = jnp.exp(scores - top)
-            total = jnp.sum(raised, axis=-1, keepdims=True)
-            low = (raised / total).astype(bf16)
-            pair.append(product(low, packed[:, 1536 + 64 * g : 1600 + 64 * g], NN).astype(bf16))
-            kept = jnp.where(lane == g, top + jnp.log(total), kept)
+        pair = [
+            product(weighting[g], packed[:, 1536 + 64 * g : 1600 + 64 * g], NN).astype(bf16)
+            for g in (h, h + 1)
+        ]
         attended[:, 64 * h : 64 * h + 128] = jnp.concatenate(pair, axis=1)
-    lse[...] = kept
     grad_two[...] = (cot[...].astype(f32) * inside * scale(1)).astype(bf16)
 
 
-def up_kernel(info, attended, tok, grad_two, small, proj_own, proj_other, *rest):
-    refs, (middle, normed, hidden, active, own, away, proj, weight, grad) = rest[:8], rest[8:]
+def hidden_units(block, normed, grad_two, small, branch, grad_normed, bias, weights, scratch):
+    active, low = scratch[:2]
+    for r in range(2):
+        rows = slice(256 * r, 256 * r + 256)
+        value = product(normed[rows, :], weights[0], NN) + small[pl.ds(8 + block, 1), :]
+        share = 0.5 * (1.0 + lax.erf(value * (0.5**0.5)))
+        active[rows, :] = (value * share).astype(bf16)
+        slope = share + value * (jnp.exp(-0.5 * value * value) * 0.3989422804014327)
+        low[rows, :] = (product(grad_two[rows, :], weights[1], NT) * slope).astype(bf16)
+    bias[pl.ds(8 + block, 1), :] = sums(low[...].astype(f32))
+    for r in range(2):
+        rows = slice(256 * r, 256 * r + 256)
+        branch[rows, :] += product(active[rows, :], weights[1], NN)
+        grad_normed[rows, :] += product(low[rows, :], weights[0], NT)
+    scratch[2][...] = product(normed[...], low[...], TN).astype(bf16)
+    scratch[3][...] = product(active[...], grad_two[...], TN).astype(bf16)
+
+
+def load_units(scratch, refs, i, t):
+    for step in range(2):
+
+        @pl.when(t == step)
+        def _():
+            up = [[(refs[4 * c + step], 4 * yr) for yr in range(2)] for c in range(2)]
+            down = [[(refs[4 * c + 2 + yr], 4 * step) for yr in range(2)] for c in range(2)]
+            load_line(scratch[4], up, i)
+            load_line(scratch[5], down, i)
+
+    return scratch[4][...], scratch[5][...]
+
+
+def save_units(scratch, own, away, i, t):
+    for m, c, yr, z in rel_places():
+        for part in range(2):
+            here = slice(384 * part, 384 * part + 384)
+            (own, away)[c][t, 4 * yr + z, part] = scratch[2][rows_of(i, m), here]
+            (own, away)[c][2 + yr, 4 * t + z, part] = scratch[3][rows_of(i, m), here]
+
+
+def first_units_kernel(info, attended, tok, grad_two, small, proj_own, proj_other, *rest):
+    refs, (middle, normed, branch, grad_normed, bias, own, away, proj, *scratch) = rest[:8], rest[8:]
     i, x, t = info[0], info[1], pl.program_id(0)
-    block = ((t & 1) ^ x) * 2 + (t >> 1)
 
     @pl.when(t == 0)
     def _():
-        load_direct(proj, proj_own, proj_other, i, (1, 2, 4))
+        load_direct(proj, proj_own, proj_other, i, (2, 4, 1))
         for r in range(2):
             rows = slice(256 * r, 256 * r + 256)
             _, _, scale, _ = row_facts(info, r)
-            branch = product(attended[rows, :], proj[...], NN) + small[4:5, :]
-            after = tok[rows, :].astype(f32) + scale(0) * branch
+            after = tok[rows, :].astype(f32) + scale(0) * (
+                product(attended[rows, :], proj[...], NN) + small[4:5, :]
+            )
             middle[rows, :] = after
             unit, _ = unit_of(after)
             normed[rows, :] = (unit * small[5:6, :] + small[6:7, :]).astype(bf16)
-
-    for step in range(4):
-
-        @pl.when(t == step)
-        def _():
-            load_chunk(weight, refs, i, step >> 1, step & 1)
-
-    value = product(normed[...], weight[...], NN) + small[pl.ds(8 + block, 1), :]
-    hidden[0] = value
-    low = (0.5 * value * (1.0 + lax.erf(value * (0.5**0.5)))).astype(bf16)
-    active[0] = low
-    grad[...] = product(low, grad_two[...], TN).astype(bf16)
-    far = block ^ (i >> 2)
-    spot = (far & 1) * 2 + (far >> 1)
-    for line in range(2):
-        for xr in range(2):
-            for near in range(4):
-                c, yr = near & 1, near >> 1
-                array, part = slot(line, xr, yr)
-                row = ((i & 3) ^ near) * 192 + ((xr ^ x) * 2 + line) * PIECE
-                (own, away)[c][array, part * 4 + spot] = grad[pl.ds(pl.multiple_of(row, 16), PIECE), :]
-
-
-def down_kernel(line, info, normed, grad_two, hidden, active, small, *rest):
-    refs1 = [None] * 8
-    refs1[2 * line], refs1[2 * line + 1], refs1[4 + 2 * line], refs1[5 + 2 * line] = rest[:4]
-    refs2, rest = rest[4:12], rest[12:]
-    if line == 0:
-        branch, grad_normed, bias, own, away, weight1, weight2, grad = rest
-    else:
-        branch_in, grad_normed_in, bias_in, middle, cot, result, grad_middle, grad_one, bias = rest[:9]
-        own, away, weight1, weight2, grad, branch, grad_normed = rest[9:]
+        branch[...] = jnp.zeros_like(branch)
+        grad_normed[...] = jnp.zeros_like(grad_normed)
+        bias[...] = jnp.zeros_like(bias)
+        bias[7:8, :] = sums(grad_two[...].astype(f32))
+
+    weights = load_units(scratch, refs, i, t)
+    hidden_units(2 * (t ^ x), normed, grad_two, small, branch, grad_normed, bias, weights, scratch)
+    save_units(scratch, own, away, i, t)
+
+
+def second_units_kernel(
+    info, normed, grad_two, small, branch_in, grad_normed_in, bias_in, middle, cot, *rest
+):
+    refs, (result, grad_middle, grad_one, bias, own, away, branch, grad_normed, *scratch) = rest[:8], rest[8:]
     i, x, t = info[0], info[1], pl.program_id(0)
-    block = (t ^ x) * 2 + line
 
     @pl.when(t == 0)
     def _():
-        if line == 0:
-            branch[...] = jnp.zeros_like(branch)
-            grad_normed[...] = jnp.zeros_like(grad_normed)
-            bias[...] = jnp.zeros_like(bias)
-            bias[7:8, :] = sums(grad_two[...].astype(f32))
-        else:
-            branch[...] = branch_in[...]
-            grad_normed[...] = grad_normed_in[...]
-            bias[...] = bias_in[...]
-
-    for step in range(2):
-
-        @pl.when(t == step)
-        def _():
-            load_chunk(weight1, refs1, i, line, step)
-
-    far = block ^ (i >> 2)
-    spot = (far & 1) * 2 + (far >> 1)
-    for row_line in range(2):
-        for xr in range(2):
-            for near in range(4):
-                c, yr = near & 1, near >> 1
-                array, part = slot(row_line, xr, yr)
-                row = ((i & 3) ^ near) * 192 + ((xr ^ x) * 2 + row_line) * PIECE
-                weight2[pl.ds(pl.multiple_of(row, 16), PIECE), :] = refs2[4 * c + array][part * 4 + spot]
-
-    branch[...] += product(active[0], weight2[...], NN)
-    value = hidden[0]
-    slope = 0.5 * (1.0 + lax.erf(value * (0.5**0.5))) + value * (
-        jnp.exp(-0.5 * value * value) * 0.3989422804014327
-    )
-    low = (product(grad_two[...], weight2[...], NT) * slope).astype(bf16)
-    bias[pl.ds(8 + block, 1), :] = sums(low.astype(f32))
-    grad_normed[...] += product(low, weight1[...], NT)
-    grad[...] = product(normed[...], low, TN).astype(bf16)
-    for m in range(16):
-        c, yr, z0r, z1r = m & 1, (m >> 1) & 1, (m >> 2) & 1, (m >> 3) & 1
-        array, part = (t, yr) if line == 0 else (yr, t)
-        row = pl.multiple_of((i ^ m) * PIECE, 16)
-        (own, away)[c][array, part * 4 + z0r * 2 + z1r] = grad[pl.ds(row, PIECE), :]
-
-    if line == 1:
-
-        @pl.when(t == 1)
-        def _():
-            for r in range(2):
-                rows = slice(256 * r, 256 * r + 256)
-                _, _, scale, inside = row_facts(info, r)
-                after = middle[rows, :]
-                result[rows, :] = (
-                    (after + scale(1) * (branch[rows, :] + small[7:8, :])) * inside
-                ).astype(bf16)
-                unit, root = unit_of(after)
-                incoming = grad_normed[rows, :]
-                bias[5:6, :] += sums(incoming * unit)
-                bias[6:7, :] += sums(incoming)
-                total = cot[rows, :].astype(f32) * inside + unit_back(unit, root, small[5:6, :], incoming)
-                grad_middle[rows, :] = total
-                low_one = (total * scale(0)).astype(bf16)
-                grad_one[rows, :] = low_one
-                bias[4:5, :] += sums(low_one.astype(f32))
+        branch[...] = branch_in[...]
+        grad_normed[...] = grad_normed_in[...]
+        bias[...] = bias_in[...]
+
+    weights = load_units(scratch, refs, i, t)
+    hidden_units(2 * (t ^ x) + 1, normed, grad_two, small, branch, grad_normed, bias, weights, scratch)
+    save_units(scratch, own, away, i, t)
+
+    @pl.when(t == 1)
+    def _():
+        for r in range(2):
+            rows = slice(256 * r, 256 * r + 256)
+            _, _, scale, inside = row_facts(info, r)
+            after = middle[rows, :]
+            result[rows, :] = (
+                (after + scale(1) * (branch[rows, :] + small[7:8, :])) * inside
+            ).astype(bf16)
+            unit, root = unit_of(after)
+            incoming = grad_normed[rows, :]
+            bias[5:6, :] += sums(incoming * unit)
+            bias[6:7, :] += sums(incoming)
+            total = cot[rows, :].astype(f32) * inside + unit_back(unit, root, small[5:6, :], incoming)
+            grad_middle[rows, :] = total
+            low_one = (total * scale(0)).astype(bf16)
+            grad_one[rows, :] = low_one
+            bias[4:5, :] += sums(low_one.astype(f32))
 
 
 def attend_back_kernel(group, info, queries, keys, values, lse, attended, grad_one, normed, *rest):
     if group == 0:
-        proj_own, proj_other, grad_packed, own, away, weight, proj_rest, grad, total = rest
+        proj_own, proj_other, grad_packed, own, away, weight, proj_rest, grad, *heads, total = rest
     else:
-        weight, proj_rest, grad_packed, own, away, grad = rest
+        weight, proj_rest, grad_packed, own, away, grad, *heads = rest
     i, x, r = info[0], info[1], pl.program_id(0)
     if group == 0:
 
         @pl.when(r == 0)
         def _():
-            load_direct(weight, proj_own, proj_other, i, (1, 2, 4))
+            load_direct(weight, proj_own, proj_other, i, (2, 4, 1))
             total[...] = jnp.zeros_like(total)
 
         total[...] += product(attended[...], grad_one[...], TN)
@@ -645,23 +665,26 @@
     same = column == across
     grad_attended = product(grad_one[...], weight[384 * group : 384 * group + 384, :], NT).astype(bf16)
     rows = pl.ds(pl.multiple_of(r * 256, 256), 256)
+    scores, backs, lows, highs = heads
+    queried = [queries[:, 64 * g : 64 * g + 64] * 0.125 for g in range(6)]
+    returned = [grad_attended[:, 64 * g : 64 * g + 64] for g in range(6)]
+    for g in range(6):
+        here = slice(64 * g, 64 * g + 64)
+        scores[g] = product(queried[g], keys[:, here], NT)
+        backs[g] = product(returned[g], values[:, here], NT)
+    for g in range(6):
+        head = 6 * group + g
+        weighting = jnp.where(same, jnp.exp(scores[g] - lse[:, head : head + 1]), 0.0)
+        highs[g] = weighting.astype(bf16)
+        share = backs[g] * weighting
+        inner = jnp.sum(share, axis=-1, keepdims=True)
+        lows[g] = (share - weighting * inner).astype(bf16)
     for h in range(0, 6, 2):
         pairs = ([], [], [])
         for g in (h, h + 1):
-            here = slice(64 * g, 64 * g + 64)
-            query = queries[:, here] * 0.125
-            key = keys[:, here]
-            value = values[:, here]
-            back = grad_attended[:, here]
-            scores = product(query, key, NT)
-            head = 6 * group + g
-            weighting = jnp.where(same, jnp.exp(scores - lse[:, head : head + 1]), 0.0)
-            grad_weighting = product(back, value, NT)
-            pairs[2].append(product(weighting.astype(bf16), back, TN))
-            inner = jnp.sum(grad_weighting * weighting, axis=-1, keepdims=True)
-            low = (weighting * (grad_weighting - inner)).astype(bf16)
-            pairs[0].append(product(low, key, NN) * 0.125)
-            pairs[1].append(product(low, query, TN))
+            pairs[0].append(product(lows[g], keys[:, 64 * g : 64 * g + 64], NN) * 0.125)
+            pairs[1].append(product(lows[g], queried[g], TN))
+            pairs[2].append(product(highs[g], returned[g], TN))
         for k in range(3):
             grad_packed[rows, 384 * k + 64 * h : 384 * k + 64 * h + 128] = jnp.concatenate(
                 pairs[k], axis=1
@@ -684,9 +707,9 @@
 
 
 def tokens_back_kernel(r, info, tok, back0, back1, grad_middle, bias_in, small, *rest):
-    refs, (query_own, query_other), (tokens_grad, bias, weight) = rest[:8], rest[8:10], rest[-3:]
+    refs, (tokens_grad, bias, weight) = rest[:12], rest[-3:]
     i, x = info[0], info[1]
-    load_qkv(weight, refs, query_own, query_other, i, x)
+    load_qkv(weight, refs, i, x)
     bias[...] = bias_in[...]
     for part, back in ((0, back0), (1, back1)):
         columns = slice(384 * part, 384 * part + 384)
@@ -722,12 +745,30 @@
             rows, chosen, (NN, ((), ())), precision=lax.Precision.HIGHEST, preferred_element_type=f32
         )
 
-    narrow = cut(bias[0:8, :], i * 48, 128)
+    narrow = cut(bias[...], i * 48, 128)
     for k in range(8):
         vectors[k][...] = narrow[k, 0:48]
-    wide = cut(bias[8:16, :], (i & 3) * 192, 256)
-    chosen = lax.broadcasted_iota(jnp.int32, (8, 256), 0) == (i >> 2)
-    vectors[8][...] = jnp.sum(jnp.where(chosen, wide, 0.0), axis=0)[0:192]
+    broad = jnp.concatenate([narrow[8 + k : 9 + k, 0:48] for k in range(4)], axis=1)
+    vectors[8][...] = broad[0]
+
+
+def units_results_kernel(info, mine0, other0, mine1, other1, fc1, fc2):
+    x = info[1]
+    blocks = []
+    for half in range(2):
+        for mine, other in ((mine0, other0), (mine1, other1)):
+            pieces = [
+                jnp.concatenate(
+                    [jnp.where(x == half, mine[k, p].astype(f32), other[k, p].astype(f32)) for p in range(2)],
+                    axis=1,
+                )
+                for k in range(2)
+            ]
+            fc2[48 * len(blocks) : 48 * len(blocks) + 48, :] = pieces[1]
+            blocks.append(pieces[0])
+    for j in range(0, 16, 2):
+        cuts = [b[:, 48 * k : 48 * k + 48] for k in (j, j + 1) for b in blocks]
+        fc1[:, 192 * j : 192 * j + 384] = jnp.concatenate(cuts, axis=1)
 
 
 def whole(shape):
@@ -736,10 +777,6 @@
 
 def rowwise(width):
     return pl.BlockSpec((256, width), lambda r, info: (r, 0))
-
-
-def steps(shape):
-    return pl.BlockSpec((1,) + shape, lambda t, info: (t, 0, 0))
 
 
 def run_kernel(kernel, grid, info, operands, outs, scratch, microseconds, alias=None):
@@ -795,145 +832,117 @@
         return [(None, array) for array in arrays]
 
     vectors = (ln1_gain, ln1_bias, q_bias, v_bias, proj_bias, ln2_gain, ln2_bias, fc2_bias, fc1_bias)
-    pair, ahead, up, down = run_kernel(
+    lead, units0, units1 = run_kernel(
         prepare_kernel,
         1,
-        info,
+        jnp.stack([i, x]),
         full(qkv_weight, fc1_weight, fc2_weight, *vectors),
-        [
-            (None, (2, PIECE, 384), bf16),
-            (None, (1, 64, WIDE), bf16),
-            (None, (2, PIECE, WIDE), bf16),
-            (None, (2, PIECE, WIDE), bf16),
-        ],
+        [(None, (1, 160, 384), bf16), (None, (2, PIECE, WIDE), bf16), (None, (2, PIECE, WIDE), bf16)],
         [],
         2,
     )
 
-    far = hop(pair, BIT_Z1)
-    ahead = join(ahead, hop(ahead, BIT_Y))
-    pair = jnp.stack([pair, far], axis=1)
+    proj = tie(proj_weight[None], lead)
+    proj = join(proj, hop(proj, BIT_Y))
+
+    pair = join(lead, hop(lead, BIT_Z1))
     far = hop(pair, BIT_Z0)
-    ahead_far = hop(ahead, BIT_Z1)
-    ahead = join(ahead, ahead_far)
-    line0, line1 = join(pair[0], far[0]), join(pair[1], far[1])
-    wide0 = join(line0, hop(line0, BIT_Y))
-    wide1 = join(line1, swap(line1))
-    line0, line1, up = lax.optimization_barrier((line0, line1, up))
-    got0, got1 = hop(line0, BIT_Y), swap(line1)
-    up_far = hop(up, BIT_Z1)
-    got0, got1, up_far = lax.optimization_barrier((got0, got1, up_far))
-    wide0, wide1 = join(line0, got0), join(line1, got1)
-    got0, got1, ahead_far = swap(wide0), hop(wide1, BIT_Y), hop(ahead, BIT_Z0)
-    up = jnp.stack([up, up_far], axis=1)
-    up_far = hop(up, BIT_Z0)
-    down = tie(join(down, proj_weight[None]), got0, got1)
-    ahead = join(ahead, ahead_far)
-    got0, got1, up_far = lax.optimization_barrier((got0, got1, up_far))
-    first = to_other_core((wide0, got0, wide1, got1))
-    ahead_other = hop(ahead, BIT_C)
-
-    up_line0, up_line1 = join(up[0], up_far[0]), join(up[1], up_far[1])
-    up_got0, up_got1 = hop(up_line0, BIT_Y), swap(up_line1)
-    down_far = hop(down, BIT_Z1)
-
-    vectors = jnp.concatenate([ahead[:, PIECE : PIECE + 9, :192], ahead_other[:, PIECE : PIECE + 9, :192]])
-    origin = jnp.array([(p >> 1 & 1) * 8 + (p >> 2 & 1) * 4 + (p & 1) * 2 + (p >> 3) for p in range(16)])
+    line_b, line_q, line_a = (join(pair[:, k], far[:, k]) for k in (slice(0, 48), slice(48, 96), slice(96, 160)))
+    line_a, line_b, line_q, units0 = lax.optimization_barrier((line_a, line_b, line_q, units0))
+    got_a, got_b, got_q = hop(line_a, BIT_Y), swap(line_b), hop(line_q, BIT_Y)
+    units_far = hop(units0, BIT_Z1)
+    got_a, got_b = lax.optimization_barrier((got_a, got_b))
+    wide_a, wide_b = join(line_a, got_a), join(line_b, got_b)
+    got_a, got_b = swap(wide_a[:, :PIECE]), hop(wide_b, BIT_Y)
+    wide_q = join(line_q, got_q)
+    got_q = swap(wide_q)
+    units_far = tie(units_far, wide_a, wide_b)
+    units0 = jnp.stack([units0, units_far], axis=1)
+    units_far = hop(units0, BIT_Z0)
+    units1 = tie(units1, wide_a, wide_b, units0)
+    next_far = hop(units1, BIT_Z1)
+    got_a, got_b, got_q, units_far, next_far, proj = lax.optimization_barrier(
+        (got_a, got_b, got_q, units_far, next_far, proj)
+    )
+    first = to_other_core((wide_a, got_a, wide_b, got_b, wide_q, got_q))
+
+    units_line = join(units0[0], units_far[0]), join(units0[1], units_far[1])
+    units_got = hop(units_line[0], BIT_Y), swap(units_line[1])
+    units1 = jnp.stack([units1, next_far], axis=1)
+    next_far = hop(units1, BIT_Z0)
+    proj_far = hop(proj, BIT_Z1)
+
+    vectors = jnp.concatenate([first[k][:, PIECE : PIECE + 12, :PIECE] for k in (0, 6)])
+    origin = jnp.array([(p & 1) * 8 + (p >> 1 & 1) * 4 + (p >> 2 & 1) * 2 + (p >> 3) for p in range(16)])
     turned = jnp.arange(16)[:, None] == (origin ^ i)[None, :]
     vectors = jnp.einsum("mp,pkl->kml", turned.astype(bf16), vectors, preferred_element_type=f32)
-    small = jnp.concatenate(
-        [vectors[:8, :, :48].reshape(8, WIDE), vectors[8].reshape(4, WIDE), jnp.zeros((4, WIDE), f32)]
-    )
+    small = jnp.concatenate([vectors.reshape(12, WIDE), jnp.zeros((4, WIDE), f32)])
 
     packed, normed_one = run_kernel(
         qkv_kernel,
         1,
         info,
-        full(tok, small, *first, ahead, ahead_other),
+        full(tok, small, *first),
         [(None, (count, 3 * WIDE), bf16), (None, (count, WIDE), bf16)],
         [((3, WIDE, WIDE), bf16)],
         7,
     )
 
-    up_got0, up_got1, down_far, _ = lax.optimization_barrier((up_got0, up_got1, down_far, packed))
-    up_wide0, up_wide1 = join(up_line0, up_got0), join(up_line1, up_got1)
-    up_got0, up_got1 = swap(up_wide0), hop(up_wide1, BIT_Y)
-    down = jnp.stack([down, down_far], axis=1)
-    down_far = hop(down, BIT_Z0)
+    units_got, next_far, proj_far, _ = lax.optimization_barrier((units_got, next_far, proj_far, packed))
+    units_wide = tuple(join(line, got) for line, got in zip(units_line, units_got))
+    units_got = swap(units_wide[0]), hop(units_wide[1], BIT_Y)
+    next_line = tuple(join(units1[k], next_far[k]) for k in range(2))
+    next_got = hop(next_line[0], BIT_Y), swap(next_line[1])
+    proj = join(proj, proj_far)
+    proj_far = hop(proj, BIT_Z0)
 
     attended, grad_two, lse = run_kernel(
         attend_kernel,
         2,
-        tie(info, up_wide0, up_wide1, down),
+        tie(info, *units_wide, *next_line, proj),
         [(rowwise(3 * WIDE), packed), (rowwise(WIDE), cot)],
         [
             (rowwise(WIDE), (count, WIDE), bf16),
             (rowwise(WIDE), (count, WIDE), bf16),
             (rowwise(128), (count, 128), f32),
         ],
-        [],
-        12,
-    )
-
-    up_got0, up_got1, down_far, _ = lax.optimization_barrier((up_got0, up_got1, down_far, lse))
-    up = to_other_core((up_wide0, up_got0, up_wide1, up_got1))
-    down_line0, down_line1, proj = (join(down[k], down_far[k]) for k in range(3))
-    down_got0, down_got1 = hop(down_line0, BIT_Y), swap(down_line1)
-    proj = join(proj, hop(proj, BIT_Y))
+        [((HEADS, 256, 256), f32), ((HEADS, 256, 256), bf16)],
+        10,
+    )
+
+    units_got, next_got, proj_far, _ = lax.optimization_barrier((units_got, next_got, proj_far, lse))
+    proj = join(proj, proj_far)
     proj_other = hop(proj, BIT_C)
-    down_wide0, down_wide1 = join(down_line0, down_got0), join(down_line1, down_got1)
-    down_got0, down_got1 = swap(down_wide0), hop(down_wide1, BIT_Y)
-
-    parts = (4, 8, PIECE, WIDE)
-    middle, normed_two, hidden, active, fc2_own, fc2_away = run_kernel(
-        up_kernel,
-        4,
-        tie(info, down_wide0, down_wide1),
-        full(attended, tok, grad_two, small, proj, proj_other, *up),
-        [
-            (None, (count, WIDE), f32),
-            (None, (count, WIDE), bf16),
-            (steps((count, WIDE)), (4, count, WIDE), f32),
-            (steps((count, WIDE)), (4, count, WIDE), bf16),
-            (None, parts, bf16),
-            (None, parts, bf16),
-        ],
-        [((WIDE, WIDE), bf16)] * 3,
+    units = to_other_core((units_wide[0], units_got[0], units_wide[1], units_got[1]))
+    next_wide = tuple(join(line, got) for line, got in zip(next_line, next_got))
+    next_got = swap(next_wide[0]), hop(next_wide[1], BIT_Y)
+
+    wide_f32 = (None, (count, WIDE), f32)
+    wide_bf16 = (None, (count, WIDE), bf16)
+    vectors_f32 = (None, (16, WIDE), f32)
+    parts = (None, (4, 8, 2, PIECE, 384), bf16)
+    unit_scratch = [((count, WIDE), bf16)] * 2 + [((WIDE, WIDE), bf16)] * 4
+    middle, normed_two, branch, grad_normed, bias, units_own, units_away = run_kernel(
+        first_units_kernel,
+        2,
+        tie(info, *next_wide),
+        full(attended, tok, grad_two, small, proj, proj_other, *units),
+        [wide_f32, wide_bf16, wide_f32, wide_f32, vectors_f32, parts, parts],
+        [((WIDE, WIDE), bf16)] + unit_scratch,
         16,
     )
-
-    down_got0, down_got1, _ = lax.optimization_barrier((down_got0, down_got1, normed_two))
-    down = to_other_core((down_wide0, down_got0, down_wide1, down_got1))
-    fc2_came = hop(fc2_away, BIT_C)
-    half = (2, 8, PIECE, WIDE)
-    whole_f32 = (None, (count, WIDE), f32)
-    whole_bf16 = (None, (count, WIDE), bf16)
-
-    def down_back(line, info, more, outs, scratch):
-        block = pl.BlockSpec((1, count, WIDE), lambda t, _: (2 * line + t, 0, 0))
-        return run_kernel(
-            functools.partial(down_kernel, line),
-            2,
-            info,
-            full(normed_two, grad_two)
-            + [(block, hidden), (block, active)]
-            + full(small, *up[2 * line : 2 * line + 2], *up[4 + 2 * line : 6 + 2 * line], *down, *more),
-            outs + [(None, (16, WIDE), f32), (None, half, bf16), (None, half, bf16)],
-            [((WIDE, WIDE), bf16)] * 3 + scratch,
-            13,
-        )
-
-    branch, grad_normed, bias, fc1_own0, fc1_away0 = down_back(0, info, (), [whole_f32] * 2, [])
-    fc2_came, bias = lax.optimization_barrier((fc2_came, bias))
-    two = core_sums(fc2_own, fc2_came)
+    next_got, bias, units_away = lax.optimization_barrier((next_got, bias, units_away))
+    units = to_other_core((next_wide[0], next_got[0], next_wide[1], next_got[1]))
+    two = core_sums(units_own, hop(units_away, BIT_C))
     two_got = first_hops(two)
-    one_came0 = hop(fc1_away0, BIT_C)
-    output, grad_middle, grad_one, bias, fc1_own1, fc1_away1 = down_back(
-        1,
+    output, grad_middle, grad_one, bias, units_own, units_away = run_kernel(
+        second_units_kernel,
+        2,
         tie(info, *two),
-        (branch, grad_normed, bias, middle, cot),
-        [whole_bf16, whole_f32, whole_bf16],
-        [((count, WIDE), f32)] * 2,
+        full(normed_two, grad_two, small, branch, grad_normed, bias, middle, cot, *units),
+        [wide_bf16, wide_f32, wide_bf16, vectors_f32, parts, parts],
+        [((count, WIDE), f32)] * 2 + unit_scratch,
+        18,
     )
 
     def attend_back(group, info, more, outs, scratch):
@@ -949,13 +958,16 @@
             + [(rowwise(128), lse), (rowwise(WIDE), attended), (rowwise(WIDE), grad_one)]
             + full(normed_one, *more),
             [(None, (count, 1152), bf16), (None, narrow, bf16), (None, narrow, bf16)] + outs,
-            [((2, 2, WIDE, 384), bf16)] + scratch,
+            [((2, 2, WIDE, 384), bf16)]
+            + [((6, 256, 256), f32)] * 2
+            + [((6, 256, 256), bf16)] * 2
+            + scratch,
             14,
         )
 
-    two_got, one_came0, bias = lax.optimization_barrier((two_got, one_came0, bias))
+    two_got, bias, units_away = lax.optimization_barrier((two_got, bias, units_away))
     two = first_sums(two, two_got)
-    two_got, one_came1 = second_hops(two), hop(fc1_away1, BIT_C)
+    two_got, one_came = second_hops(two), hop(units_away, BIT_C)
     back0, head_own0, head_away0, proj_full, proj_rest = attend_back(
         0,
         tie(info, *two),
@@ -964,20 +976,22 @@
         [((WIDE, WIDE), f32)],
     )
 
-    two_got, one_came1, _ = lax.optimization_barrier((two_got, one_came1, proj_rest))
+    two_got, one_came, proj_rest, head_away0 = lax.optimization_barrier(
+        (two_got, one_came, proj_rest, head_away0)
+    )
     two = second_sums(two, two_got)
-    one = tuple(
-        plus(own[k], came[k])
-        for own, came in ((fc1_own0, one_came0), (fc1_own1, one_came1))
-        for k in range(2)
-    )
+    one = core_sums(units_own, one_came)
     one_got, two_got, zero_came = first_hops(one), third_hops(two), hop(head_away0, BIT_C)
     back1, head_own1, head_away1 = attend_back(1, tie(info, *two, *one), (proj_full, proj_rest), [], [])
 
-    two_got, one_got, zero_came, _ = lax.optimization_barrier((two_got, one_got, zero_came, back1))
+    two_got, one_got, zero_came, head_away1 = lax.optimization_barrier(
+        (two_got, one_got, zero_came, head_away1)
+    )
     two, one, zero = third_sums(two, two_got), first_sums(one, one_got), core_sums(head_own0, zero_came)
     last_came = hop(head_away1, BIT_C)
-    two_got, one_got, zero_got = fourth_hops(two), second_hops(one), first_hops(zero)
+    two_got = fourth_hops(two)
+    got_x, got_y = together(swap, one[3], zero[1]), together(hop_y, one[1], zero[3])
+    one_got, zero_got = (got_y[0], got_x[0]), (got_x[1], got_y[1])
 
     def tokens_back(r, info, more, alias):
         def row(width):
@@ -988,7 +1002,7 @@
             1,
             info,
             [(row(WIDE), tok), (row(1152), back0), (row(1152), back1), (row(WIDE), grad_middle)]
-            + full(bias, small, *first, ahead, ahead_other)
+            + full(bias, small, *first)
             + more,
             [(row(WIDE), (count, WIDE), f32), (None, (16, WIDE), f32)],
             [((3, WIDE, WIDE), bf16)],
@@ -1007,9 +1021,11 @@
         second_sums(one, one_got),
         first_sums(zero, zero_got),
     )
-    last_got, one_got, zero_got, two_other = first_hops(last), third_hops(one), second_hops(zero), swap(two)
+    one_got = third_hops(one)
+    got_x, got_y = together(swap, last[1], zero[3], two), together(hop_y, last[3], zero[1])
+    last_got, zero_got, two_other = (got_x[0], got_y[0]), (got_y[1], got_x[1]), got_x[2]
     tokens_grad, bias = tokens_back(
-        1, tie(info, *last, two, *one, *zero), [(pl.BlockSpec(memory_space=pl.ANY), tokens_grad)], {17: 0}
+        1, tie(info, *last, two, *one, *zero), [(pl.BlockSpec(memory_space=pl.ANY), tokens_grad)], {19: 0}
     )
 
     last_got, one_got, zero_got, two_other, bias = lax.optimization_barrier(
@@ -1021,11 +1037,11 @@
             second_hops(last),
             fourth_hops(one),
             third_hops(zero),
-            (hop(bias, BIT_C), hop(bias, BIT_Y), hop(bias, BIT_C | BIT_Y)),
+            hop(bias, BIT_Y),
         )
     )
     last, one, zero = second_sums(last, last_got), fourth_sums(one, one_got), third_sums(zero, zero_got)
-    bias = (bias + bias_got[0]) + (bias_got[1] + bias_got[2])
+    bias = bias + bias_got
     last_got, one_other, zero_got, bias_got = lax.optimization_barrier(
         (third_hops(last), swap(one), fourth_hops(zero), hop(bias, BIT_Z0))
     )
@@ -1033,9 +1049,18 @@
     last_got, zero_other, bias_got = lax.optimization_barrier(
         (fourth_hops(last), swap(zero), hop(bias, BIT_Z1))
     )
+    fc1_grad, fc2_grad = run_kernel(
+        units_results_kernel,
+        1,
+        info,
+        full(two, two_other, one, one_other),
+        [(None, (PIECE, 4 * WIDE), f32), (None, (4 * PIECE, WIDE), f32)],
+        [],
+        3,
+    )
     last, bias = fourth_sums(last, last_got), bias + bias_got
-    last_other, bias_got = swap(last), swap(bias)
-    bias = bias + bias_got
+    last_other, bias_got = swap(last), (swap(bias), hop(bias, BIT_C), cross(bias))
+    bias = (bias + bias_got[0]) + (bias_got[1] + bias_got[2])
     qkv_grad, proj_grad, *narrow = run_kernel(
         results_kernel,
         1,
@@ -1047,8 +1072,6 @@
         [],
         3,
     )
-    fc1_grad = jnp.concatenate([place(one, one_other, x, k >> 1, k & 1) for k in range(4)], axis=1)
-    fc2_grad = jnp.concatenate([place(two, two_other, x, k >> 1, k & 1) for k in range(4)], axis=0)
     return (
         output.reshape(tokens.shape),
         tokens_grad.reshape(tokens.shape),

time: 273 us -> 255 us (0.934)
  waiting for transfers between devices: 73.2 us -> 59.1 us
  Pallas kernels: 108 us -> 95 us
  starting transfers between devices: 68.1 us -> 75.2 us
  local copies, waits for them, and re-layouts: 6.1 us -> 10.5 us
  other arithmetic: 11.5 us -> 8.01 us
    ppermute x56 -> x53, waiting for transfers between devices: 67.7 us -> 50.6 us  [hop(): return lax.ppermute(array, 'fsdp', [(i, i ^ bit) for i in range(16)])]
    ppermute x56 -> x53, starting transfers between devices: 44 us -> 58.7 us  [hop(): return lax.ppermute(array, 'fsdp', [(i, i ^ bit) for i in range(16)])]
    pallas_call x11, Pallas kernels: 108 us -> 95 us  [run_kernel(): pl.pallas_call(kernel, grid_spec=pltpu.PrefetchScalarGridSpec(num_scalar_...]
    ppermute x19 -> x17, starting transfers between devices: 24.1 us -> 16.4 us  [swap(): return lax.ppermute(array, 'dp', [(0, 1), (1, 0)])]
    unnamed x66 -> x85, local copies, waits for them, and re-layouts: 4.8 us -> 8.32 us
    ppermute x19 -> x17, waiting for transfers between devices: 5.5 us -> 8.06 us  [swap(): return lax.ppermute(array, 'dp', [(0, 1), (1, 0)])]
  transfers between devices with their start and end apart: 75 -> 71, of which waited for: 27 -> 25; matrix products, arithmetic and copies ran while one was open for 4% -> 4% of each run, Pallas kernels for 38% -> 36%
where the time goes in v3:
time: 255 us; the launch traced here: 250 us
  Pallas kernels  95 us (37%)
  starting transfers between devices  75.2 us (29%)
  waiting for transfers between devices  59.1 us (23%)
  local copies, waits for them, and re-layouts  10.5 us (4%)
  other arithmetic  8.01 us (3%)
    pallas_call x11, Pallas kernels, run_kernel(): pl.pallas_call(kernel, grid_spec=pltpu.PrefetchScalarGridSpec(num_scalar_...  95 us
    ppermute x53, starting transfers between devices, hop(): return lax.ppermute(array, 'fsdp', [(i, i ^ bit) for i in range(16)])  58.7 us
    ppermute x53, waiting for transfers between devices, hop(): return lax.ppermute(array, 'fsdp', [(i, i ^ bit) for i in range(16)])  50.6 us
    ppermute x17, starting transfers between devices, swap(): return lax.ppermute(array, 'dp', [(0, 1), (1, 0)])  16.4 us
    unnamed x85, local copies, waits for them, and re-layouts  8.32 us
    ppermute x17, waiting for transfers between devices, swap(): return lax.ppermute(array, 'dp', [(0, 1), (1, 0)])  8.06 us
  transfers between devices with their start and end apart: 71, of which 25 were waited for; matrix products, arithmetic and copies ran while one was open for 4% of the time, Pallas kernels for 36%

profile of v3, /device:TPU:0, one launch (start us, length us, event | category | flops | bytes accessed | tf_op | source)
XLA Modules:
  0.0 250.0 jit_solution(16334005675039274542)
XLA Ops:
  1.2 3.0 %shard_map.289 = (bf16[1,160,384]{2,1,0:T(8,128)(2,1)}, bf16[2,48,768]{2,1,0:T(8,128)(2,1)}, bf16[2,48,768]{2,1,0:T(8,128)(2,1)}) custom-call(s32[2]{0:T(128)} %pad_add_fusion.1.info, bf16[48,2304]{1,0:T(8,128)(2,1)} %qkv.1, bf16[48,3072]{1,0:T(8,128)(2,1)} %fc1.1, bf16[192,768]{1,0:T(8,128)(2,1)} %fc2.1, bf16[48]{0:T(256)(128)(2,1)} %rest_0_.1, ...), custom_call_target="tpu_custom_call" | custom-call | flops 2300000000 | bytes 1048576 | tf_op jit(solution)/shard_map/pallas_call | solution.py:783
  4.3 4.0 %collective-permute-start = (bf16[1,160,384]{2,1,0:T(8,128)(2,1)}, bf16[1,160,384]{2,1,0:T(8,128)(2,1)S(1)}, u32[]{:S(2)}, u32[]{:S(2)}) collective-permute-start(bf16[1,160,384]{2,1,0:T(8,128)(2,1)} %get-tuple-element.137), channel_id=1, source_target_pairs={{0,8},{1,9},{2,10},{3,11},{4,12},{5,13},{6,14},{7,15},{8,0},{9,1},... | collective-permute-start | bytes 368648 | tf_op jit(solution)/shard_map/ppermute | solution.py:307
  8.3 1.5 collective-permute-start.11
  10.8 3.7 %collective-permute-done = bf16[1,160,384]{2,1,0:T(8,128)(2,1)S(1)} collective-permute-done((bf16[1,160,384]{2,1,0:T(8,128)(2,1)}, bf16[1,160,384]{2,1,0:T(8,128)(2,1)S(1)}, u32[]{:S(2)}, u32[]{:S(2)}) %collective-permute-start) | collective-permute-done | bytes 122912 | tf_op jit(solution)/shard_map/ppermute | solution.py:307
  15.7 6.0 %collective-permute-done.1 = bf16[2,160,384]{2,1,0:T(8,128)(2,1)S(1)} collective-permute-done((bf16[2,160,384]{2,1,0:T(8,128)(2,1)S(1)}, bf16[2,160,384]{2,1,0:T(8,128)(2,1)S(1)}, u32[]{:S(2)}, u32[]{:S(2)}) %collective-permute-start.1) | collective-permute-done | bytes 245792 | tf_op jit(solution)/shard_map/ppermute | solution.py:307
  21.9 1.4 collective-permute-start.2
  23.3 1.6 collective-permute-start.3
  25.4 3.3 %collective-permute-start.4 = (bf16[2,48,768]{2,1,0:T(8,128)(2,1)S(1)}, bf16[2,48,768]{2,1,0:T(8,128)(2,1)S(1)}, u32[]{:S(2)}, u32[]{:S(2)}) collective-permute-start(bf16[2,48,768]{2,1,0:T(8,128)(2,1)S(1)} %copy-done.10), channel_id=1, source_target_pairs={{0,8},{1,9},{2,10},{3,11},{4,12},{5,13},{6,14},{7,15},{8,0},{9,1},... | collective-permute-start | bytes 442376 | tf_op jit(solution)/shard_map/ppermute | solution.py:307
  28.8 1.8 collective-permute-done.7
  31.8 1.6 collective-permute-start.6
  35.1 1.5 collective-permute-start.9
  37.3 3.3 %collective-permute-start.10 = (bf16[2,48,768]{2,1,0:T(8,128)(2,1)S(1)}, bf16[2,48,768]{2,1,0:T(8,128)(2,1)S(1)}, u32[]{:S(2)}, u32[]{:S(2)}) collective-permute-start(bf16[2,48,768]{2,1,0:T(8,128)(2,1)S(1)} %copy-done.9), channel_id=1, source_target_pairs={{0,8},{1,9},{2,10},{3,11},{4,12},{5,13},{6,14},{7,15},{8,0},{9,1},... | collective-permute-start | bytes 442376 | tf_op jit(solution)/shard_map/ppermute | solution.py:307
  40.6 4.5 %collective-permute-done.10 = bf16[2,48,768]{2,1,0:T(8,128)(2,1)S(1)} collective-permute-done((bf16[2,48,768]{2,1,0:T(8,128)(2,1)S(1)}, bf16[2,48,768]{2,1,0:T(8,128)(2,1)S(1)}, u32[]{:S(2)}, u32[]{:S(2)}) %collective-permute-start.10) | collective-permute-done | bytes 147488 | tf_op jit(solution)/shard_map/ppermute | solution.py:307
  49.3 3.3 %collective-permute-start.15 = (bf16[2,48,768]{2,1,0:T(8,128)(2,1)S(1)}, bf16[2,48,768]{2,1,0:T(8,128)(2,1)S(1)}, u32[]{:S(2)}, u32[]{:S(2)}) collective-permute-start(bf16[2,48,768]{2,1,0:T(8,128)(2,1)S(1)} %pad_maximum_fusion.21), channel_id=1, source_target_pairs={{0,8},{1,9},{2,10},{3,11},{4,12},{5,13},{6,14},{7,15},{8,0},{9,1},... | collective-permute-start | bytes 442376 | tf_op jit(solution)/shard_map/ppermute | solution.py:307
  53.5 1.5 collective-permute-start.13
  55.0 1.4 collective-permute-start.14
  56.3 6.8 %shard_map.290 = (bf16[512,2304]{1,0:T(8,128)(2,1)}, bf16[512,768]{1,0:T(8,128)(2,1)}) custom-call(s32[20]{0:T(128)} %pad_add_fusion.info, bf16[512,768]{1,0:T(8,128)(2,1)} %bitcast.222, f32[16,768]{1,0:T(8,128)} %concatenate.92.small, bf16[8,64,384]{2,1,0:T(8,128)(2,1)} %copy-done.3, bf16[8,48,384]{2,1,0:T(8,128)(2,1)} %collective-permute-done.5.rest_1_, ...), custom_call_target="tpu_custom_call" | custom-call | flops 8049999872 | bytes 1048576 | tf_op jit(solution)/shard_map/pallas_call | solution.py:783
  65.8 1.9 collective-permute-start.26
  69.4 8.0 %shard_map.291 = (bf16[512,768]{1,0:T(8,128)(2,1)}, bf16[512,768]{1,0:T(8,128)(2,1)}, f32[512,128]{1,0:T(8,128)}) custom-call(s32[20]{0:T(128)} %pad_add_fusion.info, bf16[512,2304]{1,0:T(8,128)(2,1)} %get-tuple-element.154.packed.queries.keys.values, bf16[512,768]{1,0:T(8,128)(2,1)} %bitcast.220), custom_call_target="tpu_custom_call" | custom-call | flops 11500000256 | bytes 1048576 | tf_op jit(solution)/shard_map/pallas_call | solution.py:783
  78.0 6.4 %collective-permute-done.23.rest_3_ = bf16[8,48,768]{2,1,0:T(8,128)(2,1)S(1)} collective-permute-done((bf16[8,48,768]{2,1,0:T(8,128)(2,1)S(1)}, bf16[8,48,768]{2,1,0:T(8,128)(2,1)S(1)}, u32[]{:S(2)}, u32[]{:S(2)}) %collective-permute-start.23) | collective-permute-done | bytes 589856 | tf_op jit(solution)/shard_map/ppermute | solution.py:307
  85.6 1.6 collective-permute-start.33
  89.8 16.2 %shard_map.292 = (f32[512,768]{1,0:T(8,128)}, bf16[512,768]{1,0:T(8,128)(2,1)}, f32[512,768]{1,0:T(8,128)}, f32[512,768]{1,0:T(8,128)}, f32[16,768]{1,0:T(8,128)...) custom-call(s32[20]{0:T(128)} %pad_add_fusion.info, ...), custom_call_target="tpu_custom_call" | custom-call | flops 18400000000 | bytes 1048576 | tf_op jit(solution)/shard_map/pallas_call | solution.py:783
  107.3 5.6 %collective-permute-done.34 = bf16[4,8,2,48,384]{4,3,2,1,0:T(8,128)(2,1)S(1)} collective-permute-done((bf16[4,8,2,48,384]{4,3,2,1,0:T(8,128)(2,1)}, bf16[4,8,2,48,384]{4,3,2,1,0:T(8,128)(2,1)S(1)}, u32[]{:S(2)}, u32[]{:S(2)}) %collective-permute-start.34) | collective-permute-done | bytes 2359328 | tf_op jit(solution)/shard_map/ppermute | solution.py:307
  112.9 2.2 add_convert_fusion.4
  115.1 1.5 collective-permute-start.40
  119.3 19.1 %shard_map.293 = (bf16[512,768]{1,0:T(8,128)(2,1)}, f32[512,768]{1,0:T(8,128)}, bf16[512,768]{1,0:T(8,128)(2,1)}, f32[16,768]{1,0:T(8,128)}, bf16[4,8,2,48,384]{...) custom-call(s32[20]{0:T(128)} %pad_add_fusion.info, bf16[512,768]{1,0:T(8,128)(2,1)} %get-tuple-element.174.normed, ...), custom_call_target="tpu_custom_call" | custom-call | flops 20700000256 | bytes 1048576 | tf_op jit(solution)/shard_map/pallas_call | solution.py:783
  140.6 12.5 %shard_map.294 = (bf16[512,1152]{1,0:T(8,128)(2,1)}, bf16[4,8,48,384]{3,2,1,0:T(8,128)(2,1)}, bf16[4,8,48,384]{3,2,1,0:T(8,128)(2,1)}, bf16[768,768]{1,0:T(8,128)(2,1)}, bf16[768,384]{1,0:T(8,128)(2,1)}) custom-call(s32[20]{0:T(128)} %pad_add_fusion.info, bf16[512,2304]{1,0:T(8,128)(2,1)} %get-tuple-element.154.packed.queries.keys.values, ...), custom_call_target="tpu_custom_call" | custom-call | flops 16099999744 | bytes 1048576 | tf_op jit(solution)/shard_map/pallas_call | solution.py:783
  153.4 1.4 copy-done
  155.4 1.5 collective-permute-start.46
  157.9 2.2 collective-permute-start.44
  160.2 11.2 %shard_map.295 = (bf16[512,1152]{1,0:T(8,128)(2,1)}, bf16[4,8,48,384]{3,2,1,0:T(8,128)(2,1)}, bf16[4,8,48,384]{3,2,1,0:T(8,128)(2,1)}) custom-call(s32[20]{0:T(128)} %pad_add_fusion.info, bf16[512,2304]{1,0:T(8,128)(2,1)} %get-tuple-element.154.packed.queries.keys.values, bf16[512,2304]{1,0:T(8,128)(2,1)} %get-tuple-element.154.packed.queries.keys.values, ...), custom_call_target="tpu_custom_call" | custom-call | flops 16099999744 | bytes 1048576 | tf_op jit(solution)/shard_map/pallas_call | solution.py:783
  171.9 5.0 %collective-permute-start.48 = (bf16[2,2,48,384]{3,2,1,0:T(8,128)(2,1)S(1)}, bf16[2,2,48,384]{3,2,1,0:T(8,128)(2,1)S(1)}, u32[]{:S(2)}, u32[]{:S(2)}) collective-permute-start(bf16[2,2,48,384]{3,2,1,0:T(8,128)(2,1)S(1)} %get-tuple-element.296), channel_id=1, source_target_pairs={{0,8},{1,9},{2,10},{3,11},{4,12},{5,13},{6,14},{7,15},{8,0},{9,1},... | collective-permute-start | bytes 442376 | tf_op jit(solution)/shard_map/ppermute | solution.py:307
  179.7 6.1 %shard_map.296 = (f32[512,768]{1,0:T(8,128)}, f32[16,768]{1,0:T(8,128)}) custom-call(s32[20]{0:T(128)} %pad_add_fusion.info, bf16[512,768]{1,0:T(8,128)(2,1)} %bitcast.224, bf16[512,1152]{1,0:T(8,128)(2,1)} %get-tuple-element.209.back0, bf16[512,1152]{1,0:T(8,128)(2,1)} %get-tuple-element.210.back1, f32[512,768]{1,0:T(8,128)} %get-tuple-element.211.grad_middle, ...), custom_call_target="tpu_custom_call" | custom-call | flops 6899999744 | bytes 1048576 | tf_op jit(solution)/shard_map/pallas_call | solution.py:783
  185.8 7.7 %collective-permute-done.49 = bf16[16,48,384]{2,1,0:T(8,128)(2,1)S(1)} collective-permute-done((bf16[16,48,384]{2,1,0:T(8,128)(2,1)S(1)}, bf16[16,48,384]{2,1,0:T(8,128)(2,1)S(1)}, u32[]{:S(2)}, u32[]{:S(2)}) %collective-permute-start.49) | collective-permute-done | bytes 589856 | tf_op jit(solution)/shard_map/ppermute | solution.py:307
  196.2 2.5 collective-permute-start.54
  200.2 6.1 %shard_map.297 = (f32[512,768]{1,0:T(8,128)}, f32[16,768]{1,0:T(8,128)}) custom-call(s32[20]{0:T(128)} %pad_add_fusion.info, bf16[512,768]{1,0:T(8,128)(2,1)} %bitcast.225, bf16[512,1152]{1,0:T(8,128)(2,1)} %get-tuple-element.209.back0, bf16[512,1152]{1,0:T(8,128)(2,1)} %get-tuple-element.210.back1, ...), custom_call_target="tpu_custom_call", output_to_operand_aliasing={{0}: (19, {})} | custom-call | flops 6899999744 | bytes 1048576 | tf_op jit(solution)/shard_map/pallas_call | solution.py:783
  206.3 3.5 %collective-permute-done.53 = bf16[12,48,384]{2,1,0:T(8,128)(2,1)S(1)} collective-permute-done((bf16[12,48,384]{2,1,0:T(8,128)(2,1)S(1)}, bf16[12,48,384]{2,1,0:T(8,128)(2,1)S(1)}, u32[]{:S(2)}, u32[]{:S(2)}) %collective-permute-start.53) | collective-permute-done | bytes 442400 | tf_op jit(solution)/shard_map/ppermute | solution.py:307
  209.9 4.1 %collective-permute-done.52 = bf16[16,48,384]{2,1,0:T(8,128)(2,1)S(1)} collective-permute-done((bf16[16,48,384]{2,1,0:T(8,128)(2,1)S(1)}, bf16[16,48,384]{2,1,0:T(8,128)(2,1)S(1)}, u32[]{:S(2)}, u32[]{:S(2)}) %collective-permute-start.52) | collective-permute-done | bytes 589856 | tf_op jit(solution)/shard_map/ppermute | solution.py:311
  215.6 1.4 collective-permute-start.55
  218.2 3.4 %collective-permute-done.59 = f32[16,768]{1,0:T(8,128)S(1)} collective-permute-done((f32[16,768]{1,0:T(8,128)S(1)}, f32[16,768]{1,0:T(8,128)S(1)}, u32[]{:S(2)}, u32[]{:S(2)}) %collective-permute-start.59) | collective-permute-done | bytes 49184 | tf_op jit(solution)/shard_map/ppermute | solution.py:307
  221.6 1.2 collective-permute-done.57
  223.8 1.2 collective-permute-start.61
  225.1 2.6 %collective-permute-start.62 = (bf16[2,48,384]{2,1,0:T(8,128)(2,1)S(1)}, bf16[2,48,384]{2,1,0:T(8,128)(2,1)S(1)}, u32[]{:S(2)}, u32[]{:S(2)}) collective-permute-start(bf16[2,48,384]{2,1,0:T(8,128)(2,1)S(1)} %fusion.63), channel_id=1, source_target_pairs={{0,8},{1,9},{2,10},{3,11},{4,12},{5,13},{6,14},{7,15},{8,0},{9,1},... | collective-permute-start | bytes 221192 | tf_op jit(solution)/shard_map/ppermute | solution.py:307
  228.7 3.1 %collective-permute-done.63 = f32[16,768]{1,0:T(8,128)S(1)} collective-permute-done((f32[16,768]{1,0:T(8,128)S(1)}, f32[16,768]{1,0:T(8,128)S(1)}, u32[]{:S(2)}, u32[]{:S(2)}) %collective-permute-start.63) | collective-permute-done | bytes 49184 | tf_op jit(solution)/shard_map/ppermute | solution.py:307
  231.9 2.1 collective-permute-start.66
  235.8 3.1 %shard_map.299 = (f32[48,3072]{1,0:T(8,128)}, f32[192,768]{1,0:T(8,128)}) custom-call(s32[20]{0:T(128)} %pad_add_fusion.info, bf16[2,2,48,384]{3,2,1,0:T(8,128)(2,1)} %copy-done.4, bf16[2,2,48,384]{3,2,1,0:T(8,128)(2,1)} %bitcast.217, bf16[2,2,48,384]{3,2,1,0:T(8,128)(2,1)} %copy-done.11, bf16[2,2,48,384]{3,2,1,0:T(8,128)(2,1)} %copy-done.34), custom_call_target="tpu_custom_call" | custom-call | flops 3449999872 | bytes 1048576 | tf_op jit(solution)/shard_map/pallas_call | solution.py:783
  243.0 2.0 collective-permute-done.68
  246.7 2.8 %shard_map.298 = (f32[48,2304]{1,0:T(8,128)}, f32[48,768]{1,0:T(8,128)}, f32[48]{0:T(128)}, f32[48]{0:T(128)}, f32[48]{0:T(128)}, /*index=5*/f32[48]{0:T(128)}, ...) custom-call(s32[20]{0:T(128)} %pad_add_fusion.info, bf16[2,48,384]{2,1,0:T(8,128)(2,1)} %copy-done.15, ...), custom_call_target="tpu_custom_call" | custom-call | flops 3449999872 | bytes 1048576 | tf_op jit(solution)/shard_map/pallas_call | solution.py:783
  (277 shorter events, 48.4 us)
Async XLA Ops:
  4.3 10.2 %collective-permute-start = (bf16[1,160,384]{2,1,0:T(8,128)(2,1)}, bf16[1,160,384]{2,1,0:T(8,128)(2,1)S(1)}, u32[]{:S(2)}, u32[]{:S(2)}) collective-permute-start(bf16[1,160,384]{2,1,0:T(8,128)(2,1)} %get-tuple-element.137), channel_id=1, source_target_pairs={{0,8},{1,9},{2,10},{3,11},{4,12},{5,13},{6,14},{7,15},{8,0},{9,1},... | collective-permute-start | bytes 368648 | tf_op jit(solution)/shard_map/ppermute | solution.py:307
  8.3 28.9 %collective-permute-start.11 = (bf16[1,48,768]{2,1,0:T(8,128)(2,1)S(1)}, bf16[1,48,768]{2,1,0:T(8,128)(2,1)S(1)}, u32[]{:S(2)}, u32[]{:S(2)}) collective-permute-start(bf16[1,48,768]{2,1,0:T(8,128)(2,1)S(1)} %bitcast.218), channel_id=1, source_target_pairs={{0,2},{1,3},{2,0},{3,1},{4,6},{5,7},{6,4},{7,5},{8,10},{9,11},{10,... | collective-permute-start | bytes 221192 | tf_op jit(solution)/shard_map/ppermute | solution.py:307
  21.9 9.9 %collective-permute-start.2 = (bf16[4,64,384]{2,1,0:T(8,128)(2,1)S(1)}, bf16[4,64,384]{2,1,0:T(8,128)(2,1)S(1)}, u32[]{:S(2)}, u32[]{:S(2)}) collective-permute-start(bf16[4,64,384]{2,1,0:T(8,128)(2,1)S(1)} %pad_maximum_fusion.18), channel_id=1, source_target_pairs={{0,2},{1,3},{2,0},{3,1},{4,6},{5,7},{6,4},{7,5},{8,10},{9,11},{10,... | collective-permute-start | bytes 589832 | tf_op jit(solution)/shard_map/ppermute | solution.py:307
  23.3 8.5 %collective-permute-start.3 = (bf16[4,48,384]{2,1,0:T(8,128)(2,1)S(1)}, bf16[4,48,384]{2,1,0:T(8,128)(2,1)S(1)}, u32[]{:S(2)}, u32[]{:S(2)}) collective-permute-start(bf16[4,48,384]{2,1,0:T(8,128)(2,1)S(1)} %get-tuple-element.140), channel_id=1, source_target_pairs={{0,16},{16,0},{1,17},{17,1},{2,18},{18,2},{3,19},{19,3},{4,20},{20... | collective-permute-start | bytes 442376 | tf_op jit(solution)/shard_map/ppermute | solution.py:311
  25.4 9.2 %collective-permute-start.4 = (bf16[2,48,768]{2,1,0:T(8,128)(2,1)S(1)}, bf16[2,48,768]{2,1,0:T(8,128)(2,1)S(1)}, u32[]{:S(2)}, u32[]{:S(2)}) collective-permute-start(bf16[2,48,768]{2,1,0:T(8,128)(2,1)S(1)} %copy-done.10), channel_id=1, source_target_pairs={{0,8},{1,9},{2,10},{3,11},{4,12},{5,13},{6,14},{7,15},{8,0},{9,1},... | collective-permute-start | bytes 442376 | tf_op jit(solution)/shard_map/ppermute | solution.py:307
  30.6 14.5 %collective-permute-start.8 = (bf16[8,48,384]{2,1,0:T(8,128)(2,1)S(1)}, bf16[8,48,384]{2,1,0:T(8,128)(2,1)}, u32[]{:S(2)}, u32[]{:S(2)}) collective-permute-start(bf16[8,48,384]{2,1,0:T(8,128)(2,1)S(1)} %constant_dynamic-update-slice_fusion.6.rest_4_), channel_id=1, source_target_pairs={{0,16},{16,0},{1,17},{17,1},{2,18},{18,2},{3,19},{19,3},{4,20},{20... | collective-permute-start | bytes 884744 | tf_op jit(solution)/shard_map/ppermute | solution.py:311
  31.8 13.9 %collective-permute-start.6 = (bf16[8,48,384]{2,1,0:T(8,128)(2,1)S(1)}, bf16[8,48,384]{2,1,0:T(8,128)(2,1)}, u32[]{:S(2)}, u32[]{:S(2)}) collective-permute-start(bf16[8,48,384]{2,1,0:T(8,128)(2,1)S(1)} %constant_dynamic-update-slice_fusion.4.rest_2_), channel_id=1, source_target_pairs={{0,2},{1,3},{2,0},{3,1},{4,6},{5,7},{6,4},{7,5},{8,10},{9,11},{10,... | collective-permute-start | bytes 884744 | tf_op jit(solution)/shard_map/ppermute | solution.py:307
  34.6 11.2 %collective-permute-start.5 = (bf16[8,48,384]{2,1,0:T(8,128)(2,1)S(1)}, bf16[8,48,384]{2,1,0:T(8,128)(2,1)}, u32[]{:S(2)}, u32[]{:S(2)}) collective-permute-start(bf16[8,48,384]{2,1,0:T(8,128)(2,1)S(1)} %slice.574), channel_id=1, source_target_pairs={{0,16},{16,0},{1,17},{17,1},{2,18},{18,2},{3,19},{19,3},{4,20},{20... | collective-permute-start | bytes 884744 | tf_op jit(solution)/shard_map/ppermute | solution.py:311
  35.1 10.9 %collective-permute-start.9 = (bf16[2,2,48,768]{3,2,1,0:T(8,128)(2,1)S(1)}, bf16[2,2,48,768]{3,2,1,0:T(8,128)(2,1)S(1)}, u32[]{:S(2)}, u32[]{:S(2)}) collective-permute-start(bf16[2,2,48,768]{3,2,1,0:T(8,128)(2,1)S(1)} %pad_maximum_fusion.8), channel_id=1, source_target_pairs={{0,4},{1,5},{2,6},{3,7},{4,0},{5,1},{6,2},{7,3},{8,12},{9,13},{10,... | collective-permute-start | bytes 884744 | tf_op jit(solution)/shard_map/ppermute | solution.py:307
  37.3 7.9 %collective-permute-start.10 = (bf16[2,48,768]{2,1,0:T(8,128)(2,1)S(1)}, bf16[2,48,768]{2,1,0:T(8,128)(2,1)S(1)}, u32[]{:S(2)}, u32[]{:S(2)}) collective-permute-start(bf16[2,48,768]{2,1,0:T(8,128)(2,1)S(1)} %copy-done.9), channel_id=1, source_target_pairs={{0,8},{1,9},{2,10},{3,11},{4,12},{5,13},{6,14},{7,15},{8,0},{9,1},... | collective-permute-start | bytes 442376 | tf_op jit(solution)/shard_map/ppermute | solution.py:307
  46.4 8.6 %collective-permute-start.19 = (bf16[8,48,384]{2,1,0:T(8,128)(2,1)}, bf16[8,48,384]{2,1,0:T(8,128)(2,1)}, u32[]{:S(2)}, u32[]{:S(2)}) collective-permute-start(bf16[8,48,384]{2,1,0:T(8,128)(2,1)} %collective-permute-done.6.rest_3_), channel_id=1, source_target_pairs={{0,1},{1,0},{2,3},{3,2},{4,5},{5,4},{6,7},{7,6},{8,9},{9,8},{10,11... | collective-permute-start | bytes 884744 | tf_op jit(solution)/shard_map/ppermute | solution.py:307
  47.7 8.6 %collective-permute-start.21 = (bf16[8,48,384]{2,1,0:T(8,128)(2,1)}, bf16[8,48,384]{2,1,0:T(8,128)(2,1)}, u32[]{:S(2)}, u32[]{:S(2)}) collective-permute-start(bf16[8,48,384]{2,1,0:T(8,128)(2,1)} %collective-permute-done.8.rest_5_), channel_id=1, source_target_pairs={{0,1},{1,0},{2,3},{3,2},{4,5},{5,4},{6,7},{7,6},{8,9},{9,8},{10,11... | collective-permute-start | bytes 884744 | tf_op jit(solution)/shard_map/ppermute | solution.py:307
  49.3 13.8 %collective-permute-start.15 = (bf16[2,48,768]{2,1,0:T(8,128)(2,1)S(1)}, bf16[2,48,768]{2,1,0:T(8,128)(2,1)S(1)}, u32[]{:S(2)}, u32[]{:S(2)}) collective-permute-start(bf16[2,48,768]{2,1,0:T(8,128)(2,1)S(1)} %pad_maximum_fusion.21), channel_id=1, source_target_pairs={{0,8},{1,9},{2,10},{3,11},{4,12},{5,13},{6,14},{7,15},{8,0},{9,1},... | collective-permute-start | bytes 442376 | tf_op jit(solution)/shard_map/ppermute | solution.py:307
  52.6 10.5 %collective-permute-start.12 = (bf16[4,48,768]{2,1,0:T(8,128)(2,1)S(1)}, bf16[4,48,768]{2,1,0:T(8,128)(2,1)S(1)}, u32[]{:S(2)}, u32[]{:S(2)}) collective-permute-start(bf16[4,48,768]{2,1,0:T(8,128)(2,1)S(1)} %pad_maximum_fusion.12), channel_id=1, source_target_pairs={{0,2},{1,3},{2,0},{3,1},{4,6},{5,7},{6,4},{7,5},{8,10},{9,11},{10,... | collective-permute-start | bytes 884744 | tf_op jit(solution)/shard_map/ppermute | solution.py:307
  53.5 9.7 %collective-permute-start.13 = (bf16[4,48,768]{2,1,0:T(8,128)(2,1)S(1)}, bf16[4,48,768]{2,1,0:T(8,128)(2,1)S(1)}, u32[]{:S(2)}, u32[]{:S(2)}) collective-permute-start(bf16[4,48,768]{2,1,0:T(8,128)(2,1)S(1)} %pad_maximum_fusion.13), channel_id=1, source_target_pairs={{0,16},{16,0},{1,17},{17,1},{2,18},{18,2},{3,19},{19,3},{4,20},{20... | collective-permute-start | bytes 884744 | tf_op jit(solution)/shard_map/ppermute | solution.py:311
  55.0 8.5 %collective-permute-start.14 = (bf16[2,2,48,768]{3,2,1,0:T(8,128)(2,1)S(1)}, bf16[2,2,48,768]{3,2,1,0:T(8,128)(2,1)S(1)}, u32[]{:S(2)}, u32[]{:S(2)}) collective-permute-start(bf16[2,2,48,768]{3,2,1,0:T(8,128)(2,1)S(1)} %pad_maximum_fusion.9), channel_id=1, source_target_pairs={{0,4},{1,5},{2,6},{3,7},{4,0},{5,1},{6,2},{7,3},{8,12},{9,13},{10,... | collective-permute-start | bytes 884744 | tf_op jit(solution)/shard_map/ppermute | solution.py:307
  63.7 13.6 %collective-permute-start.24 = (bf16[4,48,768]{2,1,0:T(8,128)(2,1)S(1)}, bf16[4,48,768]{2,1,0:T(8,128)(2,1)S(1)}, u32[]{:S(2)}, u32[]{:S(2)}) collective-permute-start(bf16[4,48,768]{2,1,0:T(8,128)(2,1)S(1)} %pad_maximum_fusion.14), channel_id=1, source_target_pairs={{0,2},{1,3},{2,0},{3,1},{4,6},{5,7},{6,4},{7,5},{8,10},{9,11},{10,... | collective-permute-start | bytes 884744 | tf_op jit(solution)/shard_map/ppermute | solution.py:307
  64.7 12.8 %collective-permute-start.25 = (bf16[4,48,768]{2,1,0:T(8,128)(2,1)S(1)}, bf16[4,48,768]{2,1,0:T(8,128)(2,1)S(1)}, u32[]{:S(2)}, u32[]{:S(2)}) collective-permute-start(bf16[4,48,768]{2,1,0:T(8,128)(2,1)S(1)} %pad_maximum_fusion.15), channel_id=1, source_target_pairs={{0,16},{16,0},{1,17},{17,1},{2,18},{18,2},{3,19},{19,3},{4,20},{20... | collective-permute-start | bytes 884744 | tf_op jit(solution)/shard_map/ppermute | solution.py:311
  65.8 12.1 %collective-permute-start.26 = (bf16[4,48,768]{2,1,0:T(8,128)(2,1)S(1)}, bf16[4,48,768]{2,1,0:T(8,128)(2,1)S(1)}, u32[]{:S(2)}, u32[]{:S(2)}) collective-permute-start(bf16[4,48,768]{2,1,0:T(8,128)(2,1)S(1)} %get-tuple-element.326), channel_id=1, source_target_pairs={{0,4},{1,5},{2,6},{3,7},{4,0},{5,1},{6,2},{7,3},{8,12},{9,13},{10,... | collective-permute-start | bytes 884744 | tf_op jit(solution)/shard_map/ppermute | solution.py:307
  67.7 16.6 %collective-permute-start.23 = (bf16[8,48,768]{2,1,0:T(8,128)(2,1)S(1)}, bf16[8,48,768]{2,1,0:T(8,128)(2,1)S(1)}, u32[]{:S(2)}, u32[]{:S(2)}) collective-permute-start(bf16[8,48,768]{2,1,0:T(8,128)(2,1)S(1)} %pad_maximum_fusion.1.rest_2_), channel_id=1, source_target_pairs={{0,2},{1,3},{2,0},{3,1},{4,6},{5,7},{6,4},{7,5},{8,10},{9,11},{10,... | collective-permute-start | bytes 1769480 | tf_op jit(solution)/shard_map/ppermute | solution.py:307
  68.8 15.9 %collective-permute-start.22 = (bf16[8,48,768]{2,1,0:T(8,128)(2,1)S(1)}, bf16[8,48,768]{2,1,0:T(8,128)(2,1)}, u32[]{:S(2)}, u32[]{:S(2)}) collective-permute-start(bf16[8,48,768]{2,1,0:T(8,128)(2,1)S(1)} %pad_maximum_fusion.rest_0_), channel_id=1, source_target_pairs={{0,16},{16,0},{1,17},{17,1},{2,18},{18,2},{3,19},{19,3},{4,20},{20... | collective-permute-start | bytes 1769480 | tf_op jit(solution)/shard_map/ppermute | solution.py:311
  77.4 8.2 %collective-permute-start.30 = (bf16[8,48,768]{2,1,0:T(8,128)(2,1)S(1)}, bf16[8,48,768]{2,1,0:T(8,128)(2,1)S(1)}, u32[]{:S(2)}, u32[]{:S(2)}) collective-permute-start(bf16[8,48,768]{2,1,0:T(8,128)(2,1)S(1)} %pad_maximum_fusion.1.rest_2_), channel_id=1, source_target_pairs={{0,1},{1,0},{2,3},{3,2},{4,5},{5,4},{6,7},{7,6},{8,9},{9,8},{10,11... | collective-permute-start | bytes 1769480 | tf_op jit(solution)/shard_map/ppermute | solution.py:307
  77.5 9.7 %collective-permute-start.28 = (bf16[8,48,768]{2,1,0:T(8,128)(2,1)S(1)}, bf16[8,48,768]{2,1,0:T(8,128)(2,1)S(1)}, u32[]{:S(2)}, u32[]{:S(2)}) collective-permute-start(bf16[8,48,768]{2,1,0:T(8,128)(2,1)S(1)} %pad_maximum_fusion.rest_0_), channel_id=1, source_target_pairs={{0,1},{1,0},{2,3},{3,2},{4,5},{5,4},{6,7},{7,6},{8,9},{9,8},{10,11... | collective-permute-start | bytes 1769480 | tf_op jit(solution)/shard_map/ppermute | solution.py:307
  85.6 20.4 %collective-permute-start.33 = (bf16[8,48,768]{2,1,0:T(8,128)(2,1)S(1)}, bf16[8,48,768]{2,1,0:T(8,128)(2,1)S(1)}, u32[]{:S(2)}, u32[]{:S(2)}) collective-permute-start(bf16[8,48,768]{2,1,0:T(8,128)(2,1)S(1)} %pad_maximum_fusion.3.rest_2_), channel_id=1, source_target_pairs={{0,2},{1,3},{2,0},{3,1},{4,6},{5,7},{6,4},{7,5},{8,10},{9,11},{10,... | collective-permute-start | bytes 1769480 | tf_op jit(solution)/shard_map/ppermute | solution.py:307
  87.2 18.8 %collective-permute-start.32 = (bf16[8,48,768]{2,1,0:T(8,128)(2,1)S(1)}, bf16[8,48,768]{2,1,0:T(8,128)(2,1)S(1)}, u32[]{:S(2)}, u32[]{:S(2)}) collective-permute-start(bf16[8,48,768]{2,1,0:T(8,128)(2,1)S(1)} %pad_maximum_fusion.2.rest_0_), channel_id=1, source_target_pairs={{0,16},{16,0},{1,17},{17,1},{2,18},{18,2},{3,19},{19,3},{4,20},{20... | collective-permute-start | bytes 1769480 | tf_op jit(solution)/shard_map/ppermute | solution.py:311
  106.2 10.4 %collective-permute-start.37 = (bf16[8,48,768]{2,1,0:T(8,128)(2,1)S(1)}, bf16[8,48,768]{2,1,0:T(8,128)(2,1)S(1)}, u32[]{:S(2)}, u32[]{:S(2)}) collective-permute-start(bf16[8,48,768]{2,1,0:T(8,128)(2,1)S(1)} %pad_maximum_fusion.3.rest_2_), channel_id=1, source_target_pairs={{0,1},{1,0},{2,3},{3,2},{4,5},{5,4},{6,7},{7,6},{8,9},{9,8},{10,11... | collective-permute-start | bytes 1769480 | tf_op jit(solution)/shard_map/ppermute | solution.py:307
  106.6 11.0 %collective-permute-start.35 = (bf16[8,48,768]{2,1,0:T(8,128)(2,1)S(1)}, bf16[8,48,768]{2,1,0:T(8,128)(2,1)S(1)}, u32[]{:S(2)}, u32[]{:S(2)}) collective-permute-start(bf16[8,48,768]{2,1,0:T(8,128)(2,1)S(1)} %pad_maximum_fusion.2.rest_0_), channel_id=1, source_target_pairs={{0,1},{1,0},{2,3},{3,2},{4,5},{5,4},{6,7},{7,6},{8,9},{9,8},{10,11... | collective-permute-start | bytes 1769480 | tf_op jit(solution)/shard_map/ppermute | solution.py:307
  106.7 10.9 %collective-permute-start.36 = (bf16[8,48,768]{2,1,0:T(8,128)(2,1)S(1)}, bf16[8,48,768]{2,1,0:T(8,128)(2,1)S(1)}, u32[]{:S(2)}, u32[]{:S(2)}) collective-permute-start(bf16[8,48,768]{2,1,0:T(8,128)(2,1)S(1)} %collective-permute-done.32.rest_1_), channel_id=1, source_target_pairs={{0,1},{1,0},{2,3},{3,2},{4,5},{5,4},{6,7},{7,6},{8,9},{9,8},{10,11... | collective-permute-start | bytes 1769480 | tf_op jit(solution)/shard_map/ppermute | solution.py:307
  107.1 10.5 %collective-permute-start.38 = (bf16[8,48,768]{2,1,0:T(8,128)(2,1)S(1)}, bf16[8,48,768]{2,1,0:T(8,128)(2,1)S(1)}, u32[]{:S(2)}, u32[]{:S(2)}) collective-permute-start(bf16[8,48,768]{2,1,0:T(8,128)(2,1)S(1)} %collective-permute-done.33.rest_3_), channel_id=1, source_target_pairs={{0,1},{1,0},{2,3},{3,2},{4,5},{5,4},{6,7},{7,6},{8,9},{9,8},{10,11... | collective-permute-start | bytes 1769480 | tf_op jit(solution)/shard_map/ppermute | solution.py:307
  115.1 23.3 %collective-permute-start.40 = (bf16[8,2,48,384]{3,2,1,0:T(8,128)(2,1)S(1)}, bf16[8,2,48,384]{3,2,1,0:T(8,128)(2,1)S(1)}, u32[]{:S(2)}, u32[]{:S(2)}) collective-permute-start(bf16[8,2,48,384]{3,2,1,0:T(8,128)(2,1)S(1)} %get-tuple-element.263), channel_id=1, source_target_pairs={{0,2},{1,3},{2,0},{3,1},{4,6},{5,7},{6,4},{7,5},{8,10},{9,11},{10,... | collective-permute-start | bytes 1769480 | tf_op jit(solution)/shard_map/ppermute | solution.py:307
  116.6 21.8 %collective-permute-start.39 = (bf16[8,2,48,384]{3,2,1,0:T(8,128)(2,1)S(1)}, bf16[8,2,48,384]{3,2,1,0:T(8,128)(2,1)S(1)}, u32[]{:S(2)}, u32[]{:S(2)}) collective-permute-start(bf16[8,2,48,384]{3,2,1,0:T(8,128)(2,1)S(1)} %get-tuple-element.264), channel_id=1, source_target_pairs={{0,16},{16,0},{1,17},{17,1},{2,18},{18,2},{3,19},{19,3},{4,20},{20... | collective-permute-start | bytes 1769480 | tf_op jit(solution)/shard_map/ppermute | solution.py:311
  138.5 14.6 %collective-permute-start.43 = (bf16[4,8,2,48,384]{4,3,2,1,0:T(8,128)(2,1)}, bf16[4,8,2,48,384]{4,3,2,1,0:T(8,128)(2,1)S(1)}, u32[]{:S(2)}, u32[]{:S(2)}) collective-permute-start(bf16[4,8,2,48,384]{4,3,2,1,0:T(8,128)(2,1)} %get-tuple-element.186), channel_id=1, source_target_pairs={{0,1},{1,0},{2,3},{3,2},{4,5},{5,4},{6,7},{7,6},{8,9},{9,8},{10,11... | collective-permute-start | bytes 7077896 | tf_op jit(solution)/shard_map/ppermute | solution.py:307
  138.7 14.4 %collective-permute-start.42 = (bf16[4,2,48,384]{3,2,1,0:T(8,128)(2,1)S(1)}, bf16[4,2,48,384]{3,2,1,0:T(8,128)(2,1)S(1)}, u32[]{:S(2)}, u32[]{:S(2)}) collective-permute-start(bf16[4,2,48,384]{3,2,1,0:T(8,128)(2,1)S(1)} %get-tuple-element.278), channel_id=1, source_target_pairs={{0,16},{16,0},{1,17},{17,1},{2,18},{18,2},{3,19},{19,3},{4,20},{20... | collective-permute-start | bytes 884744 | tf_op jit(solution)/shard_map/ppermute | solution.py:311
  139.9 13.1 %collective-permute-start.41 = (bf16[4,2,48,384]{3,2,1,0:T(8,128)(2,1)S(1)}, bf16[4,2,48,384]{3,2,1,0:T(8,128)(2,1)S(1)}, u32[]{:S(2)}, u32[]{:S(2)}) collective-permute-start(bf16[4,2,48,384]{3,2,1,0:T(8,128)(2,1)S(1)} %get-tuple-element.279), channel_id=1, source_target_pairs={{0,2},{1,3},{2,0},{3,1},{4,6},{5,7},{6,4},{7,5},{8,10},{9,11},{10,... | collective-permute-start | bytes 884744 | tf_op jit(solution)/shard_map/ppermute | solution.py:307
  155.4 15.9 %collective-permute-start.46 = (bf16[8,2,48,384]{3,2,1,0:T(8,128)(2,1)S(1)}, bf16[8,2,48,384]{3,2,1,0:T(8,128)(2,1)S(1)}, u32[]{:S(2)}, u32[]{:S(2)}) collective-permute-start(bf16[8,2,48,384]{3,2,1,0:T(8,128)(2,1)S(1)} %get-tuple-element.259), channel_id=1, source_target_pairs={{0,2},{1,3},{2,0},{3,1},{4,6},{5,7},{6,4},{7,5},{8,10},{9,11},{10,... | collective-permute-start | bytes 1769480 | tf_op jit(solution)/shard_map/ppermute | solution.py:307
  156.9 14.9 %collective-permute-start.45 = (bf16[8,2,48,384]{3,2,1,0:T(8,128)(2,1)S(1)}, bf16[8,2,48,384]{3,2,1,0:T(8,128)(2,1)S(1)}, u32[]{:S(2)}, u32[]{:S(2)}) collective-permute-start(bf16[8,2,48,384]{3,2,1,0:T(8,128)(2,1)S(1)} %get-tuple-element.260), channel_id=1, source_target_pairs={{0,16},{16,0},{1,17},{17,1},{2,18},{18,2},{3,19},{19,3},{4,20},{20... | collective-permute-start | bytes 1769480 | tf_op jit(solution)/shard_map/ppermute | solution.py:311
  157.9 13.5 %collective-permute-start.44 = (bf16[2,2,2,48,384]{4,3,2,0,1:T(8,128)(2,1)S(1)}, bf16[2,2,2,48,384]{4,3,2,0,1:T(8,128)(2,1)S(1)}, u32[]{:S(2)}, u32[]{:S(2)}) collective-permute-start(bf16[2,2,2,48,384]{4,3,2,0,1:T(8,128)(2,1)S(1)} %copy.48), channel_id=1, source_target_pairs={{0,4},{1,5},{2,6},{3,7},{4,0},{5,1},{6,2},{7,3},{8,12},{9,13},{10,... | collective-permute-start | bytes 884744 | tf_op jit(solution)/shard_map/ppermute | solution.py:307
  160.2 11.7 %collective-permute-start.47 = (bf16[4,8,48,384]{3,2,1,0:T(8,128)(2,1)}, bf16[4,8,48,384]{3,2,1,0:T(8,128)(2,1)S(1)}, u32[]{:S(2)}, u32[]{:S(2)}) collective-permute-start(bf16[4,8,48,384]{3,2,1,0:T(8,128)(2,1)} %get-tuple-element.200), channel_id=1, source_target_pairs={{0,1},{1,0},{2,3},{3,2},{4,5},{5,4},{6,7},{7,6},{8,9},{9,8},{10,11... | collective-permute-start | bytes 3538952 | tf_op jit(solution)/shard_map/ppermute | solution.py:307
  171.9 22.3 %collective-permute-start.48 = (bf16[2,2,48,384]{3,2,1,0:T(8,128)(2,1)S(1)}, bf16[2,2,48,384]{3,2,1,0:T(8,128)(2,1)S(1)}, u32[]{:S(2)}, u32[]{:S(2)}) collective-permute-start(bf16[2,2,48,384]{3,2,1,0:T(8,128)(2,1)S(1)} %get-tuple-element.296), channel_id=1, source_target_pairs={{0,8},{1,9},{2,10},{3,11},{4,12},{5,13},{6,14},{7,15},{8,0},{9,1},... | collective-permute-start | bytes 442376 | tf_op jit(solution)/shard_map/ppermute | solution.py:307
  176.9 17.3 %collective-permute-start.51 = (bf16[4,8,48,384]{3,2,1,0:T(8,128)(2,1)}, bf16[4,8,48,384]{3,2,1,0:T(8,128)(2,1)S(1)}, u32[]{:S(2)}, u32[]{:S(2)}) collective-permute-start(bf16[4,8,48,384]{3,2,1,0:T(8,128)(2,1)} %get-tuple-element.207), channel_id=1, source_target_pairs={{0,1},{1,0},{2,3},{3,2},{4,5},{5,4},{6,7},{7,6},{8,9},{9,8},{10,11... | collective-permute-start | bytes 3538952 | tf_op jit(solution)/shard_map/ppermute | solution.py:307
  177.7 15.8 %collective-permute-start.49 = (bf16[16,48,384]{2,1,0:T(8,128)(2,1)S(1)}, bf16[16,48,384]{2,1,0:T(8,128)(2,1)S(1)}, u32[]{:S(2)}, u32[]{:S(2)}) collective-permute-start(bf16[16,48,384]{2,1,0:T(8,128)(2,1)S(1)} %pad_maximum_fusion.4), channel_id=1, source_target_pairs={{0,2},{1,3},{2,0},{3,1},{4,6},{5,7},{6,4},{7,5},{8,10},{9,11},{10,... | collective-permute-start | bytes 1769480 | tf_op jit(solution)/shard_map/ppermute | solution.py:307
  178.7 15.5 %collective-permute-start.50 = (bf16[16,48,384]{2,1,0:T(8,128)(2,1)S(1)}, bf16[16,48,384]{2,1,0:T(8,128)(2,1)S(1)}, u32[]{:S(2)}, u32[]{:S(2)}) collective-permute-start(bf16[16,48,384]{2,1,0:T(8,128)(2,1)S(1)} %pad_maximum_fusion.5), channel_id=1, source_target_pairs={{0,16},{16,0},{1,17},{17,1},{2,18},{18,2},{3,19},{19,3},{4,20},{20... | collective-permute-start | bytes 1769480 | tf_op jit(solution)/shard_map/ppermute | solution.py:311
  196.2 18.6 %collective-permute-start.54 = (bf16[2,2,2,48,384]{4,3,2,0,1:T(8,128)(2,1)S(1)}, bf16[2,2,2,48,384]{4,3,2,0,1:T(8,128)(2,1)S(1)}, u32[]{:S(2)}, u32[]{:S(2)}) collective-permute-start(bf16[2,2,2,48,384]{4,3,2,0,1:T(8,128)(2,1)S(1)} %copy.50), channel_id=1, source_target_pairs={{0,4},{1,5},{2,6},{3,7},{4,0},{5,1},{6,2},{7,3},{8,12},{9,13},{10,... | collective-permute-start | bytes 884744 | tf_op jit(solution)/shard_map/ppermute | solution.py:307
  198.6 11.2 %collective-permute-start.53 = (bf16[12,48,384]{2,1,0:T(8,128)(2,1)S(1)}, bf16[12,48,384]{2,1,0:T(8,128)(2,1)S(1)}, u32[]{:S(2)}, u32[]{:S(2)}) collective-permute-start(bf16[12,48,384]{2,1,0:T(8,128)(2,1)S(1)} %pad_maximum_fusion.7), channel_id=1, source_target_pairs={{0,2},{1,3},{2,0},{3,1},{4,6},{5,7},{6,4},{7,5},{8,10},{9,11},{10,... | collective-permute-start | bytes 1327112 | tf_op jit(solution)/shard_map/ppermute | solution.py:307
  199.9 14.1 %collective-permute-start.52 = (bf16[16,48,384]{2,1,0:T(8,128)(2,1)S(1)}, bf16[16,48,384]{2,1,0:T(8,128)(2,1)S(1)}, u32[]{:S(2)}, u32[]{:S(2)}) collective-permute-start(bf16[16,48,384]{2,1,0:T(8,128)(2,1)S(1)} %pad_maximum_fusion.6), channel_id=1, source_target_pairs={{0,16},{16,0},{1,17},{17,1},{2,18},{18,2},{3,19},{19,3},{4,20},{20... | collective-permute-start | bytes 1769480 | tf_op jit(solution)/shard_map/ppermute | solution.py:311
  214.9 7.9 %collective-permute-start.57 = (bf16[2,2,48,384]{3,2,1,0:T(8,128)(2,1)S(1)}, bf16[2,2,48,384]{3,2,1,0:T(8,128)(2,1)S(1)}, u32[]{:S(2)}, u32[]{:S(2)}) collective-permute-start(bf16[2,2,48,384]{3,2,1,0:T(8,128)(2,1)S(1)} %fusion.35), channel_id=1, source_target_pairs={{0,8},{1,9},{2,10},{3,11},{4,12},{5,13},{6,14},{7,15},{8,0},{9,1},... | collective-permute-start | bytes 442376 | tf_op jit(solution)/shard_map/ppermute | solution.py:307
  223.8 8.1 %collective-permute-start.60 = (bf16[2,2,48,384]{3,2,0,1:T(8,128)(2,1)S(1)}, bf16[2,2,48,384]{3,2,0,1:T(8,128)(2,1)S(1)}, u32[]{:S(2)}, u32[]{:S(2)}) collective-permute-start(bf16[2,2,48,384]{3,2,0,1:T(8,128)(2,1)S(1)} %copy.53), channel_id=1, source_target_pairs={{0,4},{1,5},{2,6},{3,7},{4,0},{5,1},{6,2},{7,3},{8,12},{9,13},{10,... | collective-permute-start | bytes 442376 | tf_op jit(solution)/shard_map/ppermute | solution.py:307
  223.8 8.0 %collective-permute-start.61 = (bf16[2,2,48,384]{3,2,1,0:T(8,128)(2,1)S(1)}, bf16[2,2,48,384]{3,2,1,0:T(8,128)(2,1)S(1)}, u32[]{:S(2)}, u32[]{:S(2)}) collective-permute-start(bf16[2,2,48,384]{3,2,1,0:T(8,128)(2,1)S(1)} %fusion.16.mine1), channel_id=1, source_target_pairs={{0,16},{16,0},{1,17},{17,1},{2,18},{18,2},{3,19},{19,3},{4,20},{20... | collective-permute-start | bytes 442376 | tf_op jit(solution)/shard_map/ppermute | solution.py:311
  (62 other events, 392.9 us)
